TPU v7x, 128 devices: a whole 4x4x4 slice. The times are simulated.
128 devices in a mesh: member: 4 (over x), slab: 32 (over z, y, core).
Axes of the slice: x: 4, y: 4, z: 4, core: 2. Of those that a mesh axis runs over, the one named last changes fastest.
Arguments:
- ensemble: float32 [80, 1572864], P('member', 'slab'), may hold values from -6 to 6
- block_order: int32 [4], replicated, may hold values from 0 to 3, each once
- obs_owner: int32 [4, 256], replicated, may hold values from 0 to 127
- interp_cells: int32 [4, 256, 4], replicated, may hold values from 0 to 12287
- interp_weight: float32 [4, 256, 4], replicated, may hold values from 0.1 to 0.5
- obs_radius: int32 [4, 256], replicated, may hold values from 12288 to 49151
- obs_value: float32 [4, 256], replicated, may hold values from -6 to 6
- obs_variance: float32 [4, 256], replicated, may hold values from 0.25 to 2
Outputs:
- posterior: float32 [80, 1572864], P('member', 'slab')
Inputs may be any that keep to these rules, and one draw needn't show every extreme that they name: `block_order`: a permutation of the block numbers. `obs_owner`: the index of the block of 12288 consecutive state cells that holds the observation.
All inputs are finite; a program needn't handle non-finite values.
Results may differ from a plain program's by a relative error of at most 0.0001.
Values sent between devices are 32-bit elements; how exact they have to be, the bound alone decides.
No kernel may reach another device: no remote copies, remote signals or barrier semaphores. Data moves between devices by JAX's collectives and lax.ppermute only.
A program may use at most 128 MiB of HBM per device.

v0:
```python
import jax
import jax.numpy as jnp
from jax import lax
from jax.sharding import PartitionSpec as P

MEMBERS = 80
BLOCKS = 4


def obs_terms(prior, values, variance):
    ybar = jnp.mean(prior, axis=1)
    anomaly_y = prior - ybar[:, None]
    spread = jnp.sum(anomaly_y * anomaly_y, axis=1) / (MEMBERS - 1)
    gain = 1.0 / (spread + variance)
    shrink = -gain / (1.0 + jnp.sqrt(variance * gain))
    coeff = gain * (values - ybar)
    driver = coeff[:, None] + shrink[:, None] * anomaly_y
    return (anomaly_y, driver)


def local_priors(state, cells, weight, mine):
    picked = jnp.take(state, cells, axis=1)
    values = jnp.sum(picked * weight[None], axis=-1).T
    return jnp.where(mine[:, None], values, jnp.float32(0.0))


def taper(positions, centre, radius):
    dist = jnp.abs(positions[:, None] - centre[None, :]).astype(jnp.float32)
    return jnp.maximum(jnp.float32(0.0), 1.0 - dist / radius[None, :])


def apply_terms(current, loc, anomaly_y, driver):
    anomaly_x = current - jnp.mean(current, axis=0)[None, :]
    cov = jnp.einsum("ec,be->cb", anomaly_x, anomaly_y, precision=lax.Precision.HIGHEST) / (
        MEMBERS - 1
    )
    return current + jnp.einsum("cb,be->ec", loc * cov, driver, precision=lax.Precision.HIGHEST)


def per_device(
    ensemble,
    block_order,
    obs_owner,
    interp_cells,
    interp_weight,
    obs_radius,
    obs_value,
    obs_variance,
):
    groups = lax.axis_size("member")
    member_rank = lax.axis_index("member")
    slab_rank = lax.axis_index("slab")
    here = slab_rank * groups + member_rank
    cells_dev = ensemble.shape[1] // groups
    first = here * cells_dev
    positions = first + jnp.arange(cells_dev, dtype=jnp.int32)
    state = lax.all_to_all(ensemble, "member", split_axis=1, concat_axis=0, tiled=True)
    for step in range(BLOCKS):
        which = block_order[step]
        owner = obs_owner[which]
        cells = interp_cells[which]
        mine = owner == here
        offsets = jnp.where(mine[:, None], cells, 0)
        prior = lax.psum(
            local_priors(state, offsets, interp_weight[which], mine), ("member", "slab")
        )
        anomaly_y, driver = obs_terms(prior, obs_value[which], obs_variance[which])
        centre = owner * cells_dev + cells[:, 0]
        radius_int = obs_radius[which]
        radius = radius_int.astype(jnp.float32)
        state = apply_terms(state, taper(positions, centre, radius), anomaly_y, driver)
    return lax.all_to_all(state, "member", split_axis=0, concat_axis=1, tiled=True)


def solution(mesh):
    in_specs = (P("member", "slab"), P(), P(), P(), P(), P(), P(), P())
    out_specs = P("member", "slab")
    return jax.shard_map(
        per_device, mesh=mesh, in_specs=in_specs, out_specs=out_specs, check_vma=False
    )
```

profile of v0, /device:TPU:0, one launch (start us, length us, event | category | flops | bytes accessed | tf_op | source)
XLA Modules:
  0.0 909.2 jit_solution(11667885652835249761)
XLA Ops:
  6.6 6.0 all_to_all.28
  12.6 6.6 copy.70
  19.1 5.0 all-to-all-start
  24.2 0.7 fusion.68
  32.8 0.3 copy-done.15
  33.0 0.2 copy.71
  33.4 0.1 copy.76
  33.6 0.2 copy.75
  33.8 0.1 copy.78
  34.0 0.1 copy.80
  34.2 0.2 copy.79
  34.4 0.1 copy.82
  34.6 0.1 copy.84
  34.8 0.8 copy.83
  35.6 0.8 copy.86
  36.4 0.5 fusion.59
  36.9 0.5 constant_dynamic-slice_fusion.1
  37.5 0.6 broadcast_clamp_fusion
  38.1 0.6 fusion.60
  38.7 40.1 %all-to-all-done = f32[20,4,12288]{2,0,1:T(8,128)} async-done(((f32[20,4,12288]{2,0,1:T(8,128)}), f32[20,4,12288]{2,0,1:T(8,128)}, u32[]{:S(2)}, u32[]{:S(2)}) %all-to-all-start) | async-done | bytes 3932192 | tf_op jit(solution)/shard_map/all_to_all | solution.py:57
  78.8 3.9 all_to_all.31
  82.6 6.0 copy.73
  88.7 5.6 gather_fusion
  94.2 1.5 fusion.15
  95.7 0.8 select_bitcast_fusion.3
  96.5 0.2 all-reduce.7.cloned.1.call-start
  96.7 2.6 reduce_sum.147
  99.4 138.1 %all-reduce.5.cloned.1.call-done = f32[256,80]{1,0:T(8,128)} async-done(((f32[256,80]{1,0:T(8,128)}), f32[256,80]{1,0:T(8,128)}) %all-reduce.5.cloned.1.call-update) | async-done | bytes 81936 | tf_op jit(solution)/shard_map/psum | solution.py:64
  237.4 1.0 reduce_sum.145
  238.5 1.1 multiply_reduce_fusion.3
  239.6 17.7 %fusion.3 = f32[12288,256]{1,0:T(8,128)S(1)} fusion(f32[256]{0:T(256)S(1)} %bitcast.114, s32[256]{0:T(256)S(1)} %bitcast.110, s32[12288]{0:T(1024)S(1)} %iota_add_fusion, f32[80,12288]{1,0:T(8,128)} %all_to_all.31, f32[12288]{0:T(1024)S(1)} %broadcast_multiply_fusion.3, f32[256,80]{1,0:T(8,128)} %all-reduce.5.cloned.1.call-done, ...), kind=kOutput, calls=%fused_computation.11 | convolution fusion | flops 3046068224 | bytes 16698368 | tf_op jit(solution)/shard_map/ec,be->cb/dot_general | solution.py:34
  257.4 14.9 %fusion.69 = (f32[12288]{0:T(1024)S(1)}, f32[80,12288]{1,0:T(8,128)}) fusion(f32[80,12288]{1,0:T(8,128)S(1)} %copy-done.3, f32[12288,256]{1,0:T(8,128)S(1)} %fusion.3, f32[256,80]{1,0:T(8,128)S(1)} %copy-done.5, f32[256]{0:T(256)S(1)} %get-tuple-element.58, f32[256]{0:T(256)S(1)} %get-tuple-element.57, f32[256]{0:T(256)S(1)} %broadcast_multiply_fusion.7), kind=kOutput, calls=%fused_computation.154 | convolution fusion | flops 3021914112 | bytes 20581376 | tf_op jit(solution)/shard_map/cb,be->ec/dot_general | solution.py:37
  272.2 6.0 copy.77
  278.2 5.6 gather_fusion.1
  283.8 1.9 fusion.14
  285.8 0.8 select_bitcast_fusion.2
  286.6 137.5 %all-reduce.7.cloned.1.call-done = f32[256,80]{1,0:T(8,128)} async-done(((f32[256,80]{1,0:T(8,128)}), f32[256,80]{1,0:T(8,128)}) %all-reduce.7.cloned.1.call-update) | async-done | bytes 81936 | tf_op jit(solution)/shard_map/psum | solution.py:64
  424.1 1.0 reduce_sum.149
  425.1 1.1 multiply_reduce_fusion.2
  426.3 17.5 %fusion.2 = f32[12288,256]{1,0:T(8,128)S(1)} fusion(f32[256]{0:T(256)S(1)} %bitcast.113, s32[256]{0:T(256)S(1)} %bitcast.109, s32[12288]{0:T(1024)S(1)} %iota_add_fusion, f32[80,12288]{1,0:T(8,128)} %get-tuple-element.64, f32[12288]{0:T(1024)S(1)} %broadcast_multiply_fusion.2, f32[256,80]{1,0:T(8,128)} %all-reduce.7.cloned.1.call-done, ...), kind=kOutput, calls=%fused_computation.9 | convolution fusion | flops 3046068224 | bytes 16698368 | tf_op jit(solution)/shard_map/ec,be->cb/dot_general | solution.py:34
  443.8 14.9 %fusion.70 = (f32[12288]{0:T(1024)S(1)}, f32[80,12288]{1,0:T(8,128)}) fusion(f32[80,12288]{1,0:T(8,128)S(1)} %copy-done, f32[12288,256]{1,0:T(8,128)S(1)} %fusion.2, f32[256,80]{1,0:T(8,128)S(1)} %copy-done.6, f32[256]{0:T(256)S(1)} %get-tuple-element.56, f32[256]{0:T(256)S(1)} %get-tuple-element.55, f32[256]{0:T(256)S(1)} %broadcast_multiply_fusion.6), kind=kOutput, calls=%fused_computation.155 | convolution fusion | flops 3021914112 | bytes 20581376 | tf_op jit(solution)/shard_map/cb,be->ec/dot_general | solution.py:37
  458.7 6.0 copy.81
  464.7 5.6 gather_fusion.2
  470.3 1.6 fusion.13
  471.9 0.8 select_bitcast_fusion.1
  472.8 137.5 %all-reduce.9.cloned.1.call-done = f32[256,80]{1,0:T(8,128)} async-done(((f32[256,80]{1,0:T(8,128)}), f32[256,80]{1,0:T(8,128)}) %all-reduce.9.cloned.1.call-update) | async-done | bytes 81936 | tf_op jit(solution)/shard_map/psum | solution.py:64
  610.3 1.0 reduce_sum.153
  611.3 1.1 multiply_reduce_fusion.1
  612.4 17.5 %fusion.1 = f32[12288,256]{1,0:T(8,128)S(1)} fusion(f32[256]{0:T(256)S(1)} %bitcast.112, s32[256]{0:T(256)S(1)} %bitcast.108, s32[12288]{0:T(1024)S(1)} %iota_add_fusion, f32[80,12288]{1,0:T(8,128)} %get-tuple-element.66, f32[12288]{0:T(1024)S(1)} %broadcast_multiply_fusion.1, f32[256,80]{1,0:T(8,128)} %all-reduce.9.cloned.1.call-done, ...), kind=kOutput, calls=%fused_computation.7 | convolution fusion | flops 3046068224 | bytes 16698368 | tf_op jit(solution)/shard_map/ec,be->cb/dot_general | solution.py:34
  630.0 14.9 %fusion.71 = (f32[12288]{0:T(1024)S(1)}, f32[80,12288]{1,0:T(8,128)}) fusion(f32[80,12288]{1,0:T(8,128)S(1)} %copy-done.1, f32[12288,256]{1,0:T(8,128)S(1)} %fusion.1, f32[256,80]{1,0:T(8,128)S(1)} %copy-done.7, f32[256]{0:T(256)S(1)} %get-tuple-element.54, f32[256]{0:T(256)S(1)} %get-tuple-element.53, f32[256]{0:T(256)S(1)} %broadcast_multiply_fusion.5), kind=kOutput, calls=%fused_computation.156 | convolution fusion | flops 3021914112 | bytes 20581376 | tf_op jit(solution)/shard_map/cb,be->ec/dot_general | solution.py:37
  644.8 6.0 copy.85
  650.9 5.6 gather_fusion.3
  656.6 1.9 fusion.12
  658.4 0.8 select_bitcast_fusion
  659.2 137.5 %all-reduce.11.cloned.1.call-done = f32[256,80]{1,0:T(8,128)} async-done(((f32[256,80]{1,0:T(8,128)}), f32[256,80]{1,0:T(8,128)}) %all-reduce.11.cloned.1.call-update) | async-done | bytes 81936 | tf_op jit(solution)/shard_map/psum | solution.py:64
  796.8 1.0 reduce_sum.157
  797.8 1.1 multiply_reduce_fusion
  799.0 17.5 %fusion = f32[12288,256]{1,0:T(8,128)S(1)} fusion(f32[256]{0:T(256)S(1)} %bitcast.111, s32[256]{0:T(256)S(1)} %bitcast.107, s32[12288]{0:T(1024)S(1)} %iota_add_fusion, f32[80,12288]{1,0:T(8,128)} %get-tuple-element.68, f32[12288]{0:T(1024)S(1)} %broadcast_multiply_fusion, f32[256,80]{1,0:T(8,128)} %all-reduce.11.cloned.1.call-done, ...), kind=kOutput, calls=%fused_computation.5 | convolution fusion | flops 3046068224 | bytes 16698368 | tf_op jit(solution)/shard_map/ec,be->cb/dot_general | solution.py:34
  816.5 14.9 %convolution_add_fusion = f32[80,12288]{1,0:T(8,128)} fusion(f32[80,12288]{1,0:T(8,128)S(1)} %copy-done.2, f32[12288,256]{1,0:T(8,128)S(1)} %fusion, f32[256,80]{1,0:T(8,128)S(1)} %copy-done.8, f32[256]{0:T(256)S(1)} %get-tuple-element.52, f32[256]{0:T(256)S(1)} %get-tuple-element.51, f32[256]{0:T(256)S(1)} %broadcast_multiply_fusion.4), kind=kOutput, calls=%fused_computation.12 | convolution fusion | flops 3020943360 | bytes 20532224 | tf_op jit(solution)/shard_map/cb,be->ec/dot_general | solution.py:37
  831.4 3.9 all_to_all.32
  835.3 58.5 %all_to_all.38 = f32[4,20,12288]{2,1,0:T(8,128)S(1)} all-to-all(f32[4,20,12288]{2,1,0:T(8,128)} %all_to_all.32), channel_id=1, replica_groups=mesh['member'=4,'slab'=32] {'member'}, dimensions={0} | all-to-all | bytes 7864320 | tf_op jit(solution)/shard_map/all_to_all | solution.py:72
  893.8 2.5 copy.87
  896.4 1.1 pad.4
  897.5 4.9 copy.88
  (79 shorter events, 1.2 us)
Async XLA Ops:
  6.5 17.6 %copy-start.14 = (s32[4]{0:T(128)S(1)}, s32[4]{0:T(128)}, u32[]{:S(2)}) copy-start(s32[4]{0:T(128)} %param.11) | copy-start | bytes 52
  6.5 25.9 %copy-start.12 = (s32[4,256]{1,0:T(4,128)S(1)}, s32[4,256]{1,0:T(4,128)}, u32[]{:S(2)}) copy-start(s32[4,256]{1,0:T(4,128)} %param.12) | copy-start | bytes 12292
  6.5 25.9 %copy-start.11 = (s32[4,256,4]{1,2,0:T(4,128)S(1)}, s32[4,256,4]{1,2,0:T(4,128)}, u32[]{:S(2)}) copy-start(s32[4,256,4]{1,2,0:T(4,128)} %param.13) | copy-start | bytes 49156
  6.5 26.7 %copy-start.13 = (f32[4,256,4]{1,2,0:T(4,128)S(1)}, f32[4,256,4]{1,2,0:T(4,128)}, u32[]{:S(2)}) copy-start(f32[4,256,4]{1,2,0:T(4,128)} %param.14) | copy-start | bytes 49156
  6.5 29.8 %copy-start.17 = (s32[4,256]{1,0:T(4,128)S(1)}, s32[4,256]{1,0:T(4,128)}, u32[]{:S(2)}) copy-start(s32[4,256]{1,0:T(4,128)} %param.15) | copy-start | bytes 12292
  6.5 30.4 %copy-start.20 = (f32[4,256]{1,0:T(4,128)S(1)}, f32[4,256]{1,0:T(4,128)}, u32[]{:S(2)}) copy-start(f32[4,256]{1,0:T(4,128)} %param.16) | copy-start | bytes 12292
  6.6 30.4 %copy-start.21 = (f32[4,256]{1,0:T(4,128)S(1)}, f32[4,256]{1,0:T(4,128)}, u32[]{:S(2)}) copy-start(f32[4,256]{1,0:T(4,128)} %param.17) | copy-start | bytes 12292
  19.1 59.7 %all-to-all-start = ((f32[20,4,12288]{2,0,1:T(8,128)}), f32[20,4,12288]{2,0,1:T(8,128)}, u32[]{:S(2)}, u32[]{:S(2)}) async-start(f32[20,4,12288]{2,0,1:T(8,128)} %copy.70), calls=%async_computation | async-start | bytes 9437184 | tf_op jit(solution)/shard_map/all_to_all | solution.py:57
  24.1 213.3 %all-reduce.5.cloned.1.call-start = ((), (), s32[]{:S(2)}) async-start(), calls=%async_computation.2 | async-start | bytes 262144 | tf_op jit(solution)/shard_map/psum | solution.py:64
  32.4 0.6 copy-start.15
  96.5 327.6 %all-reduce.7.cloned.1.call-start = ((), (), s32[]{:S(2)}) async-start(), calls=%async_computation.3 | async-start | bytes 262144 | tf_op jit(solution)/shard_map/psum | solution.py:64
  239.6 17.8 %copy-start.3 = (f32[80,12288]{1,0:T(8,128)S(1)}, f32[80,12288]{1,0:T(8,128)}, u32[]{:S(2)}) copy-start(f32[80,12288]{1,0:T(8,128)} %all_to_all.31) | copy-start | bytes 11796484
  239.6 17.8 %copy-start.5 = (f32[256,80]{1,0:T(8,128)S(1)}, f32[256,80]{1,0:T(8,128)}, u32[]{:S(2)}) copy-start(f32[256,80]{1,0:T(8,128)} %all-reduce.5.cloned.1.call-done) | copy-start | bytes 245764
  286.5 323.7 %all-reduce.9.cloned.1.call-start = ((), (), s32[]{:S(2)}) async-start(), calls=%async_computation.4 | async-start | bytes 262144 | tf_op jit(solution)/shard_map/psum | solution.py:64
  426.2 17.6 %copy-start = (f32[80,12288]{1,0:T(8,128)S(1)}, f32[80,12288]{1,0:T(8,128)}, u32[]{:S(2)}) copy-start(f32[80,12288]{1,0:T(8,128)} %get-tuple-element.64) | copy-start | bytes 11796484
  426.2 17.6 %copy-start.6 = (f32[256,80]{1,0:T(8,128)S(1)}, f32[256,80]{1,0:T(8,128)}, u32[]{:S(2)}) copy-start(f32[256,80]{1,0:T(8,128)} %all-reduce.7.cloned.1.call-done) | copy-start | bytes 245764
  472.7 324.1 %all-reduce.11.cloned.1.call-start = ((), (), s32[]{:S(2)}) async-start(), calls=%async_computation.5 | async-start | bytes 262144 | tf_op jit(solution)/shard_map/psum | solution.py:64
  612.4 17.6 %copy-start.1 = (f32[80,12288]{1,0:T(8,128)S(1)}, f32[80,12288]{1,0:T(8,128)}, u32[]{:S(2)}) copy-start(f32[80,12288]{1,0:T(8,128)} %get-tuple-element.66) | copy-start | bytes 11796484
  612.4 17.6 %copy-start.7 = (f32[256,80]{1,0:T(8,128)S(1)}, f32[256,80]{1,0:T(8,128)}, u32[]{:S(2)}) copy-start(f32[256,80]{1,0:T(8,128)} %all-reduce.9.cloned.1.call-done) | copy-start | bytes 245764
  630.0 20.9 %copy-start.4 = (s32[1024]{0:T(1024)S(1)}, s32[1024]{0:T(1024)}, u32[]{:S(2)}) copy-start(s32[1024]{0:T(1024)} %broadcast_clamp_fusion) | copy-start | bytes 12292
  650.9 5.7 copy-start.9
  650.9 5.7 copy-start.10
  650.9 7.6 copy-start.16
  650.9 148.0 %copy-start.18 = (f32[1,256]{1,0:T(1,128)S(1)}, f32[1,256]{1,0:T(1,128)}, u32[]{:S(2)}) copy-start(f32[1,256]{1,0:T(1,128)} %get-tuple-element.35) | copy-start | bytes 3076
  650.9 148.0 %copy-start.19 = (f32[1,256]{1,0:T(1,128)S(1)}, f32[1,256]{1,0:T(1,128)}, u32[]{:S(2)}) copy-start(f32[1,256]{1,0:T(1,128)} %get-tuple-element.72) | copy-start | bytes 3076
  650.9 148.0 %copy-start.22 = (s32[1,256]{1,0:T(1,128)S(1)}, s32[1,256]{1,0:T(1,128)}, u32[]{:S(2)}) copy-start(s32[1,256]{1,0:T(1,128)} %get-tuple-element.43) | copy-start | bytes 3076
  650.9 148.0 %copy-start.23 = (f32[1,256]{1,0:T(1,128)S(1)}, f32[1,256]{1,0:T(1,128)}, u32[]{:S(2)}) copy-start(f32[1,256]{1,0:T(1,128)} %get-tuple-element.47) | copy-start | bytes 3076
  798.9 17.6 %copy-start.2 = (f32[80,12288]{1,0:T(8,128)S(1)}, f32[80,12288]{1,0:T(8,128)}, u32[]{:S(2)}) copy-start(f32[80,12288]{1,0:T(8,128)} %get-tuple-element.68) | copy-start | bytes 11796484
  798.9 17.5 %copy-start.8 = (f32[256,80]{1,0:T(8,128)S(1)}, f32[256,80]{1,0:T(8,128)}, u32[]{:S(2)}) copy-start(f32[256,80]{1,0:T(8,128)} %all-reduce.11.cloned.1.call-done) | copy-start | bytes 245764
Sparse Core Ops, SparseCore 0:
  96.6 140.7 all-reduce.4
  286.7 137.3 all-reduce.6
  472.8 137.3 all-reduce.8
  659.3 137.3 all-reduce.10
where the time goes:
time: 916 us; the launch traced here: 909 us
  waiting for transfers between devices  591 us (65%)
  matrix products  130 us (14%)
  local copies, waits for them, and re-layouts  80.5 us (9%)
  blocking collectives  58.5 us (6%)
  other arithmetic  22.8 us (2%)
  between operations  21.5 us (2%)
    psum x4, waiting for transfers between devices, per_device(): lax.psum(local_priors(state, offsets, interp_weight[which], mine), ('memb...  551 us
    dot_general x4, matrix products, apply_terms(): jnp.einsum('ec,be->cb', anomaly_x, anomaly_y, precision=lax.Precision.HIG...  70.3 us
    dot_general x4, matrix products, apply_terms(): jnp.einsum('cb,be->ec', loc * cov, driver, precision=lax.Precision.HIGHEST)  59.4 us
    all_to_all x1, blocking collectives, per_device(): lax.all_to_all(state, 'member', split_axis=0, concat_axis=1, tiled=True)  58.5 us
    all_to_all x1, waiting for transfers between devices, per_device(): lax.all_to_all(ensemble, 'member', split_axis=1, concat_axis=0, tiled=True)  40.1 us
    all_to_all x4, local copies, waits for them, and re-layouts, per_device(): lax.all_to_all(ensemble, 'member', split_axis=1, concat_axis=0, tiled=True)  22.4 us
    gather x4, local copies, waits for them, and re-layouts, local_priors(): picked = jnp.take(state, cells, axis=1)  22.4 us
  transfers between devices with their start and end apart: 5, of which 5 were waited for; matrix products, arithmetic and copies ran while one was open for 1% of the time, Pallas kernels for 0%

commit v1 on v0

v1 whole, which is shorter than its diff:
```python
import functools

import jax
import jax.numpy as jnp
from jax import lax
from jax.experimental import pallas as pl
from jax.experimental.pallas import tpu as pltpu
from jax.sharding import PartitionSpec as P

MEMBERS = 80
BLOCKS = 4
POINTS = 4
OBS = 256
GROUPS = 4
ROWS = MEMBERS // GROUPS
CELLS = 12288
CHUNKS = 4
CHUNK = CELLS // CHUNKS
HALF = CHUNK // 2
PACKED = 5 * HALF
TILE = 256
COLS = OBS + (BLOCKS - 1) * POINTS * OBS
PART = COLS // 2
VMEM = 60 * 1024 * 1024

f32 = jnp.float32
bf16 = jnp.bfloat16


def split(x):
    hi = x.astype(bf16)
    lo = (x - hi.astype(f32)).astype(bf16)
    return hi, lo


def whole(n):
    return [pl.BlockSpec(memory_space=pltpu.VMEM)] * n


def params(**kw):
    return pltpu.CompilerParams(vmem_limit_bytes=VMEM, **kw)


def pack_kernel(rank_ref, ens_ref, *outs):
    rank = rank_ref[0]
    for d in range(GROUPS):
        quarter = lax.rem(rank + d, GROUPS)
        for c in range(CHUNKS):
            out = outs[d * CHUNKS + c]
            at = pl.multiple_of(quarter * CELLS + c * CHUNK, 128)
            mid = pl.multiple_of(quarter * CELLS + c * CHUNK + HALF, 128)
            out[:, 0:CHUNK] = ens_ref[0:8, pl.ds(at, CHUNK)]
            out[:, CHUNK : 2 * CHUNK] = ens_ref[8:16, pl.ds(at, CHUNK)]
            out[0:4, 2 * CHUNK : PACKED] = ens_ref[16:20, pl.ds(at, HALF)]
            out[4:8, 2 * CHUNK : PACKED] = ens_ref[16:20, pl.ds(mid, HALF)]


def pack(rank, ensemble):
    return pl.pallas_call(
        pack_kernel,
        out_shape=[jax.ShapeDtypeStruct((8, PACKED), f32)] * (GROUPS * CHUNKS),
        in_specs=[pl.BlockSpec(memory_space=pltpu.SMEM)] + whole(1),
        out_specs=whole(GROUPS * CHUNKS),
        compiler_params=params(),
        cost_estimate=pl.CostEstimate(flops=0, bytes_accessed=8 * 2**20, transcendentals=0),
        name="pack",
    )(rank, ensemble)


def pick_kernel(place_ref, part_ref, weight_ref, ens_ref, keep_ref, send_ref, first, picked):
    lanes = lax.broadcasted_iota(jnp.int32, (8, 128), 1)
    lanes4 = lax.broadcasted_iota(jnp.int32, (4, 128), 1)
    unroll = 16

    def group(g, dst, at):
        def some(s, acc):
            a, b, c = acc
            for u in range(unroll):
                n = s * unroll + u
                place = place_ref[g * 128 + n]
                held = place >= 0
                base = pl.multiple_of((jnp.maximum(place, 0) >> 7) * 128, 128)
                shift = (n - place) & 127
                lane = jnp.where(held, n, -1)
                ta = pltpu.roll(ens_ref[0:8, pl.ds(base, 128)], shift, 1)
                tb = pltpu.roll(ens_ref[8:16, pl.ds(base, 128)], shift, 1)
                tc = pltpu.roll(ens_ref[16:20, pl.ds(base, 128)], shift, 1)
                hit = lanes == lane
                a = jnp.where(hit, ta, a)
                b = jnp.where(hit, tb, b)
                c = jnp.where(lanes4 == lane, tc, c)
            return a, b, c

        zero = jnp.zeros((8, 128), f32)
        a, b, c = lax.fori_loop(0, 128 // unroll, some, (zero, zero, jnp.zeros((4, 128), f32)))
        dst[0:8, pl.ds(at, 128)] = a
        dst[8:16, pl.ds(at, 128)] = b
        dst[16:20, pl.ds(at, 128)] = c

    n_first = POINTS * OBS // 128
    n_later = (BLOCKS - 1) * n_first

    def do_first(g, carry):
        group(g, first, pl.multiple_of(g * 128, 128))
        return carry

    def do_later(g, carry):
        group(g + n_first, picked, pl.multiple_of(OBS + g * 128, 128))
        return carry

    lax.fori_loop(0, n_first, do_first, 0)
    total = first[:, 0:OBS] * weight_ref[0:1, :]
    for k in range(1, POINTS):
        total = total + first[:, k * OBS : (k + 1) * OBS] * weight_ref[k : k + 1, :]
    picked[:, 0:OBS] = total
    lax.fori_loop(0, n_later, do_later, 0)
    part = part_ref[0]
    keep_ref[...] = picked[:, pl.ds(pl.multiple_of(part * PART, 128), PART)]
    send_ref[...] = picked[:, pl.ds(pl.multiple_of((1 - part) * PART, 128), PART)]


def pick(place, part, weight, ensemble):
    smem = pl.BlockSpec(memory_space=pltpu.SMEM)
    return pl.pallas_call(
        pick_kernel,
        out_shape=[jax.ShapeDtypeStruct((ROWS, PART), f32)] * 2,
        in_specs=[smem, smem] + whole(2),
        out_specs=whole(2),
        scratch_shapes=[pltpu.VMEM((ROWS, POINTS * OBS), f32), pltpu.VMEM((ROWS, COLS), f32)],
        compiler_params=params(),
        cost_estimate=pl.CostEstimate(flops=0, bytes_accessed=40 * 2**20, transcendentals=0),
        name="pick",
    )(place, part, weight, ensemble)


def updated(x, place, lhs, driver, centre, inverse):
    n = x.shape[1]
    reps = n // 128
    mean = jnp.sum(x, axis=0, keepdims=True) * f32(1.0 / MEMBERS)
    hi, lo = split(x - mean)
    cov = jnp.dot(lhs, jnp.concatenate([hi, lo, hi], axis=0), preferred_element_type=f32)
    centre = jnp.concatenate([centre] * reps, axis=1)
    inverse = jnp.concatenate([inverse] * reps, axis=1)
    loc = jnp.maximum(f32(0.0), f32(1.0) - jnp.abs(place - centre) * inverse)
    hi, lo = split(loc * cov)
    both = jnp.dot(driver, hi, preferred_element_type=f32)
    rest = jnp.dot(driver[:MEMBERS], lo, preferred_element_type=f32)
    return x + (both[:MEMBERS] + both[MEMBERS:] + rest)


def drivers_kernel(part_ref, weight_ref, terms_ref, place_ref, *refs):
    sources = refs[: 2 * GROUPS]
    lhs_ref, driver_ref, centre_ref, inverse_ref, z = refs[2 * GROUPS :]
    part = part_ref[0]
    for h in range(2):
        at = pl.multiple_of((part if h == 0 else 1 - part) * PART, 128)
        for p in range(GROUPS):
            src = sources[h * GROUPS + p]
            z[16 * p : 16 * p + 16, pl.ds(at, PART)] = src[0:16, :]
            z[64 + 4 * p : 68 + 4 * p, pl.ds(at, PART)] = src[16:20, :]
    for t in range(BLOCKS):
        begin = OBS + (t - 1) * POINTS * OBS
        if t == 0:
            prior = z[:, 0:OBS]
        else:
            prior = z[:, begin : begin + OBS] * weight_ref[t, 0:1, :]
            for k in range(1, POINTS):
                prior = prior + z[:, begin + k * OBS : begin + (k + 1) * OBS] * weight_ref[t, k : k + 1, :]
        value = terms_ref[t, 0:1, :]
        variance = terms_ref[t, 1:2, :]
        ybar = jnp.sum(prior, axis=0, keepdims=True) * f32(1.0 / MEMBERS)
        anomaly = prior - ybar
        spread = jnp.sum(anomaly * anomaly, axis=0, keepdims=True) * f32(1.0 / (MEMBERS - 1))
        gain = f32(1.0) / (spread + variance)
        shrink = -gain / (f32(1.0) + jnp.sqrt(variance * gain))
        coeff = gain * (value - ybar)
        driver = coeff + shrink * anomaly
        hi, lo = split((anomaly * f32(1.0 / (MEMBERS - 1))).T)
        lhs_ref[t] = jnp.concatenate([hi, hi, lo], axis=1)
        hi, lo = split(driver)
        driver_ref[t] = jnp.concatenate([hi, lo], axis=0)
        columns = terms_ref[t].T
        centre_ref[t] = jnp.broadcast_to(columns[:, 2:3], (OBS, 128))
        inverse_ref[t] = jnp.broadcast_to(columns[:, 3:4], (OBS, 128))
        if t < BLOCKS - 1:
            start = OBS + t * POINTS * OBS

            def step(i, carry):
                at = pl.multiple_of(start + i * TILE, 128)
                z[:, pl.ds(at, TILE)] = updated(
                    z[:, pl.ds(at, TILE)],
                    place_ref[:, pl.ds(at, TILE)],
                    lhs_ref[t],
                    driver_ref[t],
                    centre_ref[t],
                    inverse_ref[t],
                )
                return carry

            lax.fori_loop(0, (COLS - start) // TILE, step, 0)


def drivers(part, weight, terms, place, pieces):
    return pl.pallas_call(
        drivers_kernel,
        out_shape=[
            jax.ShapeDtypeStruct((BLOCKS, OBS, 3 * MEMBERS), bf16),
            jax.ShapeDtypeStruct((BLOCKS, 2 * MEMBERS, OBS), bf16),
            jax.ShapeDtypeStruct((BLOCKS, OBS, 128), f32),
            jax.ShapeDtypeStruct((BLOCKS, OBS, 128), f32),
        ],
        in_specs=[pl.BlockSpec(memory_space=pltpu.SMEM)] + whole(3 + 2 * GROUPS),
        out_specs=whole(4),
        scratch_shapes=[pltpu.VMEM((MEMBERS, COLS), f32)],
        compiler_params=params(),
        cost_estimate=pl.CostEstimate(flops=8 * 10**9, bytes_accessed=4 * 2**20, transcendentals=0),
        name="drivers",
    )(part, weight, terms, place, *pieces)


def update_kernel(first_ref, lhs_ref, driver_ref, centre_ref, inverse_ref, *refs):
    ins, outs = refs[:GROUPS], refs[GROUPS:]
    low = lax.broadcasted_iota(jnp.int32, (8, TILE), 0) < 4
    offsets = lax.broadcasted_iota(jnp.int32, (1, TILE), 1)
    first = first_ref[0]

    def join(a, b):
        return jnp.where(low, a, pltpu.roll(b, 4, 0)), jnp.where(low, pltpu.roll(a, 4, 0), b)

    def step(i, carry):
        at = i * TILE
        cols = [pl.ds(pl.multiple_of(base + at, 128), TILE) for base in (0, HALF, CHUNK, CHUNK + HALF, 2 * CHUNK)]
        rest = [ref[:, cols[4]] for ref in ins]
        pair = [join(rest[0], rest[1]), join(rest[2], rest[3])]
        xs = []
        for h in range(2):
            full = []
            for ref in ins:
                full += [ref[:, cols[h]], ref[:, cols[2 + h]]]
            xs.append(jnp.concatenate(full + [pair[0][h], pair[1][h]], axis=0))
        places = [(first + at + h * HALF + offsets).astype(f32) for h in range(2)]
        for t in range(BLOCKS):
            for h in range(2):
                xs[h] = updated(xs[h], places[h], lhs_ref[t], driver_ref[t], centre_ref[t], inverse_ref[t])
        for h in range(2):
            for p, ref in enumerate(outs):
                ref[:, cols[h]] = xs[h][16 * p : 16 * p + 8]
                ref[:, cols[2 + h]] = xs[h][16 * p + 8 : 16 * p + 16]
        for q in range(2):
            a, b = join(xs[0][64 + 8 * q : 72 + 8 * q], xs[1][64 + 8 * q : 72 + 8 * q])
            outs[2 * q][:, cols[4]] = a
            outs[2 * q + 1][:, cols[4]] = b
        return carry

    lax.fori_loop(0, HALF // TILE, step, 0)


def update(first, terms, pieces):
    return pl.pallas_call(
        update_kernel,
        out_shape=[jax.ShapeDtypeStruct((8, PACKED), f32)] * GROUPS,
        in_specs=[pl.BlockSpec(memory_space=pltpu.SMEM)] + whole(4 + GROUPS),
        out_specs=whole(GROUPS),
        compiler_params=params(),
        cost_estimate=pl.CostEstimate(flops=10 * 10**9, bytes_accessed=4 * 2**20, transcendentals=0),
        name="update",
    )(first, *terms, *pieces)


def unpack_kernel(chunk, rank_ref, *refs):
    pieces = refs[:GROUPS]
    out_ref, rows, sems = refs[-3:]
    rank = rank_ref[0]
    copies = []
    for d in range(GROUPS):
        src = pieces[d]
        rows[d, 0:8, :] = src[:, 0:CHUNK]
        rows[d, 8:16, :] = src[:, CHUNK : 2 * CHUNK]
        rows[d, 16:20, 0:HALF] = src[0:4, 2 * CHUNK : PACKED]
        rows[d, 16:20, HALF:CHUNK] = src[4:8, 2 * CHUNK : PACKED]
        at = pl.multiple_of(lax.rem(rank + d, GROUPS) * CELLS + chunk * CHUNK, 128)
        copy = pltpu.make_async_copy(rows.at[d], out_ref.at[:, pl.ds(at, CHUNK)], sems.at[d])
        copy.start()
        copies.append(copy)
    for copy in copies:
        copy.wait()


def unpack(chunk, rank, pieces, out):
    held = [] if out is None else [out]
    return pl.pallas_call(
        functools.partial(unpack_kernel, chunk),
        out_shape=jax.ShapeDtypeStruct((ROWS, GROUPS * CELLS), f32),
        in_specs=[pl.BlockSpec(memory_space=pltpu.SMEM)]
        + whole(GROUPS)
        + [pl.BlockSpec(memory_space=pl.ANY)] * len(held),
        out_specs=pl.BlockSpec(memory_space=pl.ANY),
        scratch_shapes=[pltpu.VMEM((GROUPS, ROWS, CHUNK), f32), pltpu.SemaphoreType.DMA((GROUPS,))],
        input_output_aliases={1 + GROUPS: 0} if held else {},
        compiler_params=params(),
        cost_estimate=pl.CostEstimate(flops=0, bytes_accessed=4 * 2**20, transcendentals=0),
        name="unpack",
    )(rank, *pieces, *held)


def shifted(x, axis, size, by):
    return lax.ppermute(x, axis, [(i, (i + by) % size) for i in range(size)])


def per_device(
    ensemble,
    block_order,
    obs_owner,
    interp_cells,
    interp_weight,
    obs_radius,
    obs_value,
    obs_variance,
):
    slabs = lax.axis_size("slab")
    member_rank = lax.axis_index("member")
    slab_rank = lax.axis_index("slab")
    here = slab_rank * GROUPS + member_rank
    rank = member_rank.reshape(1)
    part = (slab_rank % 2).reshape(1)

    pieces = pack(rank, ensemble)
    arrived = []
    for c in range(CHUNKS):
        arrived.append(
            [pieces[c]]
            + [shifted(pieces[d * CHUNKS + c], "member", GROUPS, d) for d in range(1, GROUPS)]
        )

    owner = obs_owner[block_order]
    cells = interp_cells.transpose(0, 2, 1)[block_order]
    weight = interp_weight.transpose(0, 2, 1)[block_order]
    everywhere = owner[:, None, :] * CELLS + cells
    local = everywhere - slab_rank * (GROUPS * CELLS)
    inside = (local >= 0) & (local < GROUPS * CELLS)
    place = jnp.where(inside, local, -1).reshape(-1)
    radius = obs_radius[block_order].astype(f32)
    zero = jnp.zeros_like(radius)
    terms = jnp.stack(
        [
            obs_value[block_order],
            obs_variance[block_order],
            everywhere[:, 0, :].astype(f32),
            1.0 / radius,
            zero,
            zero,
            zero,
            zero,
        ],
        axis=1,
    )
    columns = everywhere.astype(f32).reshape(1, -1)[:, POINTS * OBS - OBS :]

    keep, send = pick(place, part, weight[0], ensemble)
    chip = keep + lax.ppermute(send, "slab", [(i, i ^ 1) for i in range(slabs)])
    window = chip
    for by in (2, -2, 4, -4):
        window = window + shifted(chip, "slab", slabs, by)
    mine = [window] + [shifted(window, "member", GROUPS, d) for d in range(1, GROUPS)]
    other = [lax.ppermute(x, "slab", [(i, i ^ 1) for i in range(slabs)]) for x in mine]
    blocks = drivers(part, weight, terms, columns, mine + other)

    out = None
    for c in range(CHUNKS):
        first = (here * CELLS + c * CHUNK).reshape(1)
        new = update(first, blocks, arrived[c])
        back = [new[0]] + [shifted(new[d], "member", GROUPS, -d) for d in range(1, GROUPS)]
        out = unpack(c, rank, back, out)
    return out


def solution(mesh):
    in_specs = (P("member", "slab"), P(), P(), P(), P(), P(), P(), P())
    out_specs = P("member", "slab")
    return jax.shard_map(
        per_device, mesh=mesh, in_specs=in_specs, out_specs=out_specs, check_vma=False
    )
```

time: 916 us -> 201 us (0.22)
  waiting for transfers between devices: 591 us -> 16.1 us
  matrix products: 130 us -> 0 us
  Pallas kernels: 0 us -> 121 us
  local copies, waits for them, and re-layouts: 80.5 us -> 8.52 us
  blocking collectives: 58.5 us -> 0 us
  starting transfers between devices: 5.3 us -> 51.4 us
  between operations: 21.5 us -> 0.62 us
  other arithmetic: 22.8 us -> 2.31 us
    psum x4 -> x0, waiting for transfers between devices: 551 us -> none  [per_device(): lax.psum(local_priors(state, offsets, interp_weight[which], mine), ('memb...]
    dot_general x8 -> x0, matrix products: 130 us -> none  [the longest x4 70.3 us: apply_terms(): jnp.einsum('ec,be->cb', anomaly_x, anomaly_y, precision=lax.Precision.HIG...]
    pallas_call x0 -> x11, Pallas kernels: none -> 121 us  [the longest x4 56.6 us: update(): pl.pallas_call(update_kernel, out_shape=[jax.ShapeDtypeStruct((8, PACKED)...]
    all_to_all x1 -> x0, blocking collectives: 58.5 us -> none  [per_device(): lax.all_to_all(state, 'member', split_axis=0, concat_axis=1, tiled=True)]
    ppermute x0 -> x36, starting transfers between devices: none -> 51.4 us  [the longest x31 51.4 us: shifted(): return lax.ppermute(x, axis, [(i, (i + by) % size) for i in range(size)])]
    all_to_all x1 -> x0, waiting for transfers between devices: 40.1 us -> none  [per_device(): lax.all_to_all(ensemble, 'member', split_axis=1, concat_axis=0, tiled=True)]
    all_to_all x6 -> x0, local copies, waits for them, and re-layouts: 28.9 us -> none  [the longest x4 22.4 us: per_device(): lax.all_to_all(ensemble, 'member', split_axis=1, concat_axis=0, tiled=True)]
    add x3 -> x0, local copies, waits for them, and re-layouts: 18 us -> none  [apply_terms(): current + jnp.einsum('cb,be->ec', loc * cov, driver, precision=lax.Precis...]
  transfers between devices with their start and end apart: 5 -> 36, of which waited for: 5 -> 8; matrix products, arithmetic and copies ran while one was open for 1% -> 2% of each run, Pallas kernels for 0% -> 41%
where the time goes in v1:
time: 201 us; the launch traced here: 200 us
  Pallas kernels  121 us (60%)
  starting transfers between devices  51.4 us (26%)
  waiting for transfers between devices  16.1 us (8%)
  local copies, waits for them, and re-layouts  8.52 us (4%)
  other arithmetic  2.31 us (1%)
    pallas_call x4, Pallas kernels, update(): pl.pallas_call(update_kernel, out_shape=[jax.ShapeDtypeStruct((8, PACKED)...  56.6 us
    ppermute x31, starting transfers between devices, shifted(): return lax.ppermute(x, axis, [(i, (i + by) % size) for i in range(size)])  51.4 us
    pallas_call x1, Pallas kernels, pick(): pl.pallas_call(pick_kernel, out_shape=[jax.ShapeDtypeStruct((ROWS, PART),...  37 us
    ppermute x31, waiting for transfers between devices, shifted(): return lax.ppermute(x, axis, [(i, (i + by) % size) for i in range(size)])  14.5 us
    pallas_call x1, Pallas kernels, drivers(): pl.pallas_call(drivers_kernel, out_shape=[jax.ShapeDtypeStruct((BLOCKS, O...  13.8 us
    pallas_call x4, Pallas kernels, unpack(): pl.pallas_call(functools.partial(unpack_kernel, chunk), out_shape=jax.Sha...  9.49 us
    pallas_call x1, Pallas kernels, pack(): pl.pallas_call(pack_kernel, out_shape=[jax.ShapeDtypeStruct((8, PACKED),...  4.49 us
  transfers between devices with their start and end apart: 36, of which 8 were waited for; matrix products, arithmetic and copies ran while one was open for 2% of the time, Pallas kernels for 41%

profile of v1, /device:TPU:0, one launch (start us, length us, event | category | flops | bytes accessed | tf_op | source)
XLA Modules:
  0.0 200.4 jit_solution(6172737624849436842)
XLA Ops:
  0.0 0.7 compare_select_fusion
  0.7 1.3 gather_fusion.3
  2.0 0.6 gather_fusion
  2.5 0.6 slice_bitcast_fusion.weight_ref
  3.1 1.3 gather_fusion.4
  4.5 0.6 and_select_fusion.place_ref
  5.1 37.0 %pick.1 = (f32[20,1664]{1,0:T(8,128)}, f32[20,1664]{1,0:T(8,128)}) custom-call(s32[4096]{0:T(1024)} %and_select_fusion.place_ref, s32[1]{0:T(128)} %bitcast.2.part_ref, f32[4,256]{1,0:T(4,128)} %slice_bitcast_fusion.weight_ref, f32[20,49152]{1,0:T(8,128)} %ens_ref.3), custom_call_target="tpu_custom_call" | custom-call | bytes 41943040 | tf_op jit(solution)/shard_map/pick/pallas_call | solution.py:124
  42.1 1.6 collective-permute-done
  43.7 0.9 add.63
  44.7 6.8 %collective-permute-start.4 = (f32[20,1664]{1,0:T(8,128)S(1)}, f32[20,1664]{1,0:T(8,128)S(1)}, u32[]{:S(2)}, u32[]{:S(2)}) collective-permute-start(f32[20,1664]{1,0:T(8,128)S(1)} %add.63), channel_id=1, source_target_pairs={{0,28},{1,29},{2,30},{3,31},{4,0},{5,1},{6,2},{7,3},{8,4},{9,5},{1... | collective-permute-start | bytes 399368 | tf_op jit(solution)/shard_map/ppermute | solution.py:307
  51.5 5.5 %collective-permute-start.2 = (f32[20,1664]{1,0:T(8,128)S(1)}, f32[20,1664]{1,0:T(8,128)S(1)}, u32[]{:S(2)}, u32[]{:S(2)}) collective-permute-start(f32[20,1664]{1,0:T(8,128)S(1)} %add.63), channel_id=1, source_target_pairs={{0,30},{1,31},{2,0},{3,1},{4,2},{5,3},{6,4},{7,5},{8,6},{9,7},{10,... | collective-permute-start | bytes 399368 | tf_op jit(solution)/shard_map/ppermute | solution.py:307
  56.9 4.5 %pack.1 = (f32[8,7680]{1,0:T(8,128)}, f32[8,7680]{1,0:T(8,128)}, f32[8,7680]{1,0:T(8,128)}, f32[8,7680]{1,0:T(8,128)}, f32[8,7680]{1,0:T(8,128)}, /*index=5*/f32...) custom-call(s32[1]{0:T(128)} %bitcast.rank_ref, ...), custom_call_target="tpu_custom_call" | custom-call | bytes 8388608 | tf_op jit(solution)/shard_map/pack/pallas_call | solution.py:59
  61.4 1.5 collective-permute-start.12
  63.0 0.6 gather_fusion.5
  63.6 2.0 %collective-permute-done.1 = f32[20,1664]{1,0:T(8,128)S(1)} collective-permute-done((f32[20,1664]{1,0:T(8,128)S(1)}, f32[20,1664]{1,0:T(8,128)S(1)}, u32[]{:S(2)}, u32[]{:S(2)}) %collective-permute-start.1) | collective-permute-done | bytes 133152 | tf_op jit(solution)/shard_map/ppermute | solution.py:307
  65.6 0.1 add_add_fusion.refs_0_
  65.6 2.8 %collective-permute-start.7 = (f32[20,1664]{1,0:T(8,128)S(1)}, f32[20,1664]{1,0:T(8,128)S(1)}, u32[]{:S(2)}, u32[]{:S(2)}) collective-permute-start(f32[20,1664]{1,0:T(8,128)S(1)} %add_add_fusion.refs_0_), channel_id=1, source_target_pairs={{0,96},{32,0},{64,32},{96,64},{1,97},{33,1},{65,33},{97,65},{2,98}... | collective-permute-start | bytes 399368 | tf_op jit(solution)/shard_map/ppermute | solution.py:307
  68.5 0.8 collective-permute-start.6
  69.3 0.9 collective-permute-start.5
  70.2 0.6 gather_fusion.2
  70.8 0.6 gather_fusion.1
  71.4 0.6 slice.25.place_ref
  72.0 1.6 collective-permute-done.7.refs_3_
  73.6 2.7 %collective-permute-done.6.refs_2_ = f32[20,1664]{1,0:T(8,128)S(1)} collective-permute-done((f32[20,1664]{1,0:T(8,128)S(1)}, f32[20,1664]{1,0:T(8,128)S(1)}, u32[]{:S(2)}, u32[]{:S(2)}) %collective-permute-start.6) | collective-permute-done | bytes 133152 | tf_op jit(solution)/shard_map/ppermute | solution.py:307
  76.3 1.1 collective-permute-done.5.refs_1_
  77.4 0.7 stack.17.terms_ref
  78.1 1.3 collective-permute-start.13
  79.4 0.6 collective-permute-start.18
  80.0 2.0 %collective-permute-start.19 = (f32[8,7680]{1,0:T(8,128)}, f32[8,7680]{1,0:T(8,128)S(1)}, u32[]{:S(2)}, u32[]{:S(2)}) collective-permute-start(f32[8,7680]{1,0:T(8,128)} %get-tuple-element.59), channel_id=1, source_target_pairs={{0,64},{32,96},{64,0},{96,32},{1,65},{33,97},{65,1},{97,33},{2,66}... | collective-permute-start | bytes 737288 | tf_op jit(solution)/shard_map/ppermute | solution.py:307
  82.1 2.3 %collective-permute-start.20 = (f32[8,7680]{1,0:T(8,128)}, f32[8,7680]{1,0:T(8,128)S(1)}, u32[]{:S(2)}, u32[]{:S(2)}) collective-permute-start(f32[8,7680]{1,0:T(8,128)} %get-tuple-element.60), channel_id=1, source_target_pairs={{0,96},{32,0},{64,32},{96,64},{1,97},{33,1},{65,33},{97,65},{2,98}... | collective-permute-start | bytes 737288 | tf_op jit(solution)/shard_map/ppermute | solution.py:307
  84.4 13.8 %drivers.1 = (bf16[4,256,240]{2,1,0:T(8,128)(2,1)}, bf16[4,160,256]{2,1,0:T(8,128)(2,1)}, f32[4,256,128]{2,1,0:T(8,128)}, f32[4,256,128]{2,1,0:T(8,128)}) custom-call(s32[1]{0:T(128)} %bitcast.2.part_ref, f32[4,4,256]{2,1,0:T(4,128)} %copy-done.17, f32[4,8,256]{2,1,0:T(8,128)} %stack.17.terms_ref, f32[1,3328]{1,0:T(1,128)} %slice.25.place_ref, ...), custom_call_target="tpu_custom_call" | custom-call | flops 8000000000 | bytes 4194304 | tf_op jit(solution)/shard_map/drivers/pallas_call | solution.py:204
  98.2 0.1 collective-permute-start.24
  98.3 0.4 collective-permute-done.19.refs_2_
  98.7 1.6 collective-permute-start.25
  100.4 2.0 %collective-permute-start.26 = (f32[8,7680]{1,0:T(8,128)S(1)}, f32[8,7680]{1,0:T(8,128)S(1)}, u32[]{:S(2)}, u32[]{:S(2)}) collective-permute-start(f32[8,7680]{1,0:T(8,128)S(1)} %copy-done.23), channel_id=1, source_target_pairs={{0,96},{32,0},{64,32},{96,64},{1,97},{33,1},{65,33},{97,65},{2,98}... | collective-permute-start | bytes 737288 | tf_op jit(solution)/shard_map/ppermute | solution.py:307
  102.5 14.2 %update.5 = (f32[8,7680]{1,0:T(8,128)}, f32[8,7680]{1,0:T(8,128)}, f32[8,7680]{1,0:T(8,128)}, f32[8,7680]{1,0:T(8,128)}) custom-call(s32[1]{0:T(128)} %bitcast.6.first_ref, bf16[4,256,240]{2,1,0:T(8,128)(2,1)} %get-tuple-element.45.lhs_ref, bf16[4,160,256]{2,1,0:T(8,128)(2,1)} %get-tuple-element.46.driver_ref, f32[4,256,128]{2,1,0:T(8,128)} %get-tuple-element.47.centre_ref, ...), custom_call_target="tpu_custom_call" | custom-call | flops 10000000000 | bytes 4194304 | tf_op jit(solution)/shard_map/update/pallas_call | solution.py:259
  116.6 0.8 collective-permute-start.30
  117.5 1.6 collective-permute-start.31
  119.0 2.8 %collective-permute-start.32 = (f32[8,7680]{1,0:T(8,128)S(1)}, f32[8,7680]{1,0:T(8,128)S(1)}, u32[]{:S(2)}, u32[]{:S(2)}) collective-permute-start(f32[8,7680]{1,0:T(8,128)S(1)} %copy-done.20), channel_id=1, source_target_pairs={{0,96},{32,0},{64,32},{96,64},{1,97},{33,1},{65,33},{97,65},{2,98}... | collective-permute-start | bytes 737288 | tf_op jit(solution)/shard_map/ppermute | solution.py:307
  121.9 14.2 %update.6 = (f32[8,7680]{1,0:T(8,128)}, f32[8,7680]{1,0:T(8,128)}, f32[8,7680]{1,0:T(8,128)}, f32[8,7680]{1,0:T(8,128)}) custom-call(s32[1]{0:T(128)} %bitcast.7.first_ref, bf16[4,256,240]{2,1,0:T(8,128)(2,1)} %get-tuple-element.45.lhs_ref, bf16[4,160,256]{2,1,0:T(8,128)(2,1)} %get-tuple-element.46.driver_ref, f32[4,256,128]{2,1,0:T(8,128)} %get-tuple-element.47.centre_ref, ...), custom_call_target="tpu_custom_call" | custom-call | flops 10000000000 | bytes 4194304 | tf_op jit(solution)/shard_map/update/pallas_call | solution.py:259
  136.1 0.5 collective-permute-start.14
  136.6 1.5 collective-permute-start.21
  138.1 0.4 collective-permute-start.27
  138.6 0.3 copy-done.41
  138.9 14.1 %update.7 = (f32[8,7680]{1,0:T(8,128)}, f32[8,7680]{1,0:T(8,128)}, f32[8,7680]{1,0:T(8,128)}, f32[8,7680]{1,0:T(8,128)}) custom-call(s32[1]{0:T(128)} %bitcast.8.first_ref, bf16[4,256,240]{2,1,0:T(8,128)(2,1)} %get-tuple-element.45.lhs_ref, bf16[4,160,256]{2,1,0:T(8,128)(2,1)} %get-tuple-element.46.driver_ref, f32[4,256,128]{2,1,0:T(8,128)} %get-tuple-element.47.centre_ref, ...), custom_call_target="tpu_custom_call" | custom-call | flops 10000000000 | bytes 4194304 | tf_op jit(solution)/shard_map/update/pallas_call | solution.py:259
  153.0 2.3 %collective-permute-start.28 = (f32[8,7680]{1,0:T(8,128)S(1)}, f32[8,7680]{1,0:T(8,128)S(1)}, u32[]{:S(2)}, u32[]{:S(2)}) collective-permute-start(f32[8,7680]{1,0:T(8,128)S(1)} %copy-done.31), channel_id=1, source_target_pairs={{0,64},{32,96},{64,0},{96,32},{1,65},{33,97},{65,1},{97,33},{2,66}... | collective-permute-start | bytes 737288 | tf_op jit(solution)/shard_map/ppermute | solution.py:307
  155.3 0.8 collective-permute-start.29
  156.1 2.5 %collective-permute-start.33 = (f32[8,7680]{1,0:T(8,128)}, f32[8,7680]{1,0:T(8,128)S(1)}, u32[]{:S(2)}, u32[]{:S(2)}) collective-permute-start(f32[8,7680]{1,0:T(8,128)} %get-tuple-element.78), channel_id=1, source_target_pairs={{0,96},{32,0},{64,32},{96,64},{1,97},{33,1},{65,33},{97,65},{2,98}... | collective-permute-start | bytes 737288 | tf_op jit(solution)/shard_map/ppermute | solution.py:307
  158.6 0.1 collective-permute-start.34
  158.7 1.3 collective-permute-start.35
  160.1 14.1 %update.4 = (f32[8,7680]{1,0:T(8,128)}, f32[8,7680]{1,0:T(8,128)}, f32[8,7680]{1,0:T(8,128)}, f32[8,7680]{1,0:T(8,128)}) custom-call(s32[1]{0:T(128)} %bitcast.1.first_ref, bf16[4,256,240]{2,1,0:T(8,128)(2,1)} %get-tuple-element.45.lhs_ref, bf16[4,160,256]{2,1,0:T(8,128)(2,1)} %get-tuple-element.46.driver_ref, f32[4,256,128]{2,1,0:T(8,128)} %get-tuple-element.47.centre_ref, ...), custom_call_target="tpu_custom_call" | custom-call | flops 10000000000 | bytes 4194304 | tf_op jit(solution)/shard_map/update/pallas_call | solution.py:259
  174.2 2.0 collective-permute-start.15
  176.2 2.3 %collective-permute-start.22 = (f32[8,7680]{1,0:T(8,128)S(1)}, f32[8,7680]{1,0:T(8,128)S(1)}, u32[]{:S(2)}, u32[]{:S(2)}) collective-permute-start(f32[8,7680]{1,0:T(8,128)S(1)} %copy-done.28), channel_id=1, source_target_pairs={{0,64},{32,96},{64,0},{96,32},{1,65},{33,97},{65,1},{97,33},{2,66}... | collective-permute-start | bytes 737288 | tf_op jit(solution)/shard_map/ppermute | solution.py:307
  178.5 0.1 collective-permute-start.23
  178.6 2.1 %collective-permute-start.16 = (f32[8,7680]{1,0:T(8,128)}, f32[8,7680]{1,0:T(8,128)S(1)}, u32[]{:S(2)}, u32[]{:S(2)}) collective-permute-start(f32[8,7680]{1,0:T(8,128)} %get-tuple-element.55), channel_id=1, source_target_pairs={{0,64},{32,96},{64,0},{96,32},{1,65},{33,97},{65,1},{97,33},{2,66}... | collective-permute-start | bytes 737288 | tf_op jit(solution)/shard_map/ppermute | solution.py:307
  180.7 2.0 collective-permute-start.17
  182.7 2.4 %unpack.4.refs_4_ = f32[20,49152]{1,0:T(8,128)} custom-call(s32[1]{0:T(128)} %bitcast.rank_ref, f32[8,7680]{1,0:T(8,128)} %get-tuple-element.77.refs_0_, f32[8,7680]{1,0:T(8,128)} %copy-done.4, f32[8,7680]{1,0:T(8,128)} %copy-done.5, f32[8,7680]{1,0:T(8,128)} %copy-done.6), custom_call_target="tpu_custom_call" | custom-call | bytes 4194304 | tf_op jit(solution)/shard_map/unpack/pallas_call | solution.py:291
  185.1 2.4 %unpack.5.refs_4_ = f32[20,49152]{1,0:T(8,128)} custom-call(s32[1]{0:T(128)} %bitcast.rank_ref, f32[8,7680]{1,0:T(8,128)} %get-tuple-element.69.refs_0_, f32[8,7680]{1,0:T(8,128)} %copy-done.8, f32[8,7680]{1,0:T(8,128)} %copy-done.9, f32[8,7680]{1,0:T(8,128)} %copy-done.10, f32[20,49152]{1,0:T(8,128)} %unpack.4.refs_4_), custom_call_target="tpu_custom_call", output_to_operand_aliasing={{}: (5, {})} | custom-call | bytes 4194304 | tf_op jit(solution)/shard_map/unpack/pallas_call | solution.py:291
  187.5 4.4 %collective-permute-done.23.refs_3_ = f32[8,7680]{1,0:T(8,128)S(1)} collective-permute-done((f32[8,7680]{1,0:T(8,128)S(1)}, f32[8,7680]{1,0:T(8,128)S(1)}, u32[]{:S(2)}, u32[]{:S(2)}) %collective-permute-start.23) | collective-permute-done | bytes 245792 | tf_op jit(solution)/shard_map/ppermute | solution.py:307
  191.9 0.7 copy-done.15
  192.6 2.4 %unpack.6.refs_4_ = f32[20,49152]{1,0:T(8,128)} custom-call(s32[1]{0:T(128)} %bitcast.rank_ref, f32[8,7680]{1,0:T(8,128)} %get-tuple-element.61.refs_0_, f32[8,7680]{1,0:T(8,128)} %copy-done.7, f32[8,7680]{1,0:T(8,128)} %copy-done.13, f32[8,7680]{1,0:T(8,128)} %copy-done.15, f32[20,49152]{1,0:T(8,128)} %unpack.5.refs_4_), custom_call_target="tpu_custom_call", output_to_operand_aliasing={{}: (5, {})} | custom-call | bytes 4194304 | tf_op jit(solution)/shard_map/unpack/pallas_call | solution.py:291
  195.0 2.2 %collective-permute-done.17.refs_3_ = f32[8,7680]{1,0:T(8,128)S(1)} collective-permute-done((f32[8,7680]{1,0:T(8,128)}, f32[8,7680]{1,0:T(8,128)S(1)}, u32[]{:S(2)}, u32[]{:S(2)}) %collective-permute-start.17) | collective-permute-done | bytes 245792 | tf_op jit(solution)/shard_map/ppermute | solution.py:307
  197.2 0.7 copy-done.14
  197.9 2.4 %unpack.7 = f32[20,49152]{1,0:T(8,128)} custom-call(s32[1]{0:T(128)} %bitcast.rank_ref, f32[8,7680]{1,0:T(8,128)} %get-tuple-element.53.refs_0_, f32[8,7680]{1,0:T(8,128)} %copy-done.11, f32[8,7680]{1,0:T(8,128)} %copy-done.12, f32[8,7680]{1,0:T(8,128)} %copy-done.14, f32[20,49152]{1,0:T(8,128)} %unpack.6.refs_4_), custom_call_target="tpu_custom_call", output_to_operand_aliasing={{}: (5, {})} | custom-call | bytes 4194304 | tf_op jit(solution)/shard_map/unpack/pallas_call | solution.py:291
  (142 shorter events, 0.4 us)
Async XLA Ops:
  2.5 58.9 %copy-start.17 = (f32[4,4,256]{2,1,0:T(4,128)}, f32[4,4,256]{2,1,0:T(4,128)S(1)}, u32[]{:S(2)}) copy-start(f32[4,4,256]{2,1,0:T(4,128)S(1)} %gather_fusion) | copy-start | bytes 49156
  5.1 57.9 %copy-start.1 = (s32[4,256]{1,0:T(4,128)S(1)}, s32[4,256]{1,0:T(4,128)}, u32[]{:S(2)}) copy-start(s32[4,256]{1,0:T(4,128)} %param.13) | copy-start | bytes 12292
  5.1 65.1 %copy-start.2 = (f32[4,256]{1,0:T(4,128)S(1)}, f32[4,256]{1,0:T(4,128)}, u32[]{:S(2)}) copy-start(f32[4,256]{1,0:T(4,128)} %param.15) | copy-start | bytes 12292
  5.1 65.7 %copy-start.3 = (f32[4,256]{1,0:T(4,128)S(1)}, f32[4,256]{1,0:T(4,128)}, u32[]{:S(2)}) copy-start(f32[4,256]{1,0:T(4,128)} %param.14) | copy-start | bytes 12292
  42.1 1.6 collective-permute-start
  44.7 18.9 %collective-permute-start.4 = (f32[20,1664]{1,0:T(8,128)S(1)}, f32[20,1664]{1,0:T(8,128)S(1)}, u32[]{:S(2)}, u32[]{:S(2)}) collective-permute-start(f32[20,1664]{1,0:T(8,128)S(1)} %add.63), channel_id=1, source_target_pairs={{0,28},{1,29},{2,30},{3,31},{4,0},{5,1},{6,2},{7,3},{8,4},{9,5},{1... | collective-permute-start | bytes 399368 | tf_op jit(solution)/shard_map/ppermute | solution.py:307
  51.5 12.1 %collective-permute-start.3 = (f32[20,1664]{1,0:T(8,128)S(1)}, f32[20,1664]{1,0:T(8,128)S(1)}, u32[]{:S(2)}, u32[]{:S(2)}) collective-permute-start(f32[20,1664]{1,0:T(8,128)S(1)} %add.63), channel_id=1, source_target_pairs={{0,4},{1,5},{2,6},{3,7},{4,8},{5,9},{6,10},{7,11},{8,12},{9,13},{1... | collective-permute-start | bytes 399368 | tf_op jit(solution)/shard_map/ppermute | solution.py:307
  51.5 12.1 %collective-permute-start.2 = (f32[20,1664]{1,0:T(8,128)S(1)}, f32[20,1664]{1,0:T(8,128)S(1)}, u32[]{:S(2)}, u32[]{:S(2)}) collective-permute-start(f32[20,1664]{1,0:T(8,128)S(1)} %add.63), channel_id=1, source_target_pairs={{0,30},{1,31},{2,0},{3,1},{4,2},{5,3},{6,4},{7,5},{8,6},{9,7},{10,... | collective-permute-start | bytes 399368 | tf_op jit(solution)/shard_map/ppermute | solution.py:307
  56.9 8.6 %collective-permute-start.1 = (f32[20,1664]{1,0:T(8,128)S(1)}, f32[20,1664]{1,0:T(8,128)S(1)}, u32[]{:S(2)}, u32[]{:S(2)}) collective-permute-start(f32[20,1664]{1,0:T(8,128)S(1)} %add.63), channel_id=1, source_target_pairs={{0,2},{1,3},{2,4},{3,5},{4,6},{5,7},{6,8},{7,9},{8,10},{9,11},{10,... | collective-permute-start | bytes 399368 | tf_op jit(solution)/shard_map/ppermute | solution.py:307
  61.4 91.5 %collective-permute-start.12 = (f32[8,7680]{1,0:T(8,128)}, f32[8,7680]{1,0:T(8,128)S(1)}, u32[]{:S(2)}, u32[]{:S(2)}) collective-permute-start(f32[8,7680]{1,0:T(8,128)} %get-tuple-element.50), channel_id=1, source_target_pairs={{0,32},{32,64},{64,96},{96,0},{1,33},{33,65},{65,97},{97,1},{2,34}... | collective-permute-start | bytes 737288 | tf_op jit(solution)/shard_map/ppermute | solution.py:307
  65.6 18.7 %copy-start.16 = (f32[20,1664]{1,0:T(8,128)}, f32[20,1664]{1,0:T(8,128)S(1)}, u32[]{:S(2)}) copy-start(f32[20,1664]{1,0:T(8,128)S(1)} %add_add_fusion.refs_0_) | copy-start | bytes 399364
  65.6 7.9 %collective-permute-start.7 = (f32[20,1664]{1,0:T(8,128)S(1)}, f32[20,1664]{1,0:T(8,128)S(1)}, u32[]{:S(2)}, u32[]{:S(2)}) collective-permute-start(f32[20,1664]{1,0:T(8,128)S(1)} %add_add_fusion.refs_0_), channel_id=1, source_target_pairs={{0,96},{32,0},{64,32},{96,64},{1,97},{33,1},{65,33},{97,65},{2,98}... | collective-permute-start | bytes 399368 | tf_op jit(solution)/shard_map/ppermute | solution.py:307
  68.5 7.8 %collective-permute-start.6 = (f32[20,1664]{1,0:T(8,128)S(1)}, f32[20,1664]{1,0:T(8,128)S(1)}, u32[]{:S(2)}, u32[]{:S(2)}) collective-permute-start(f32[20,1664]{1,0:T(8,128)S(1)} %add_add_fusion.refs_0_), channel_id=1, source_target_pairs={{0,64},{32,96},{64,0},{96,32},{1,65},{33,97},{65,1},{97,33},{2,66}... | collective-permute-start | bytes 399368 | tf_op jit(solution)/shard_map/ppermute | solution.py:307
  69.3 8.1 %collective-permute-start.5 = (f32[20,1664]{1,0:T(8,128)S(1)}, f32[20,1664]{1,0:T(8,128)S(1)}, u32[]{:S(2)}, u32[]{:S(2)}) collective-permute-start(f32[20,1664]{1,0:T(8,128)S(1)} %add_add_fusion.refs_0_), channel_id=1, source_target_pairs={{0,32},{32,64},{64,96},{96,0},{1,33},{33,65},{65,97},{97,1},{2,34}... | collective-permute-start | bytes 399368 | tf_op jit(solution)/shard_map/ppermute | solution.py:307
  72.0 6.1 %collective-permute-start.8 = (f32[20,1664]{1,0:T(8,128)S(1)}, f32[20,1664]{1,0:T(8,128)S(1)}, u32[]{:S(2)}, u32[]{:S(2)}) collective-permute-start(f32[20,1664]{1,0:T(8,128)S(1)} %add_add_fusion.refs_0_), channel_id=1, source_target_pairs={{0,1},{1,0},{2,3},{3,2},{4,5},{5,4},{6,7},{7,6},{8,9},{9,8},{10,11... | collective-permute-start | bytes 399368 | tf_op jit(solution)/shard_map/ppermute | solution.py:365
  73.6 10.8 %copy-start.42 = (f32[20,1664]{1,0:T(8,128)}, f32[20,1664]{1,0:T(8,128)S(1)}, u32[]{:S(2)}) copy-start(f32[20,1664]{1,0:T(8,128)S(1)} %collective-permute-done.7.refs_3_) | copy-start | bytes 399364
  73.6 5.8 %collective-permute-start.11 = (f32[20,1664]{1,0:T(8,128)S(1)}, f32[20,1664]{1,0:T(8,128)S(1)}, u32[]{:S(2)}, u32[]{:S(2)}) collective-permute-start(f32[20,1664]{1,0:T(8,128)S(1)} %collective-permute-done.7.refs_3_), channel_id=1, source_target_pairs={{0,1},{1,0},{2,3},{3,2},{4,5},{5,4},{6,7},{7,6},{8,9},{9,8},{10,11... | collective-permute-start | bytes 399368 | tf_op jit(solution)/shard_map/ppermute | solution.py:365
  76.3 8.1 %copy-start.43 = (f32[20,1664]{1,0:T(8,128)}, f32[20,1664]{1,0:T(8,128)S(1)}, u32[]{:S(2)}) copy-start(f32[20,1664]{1,0:T(8,128)S(1)} %collective-permute-done.6.refs_2_) | copy-start | bytes 399364
  76.3 3.8 %collective-permute-start.10 = (f32[20,1664]{1,0:T(8,128)S(1)}, f32[20,1664]{1,0:T(8,128)S(1)}, u32[]{:S(2)}, u32[]{:S(2)}) collective-permute-start(f32[20,1664]{1,0:T(8,128)S(1)} %collective-permute-done.6.refs_2_), channel_id=1, source_target_pairs={{0,1},{1,0},{2,3},{3,2},{4,5},{5,4},{6,7},{7,6},{8,9},{9,8},{10,11... | collective-permute-start | bytes 399368 | tf_op jit(solution)/shard_map/ppermute | solution.py:365
  77.4 7.0 %copy-start.44 = (f32[20,1664]{1,0:T(8,128)}, f32[20,1664]{1,0:T(8,128)S(1)}, u32[]{:S(2)}) copy-start(f32[20,1664]{1,0:T(8,128)S(1)} %collective-permute-done.5.refs_1_) | copy-start | bytes 399364
  77.4 4.7 %collective-permute-start.9 = (f32[20,1664]{1,0:T(8,128)S(1)}, f32[20,1664]{1,0:T(8,128)S(1)}, u32[]{:S(2)}, u32[]{:S(2)}) collective-permute-start(f32[20,1664]{1,0:T(8,128)S(1)} %collective-permute-done.5.refs_1_), channel_id=1, source_target_pairs={{0,1},{1,0},{2,3},{3,2},{4,5},{5,4},{6,7},{7,6},{8,9},{9,8},{10,11... | collective-permute-start | bytes 399368 | tf_op jit(solution)/shard_map/ppermute | solution.py:365
  78.1 6.3 %copy-start.45 = (f32[20,1664]{1,0:T(8,128)}, f32[20,1664]{1,0:T(8,128)S(1)}, u32[]{:S(2)}) copy-start(f32[20,1664]{1,0:T(8,128)S(1)} %collective-permute-done.8.refs_4_) | copy-start | bytes 399364
  78.1 77.2 %collective-permute-start.13 = (f32[8,7680]{1,0:T(8,128)}, f32[8,7680]{1,0:T(8,128)S(1)}, u32[]{:S(2)}, u32[]{:S(2)}) collective-permute-start(f32[8,7680]{1,0:T(8,128)} %get-tuple-element.51), channel_id=1, source_target_pairs={{0,64},{32,96},{64,0},{96,32},{1,65},{33,97},{65,1},{97,33},{2,66}... | collective-permute-start | bytes 737288 | tf_op jit(solution)/shard_map/ppermute | solution.py:307
  79.4 5.0 %copy-start.46 = (f32[20,1664]{1,0:T(8,128)}, f32[20,1664]{1,0:T(8,128)S(1)}, u32[]{:S(2)}) copy-start(f32[20,1664]{1,0:T(8,128)S(1)} %collective-permute-done.11.refs_7_) | copy-start | bytes 399364
  79.4 18.8 %collective-permute-start.18 = (f32[8,7680]{1,0:T(8,128)}, f32[8,7680]{1,0:T(8,128)S(1)}, u32[]{:S(2)}, u32[]{:S(2)}) collective-permute-start(f32[8,7680]{1,0:T(8,128)} %get-tuple-element.58), channel_id=1, source_target_pairs={{0,32},{32,64},{64,96},{96,0},{1,33},{33,65},{65,97},{97,1},{2,34}... | collective-permute-start | bytes 737288 | tf_op jit(solution)/shard_map/ppermute | solution.py:307
  80.0 18.7 %collective-permute-start.19 = (f32[8,7680]{1,0:T(8,128)}, f32[8,7680]{1,0:T(8,128)S(1)}, u32[]{:S(2)}, u32[]{:S(2)}) collective-permute-start(f32[8,7680]{1,0:T(8,128)} %get-tuple-element.59), channel_id=1, source_target_pairs={{0,64},{32,96},{64,0},{96,32},{1,65},{33,97},{65,1},{97,33},{2,66}... | collective-permute-start | bytes 737288 | tf_op jit(solution)/shard_map/ppermute | solution.py:307
  82.1 16.2 %copy-start.25 = (f32[8,7680]{1,0:T(8,128)S(1)}, f32[8,7680]{1,0:T(8,128)}, u32[]{:S(2)}) copy-start(f32[8,7680]{1,0:T(8,128)} %get-tuple-element.66) | copy-start | bytes 737284
  82.1 16.7 %copy-start.24 = (f32[8,7680]{1,0:T(8,128)S(1)}, f32[8,7680]{1,0:T(8,128)}, u32[]{:S(2)}) copy-start(f32[8,7680]{1,0:T(8,128)} %get-tuple-element.67) | copy-start | bytes 737284
  82.1 18.3 %copy-start.23 = (f32[8,7680]{1,0:T(8,128)S(1)}, f32[8,7680]{1,0:T(8,128)}, u32[]{:S(2)}) copy-start(f32[8,7680]{1,0:T(8,128)} %get-tuple-element.68) | copy-start | bytes 737284
  82.1 18.3 %collective-permute-start.20 = (f32[8,7680]{1,0:T(8,128)}, f32[8,7680]{1,0:T(8,128)S(1)}, u32[]{:S(2)}, u32[]{:S(2)}) collective-permute-start(f32[8,7680]{1,0:T(8,128)} %get-tuple-element.60), channel_id=1, source_target_pairs={{0,96},{32,0},{64,32},{96,64},{1,97},{33,1},{65,33},{97,65},{2,98}... | collective-permute-start | bytes 737288 | tf_op jit(solution)/shard_map/ppermute | solution.py:307
  98.2 18.4 %collective-permute-start.24 = (f32[8,7680]{1,0:T(8,128)S(1)}, f32[8,7680]{1,0:T(8,128)S(1)}, u32[]{:S(2)}, u32[]{:S(2)}) collective-permute-start(f32[8,7680]{1,0:T(8,128)S(1)} %copy-done.25), channel_id=1, source_target_pairs={{0,32},{32,64},{64,96},{96,0},{1,33},{33,65},{65,97},{97,1},{2,34}... | collective-permute-start | bytes 737288 | tf_op jit(solution)/shard_map/ppermute | solution.py:307
  98.7 18.7 %collective-permute-start.25 = (f32[8,7680]{1,0:T(8,128)S(1)}, f32[8,7680]{1,0:T(8,128)S(1)}, u32[]{:S(2)}, u32[]{:S(2)}) collective-permute-start(f32[8,7680]{1,0:T(8,128)S(1)} %copy-done.24), channel_id=1, source_target_pairs={{0,64},{32,96},{64,0},{96,32},{1,65},{33,97},{65,1},{97,33},{2,66}... | collective-permute-start | bytes 737288 | tf_op jit(solution)/shard_map/ppermute | solution.py:307
  100.4 18.7 %collective-permute-start.26 = (f32[8,7680]{1,0:T(8,128)S(1)}, f32[8,7680]{1,0:T(8,128)S(1)}, u32[]{:S(2)}, u32[]{:S(2)}) collective-permute-start(f32[8,7680]{1,0:T(8,128)S(1)} %copy-done.23), channel_id=1, source_target_pairs={{0,96},{32,0},{64,32},{96,64},{1,97},{33,1},{65,33},{97,65},{2,98}... | collective-permute-start | bytes 737288 | tf_op jit(solution)/shard_map/ppermute | solution.py:307
  102.4 14.2 %copy-start.22 = (f32[8,7680]{1,0:T(8,128)S(1)}, f32[8,7680]{1,0:T(8,128)}, u32[]{:S(2)}) copy-start(f32[8,7680]{1,0:T(8,128)} %get-tuple-element.74) | copy-start | bytes 737284
  102.4 15.0 %copy-start.21 = (f32[8,7680]{1,0:T(8,128)S(1)}, f32[8,7680]{1,0:T(8,128)}, u32[]{:S(2)}) copy-start(f32[8,7680]{1,0:T(8,128)} %get-tuple-element.75) | copy-start | bytes 737284
  102.4 16.6 %copy-start.20 = (f32[8,7680]{1,0:T(8,128)S(1)}, f32[8,7680]{1,0:T(8,128)}, u32[]{:S(2)}) copy-start(f32[8,7680]{1,0:T(8,128)} %get-tuple-element.76) | copy-start | bytes 737284
  116.6 5.3 %copy-start.34 = (f32[8,7680]{1,0:T(8,128)}, f32[8,7680]{1,0:T(8,128)S(1)}, u32[]{:S(2)}) copy-start(f32[8,7680]{1,0:T(8,128)S(1)} %collective-permute-done.24.refs_1_) | copy-start | bytes 737284
  116.6 19.4 %collective-permute-start.30 = (f32[8,7680]{1,0:T(8,128)S(1)}, f32[8,7680]{1,0:T(8,128)S(1)}, u32[]{:S(2)}, u32[]{:S(2)}) collective-permute-start(f32[8,7680]{1,0:T(8,128)S(1)} %copy-done.22), channel_id=1, source_target_pairs={{0,32},{32,64},{64,96},{96,0},{1,33},{33,65},{65,97},{97,1},{2,34}... | collective-permute-start | bytes 737288 | tf_op jit(solution)/shard_map/ppermute | solution.py:307
  117.5 19.2 %collective-permute-start.31 = (f32[8,7680]{1,0:T(8,128)S(1)}, f32[8,7680]{1,0:T(8,128)S(1)}, u32[]{:S(2)}, u32[]{:S(2)}) collective-permute-start(f32[8,7680]{1,0:T(8,128)S(1)} %copy-done.21), channel_id=1, source_target_pairs={{0,64},{32,96},{64,0},{96,32},{1,65},{33,97},{65,1},{97,33},{2,66}... | collective-permute-start | bytes 737288 | tf_op jit(solution)/shard_map/ppermute | solution.py:307
  119.0 19.1 %collective-permute-start.32 = (f32[8,7680]{1,0:T(8,128)S(1)}, f32[8,7680]{1,0:T(8,128)S(1)}, u32[]{:S(2)}, u32[]{:S(2)}) collective-permute-start(f32[8,7680]{1,0:T(8,128)S(1)} %copy-done.20), channel_id=1, source_target_pairs={{0,96},{32,0},{64,32},{96,64},{1,97},{33,1},{65,33},{97,65},{2,98}... | collective-permute-start | bytes 737288 | tf_op jit(solution)/shard_map/ppermute | solution.py:307
  121.9 14.2 %copy-start.19 = (f32[8,7680]{1,0:T(8,128)S(1)}, f32[8,7680]{1,0:T(8,128)}, u32[]{:S(2)}) copy-start(f32[8,7680]{1,0:T(8,128)} %get-tuple-element.52) | copy-start | bytes 737284
  121.9 14.7 %copy-start.30 = (f32[8,7680]{1,0:T(8,128)S(1)}, f32[8,7680]{1,0:T(8,128)}, u32[]{:S(2)}) copy-start(f32[8,7680]{1,0:T(8,128)} %get-tuple-element.62) | copy-start | bytes 737284
  136.1 20.0 %collective-permute-start.14 = (f32[8,7680]{1,0:T(8,128)S(1)}, f32[8,7680]{1,0:T(8,128)S(1)}, u32[]{:S(2)}, u32[]{:S(2)}) collective-permute-start(f32[8,7680]{1,0:T(8,128)S(1)} %copy-done.19), channel_id=1, source_target_pairs={{0,96},{32,0},{64,32},{96,64},{1,97},{33,1},{65,33},{97,65},{2,98}... | collective-permute-start | bytes 737288 | tf_op jit(solution)/shard_map/ppermute | solution.py:307
  136.6 22.0 %collective-permute-start.21 = (f32[8,7680]{1,0:T(8,128)S(1)}, f32[8,7680]{1,0:T(8,128)S(1)}, u32[]{:S(2)}, u32[]{:S(2)}) collective-permute-start(f32[8,7680]{1,0:T(8,128)S(1)} %copy-done.30), channel_id=1, source_target_pairs={{0,96},{32,0},{64,32},{96,64},{1,97},{33,1},{65,33},{97,65},{2,98}... | collective-permute-start | bytes 737288 | tf_op jit(solution)/shard_map/ppermute | solution.py:307
  138.1 20.6 %collective-permute-start.27 = (f32[8,7680]{1,0:T(8,128)}, f32[8,7680]{1,0:T(8,128)S(1)}, u32[]{:S(2)}, u32[]{:S(2)}) collective-permute-start(f32[8,7680]{1,0:T(8,128)} %get-tuple-element.70), channel_id=1, source_target_pairs={{0,96},{32,0},{64,32},{96,64},{1,97},{33,1},{65,33},{97,65},{2,98}... | collective-permute-start | bytes 737288 | tf_op jit(solution)/shard_map/ppermute | solution.py:307
  138.9 14.1 %copy-start.31 = (f32[8,7680]{1,0:T(8,128)S(1)}, f32[8,7680]{1,0:T(8,128)}, u32[]{:S(2)}) copy-start(f32[8,7680]{1,0:T(8,128)} %get-tuple-element.71) | copy-start | bytes 737284
  138.9 16.4 %copy-start.29 = (f32[8,7680]{1,0:T(8,128)S(1)}, f32[8,7680]{1,0:T(8,128)}, u32[]{:S(2)}) copy-start(f32[8,7680]{1,0:T(8,128)} %get-tuple-element.72) | copy-start | bytes 737284
  153.0 7.1 %copy-start.18 = (f32[8,7680]{1,0:T(8,128)}, f32[8,7680]{1,0:T(8,128)S(1)}, u32[]{:S(2)}) copy-start(f32[8,7680]{1,0:T(8,128)S(1)} %collective-permute-done.12.refs_1_) | copy-start | bytes 737284
  153.0 21.2 %collective-permute-start.28 = (f32[8,7680]{1,0:T(8,128)S(1)}, f32[8,7680]{1,0:T(8,128)S(1)}, u32[]{:S(2)}, u32[]{:S(2)}) collective-permute-start(f32[8,7680]{1,0:T(8,128)S(1)} %copy-done.31), channel_id=1, source_target_pairs={{0,64},{32,96},{64,0},{96,32},{1,65},{33,97},{65,1},{97,33},{2,66}... | collective-permute-start | bytes 737288 | tf_op jit(solution)/shard_map/ppermute | solution.py:307
  155.3 20.9 %collective-permute-start.29 = (f32[8,7680]{1,0:T(8,128)S(1)}, f32[8,7680]{1,0:T(8,128)S(1)}, u32[]{:S(2)}, u32[]{:S(2)}) collective-permute-start(f32[8,7680]{1,0:T(8,128)S(1)} %copy-done.29), channel_id=1, source_target_pairs={{0,32},{32,64},{64,96},{96,0},{1,33},{33,65},{65,97},{97,1},{2,34}... | collective-permute-start | bytes 737288 | tf_op jit(solution)/shard_map/ppermute | solution.py:307
  156.1 22.4 %collective-permute-start.33 = (f32[8,7680]{1,0:T(8,128)}, f32[8,7680]{1,0:T(8,128)S(1)}, u32[]{:S(2)}, u32[]{:S(2)}) collective-permute-start(f32[8,7680]{1,0:T(8,128)} %get-tuple-element.78), channel_id=1, source_target_pairs={{0,96},{32,0},{64,32},{96,64},{1,97},{33,1},{65,33},{97,65},{2,98}... | collective-permute-start | bytes 737288 | tf_op jit(solution)/shard_map/ppermute | solution.py:307
  158.6 15.6 %copy-start.7 = (f32[8,7680]{1,0:T(8,128)}, f32[8,7680]{1,0:T(8,128)S(1)}, u32[]{:S(2)}) copy-start(f32[8,7680]{1,0:T(8,128)S(1)} %collective-permute-done.21.refs_1_) | copy-start | bytes 737284
  158.6 20.0 %collective-permute-start.34 = (f32[8,7680]{1,0:T(8,128)}, f32[8,7680]{1,0:T(8,128)S(1)}, u32[]{:S(2)}, u32[]{:S(2)}) collective-permute-start(f32[8,7680]{1,0:T(8,128)} %get-tuple-element.79), channel_id=1, source_target_pairs={{0,64},{32,96},{64,0},{96,32},{1,65},{33,97},{65,1},{97,33},{2,66}... | collective-permute-start | bytes 737288 | tf_op jit(solution)/shard_map/ppermute | solution.py:307
  158.7 15.5 %copy-start.8 = (f32[8,7680]{1,0:T(8,128)}, f32[8,7680]{1,0:T(8,128)S(1)}, u32[]{:S(2)}) copy-start(f32[8,7680]{1,0:T(8,128)S(1)} %collective-permute-done.27.refs_1_) | copy-start | bytes 737284
  158.7 21.9 %collective-permute-start.35 = (f32[8,7680]{1,0:T(8,128)}, f32[8,7680]{1,0:T(8,128)S(1)}, u32[]{:S(2)}, u32[]{:S(2)}) collective-permute-start(f32[8,7680]{1,0:T(8,128)} %get-tuple-element.80), channel_id=1, source_target_pairs={{0,32},{32,64},{64,96},{96,0},{1,33},{33,65},{65,97},{97,1},{2,34}... | collective-permute-start | bytes 737288 | tf_op jit(solution)/shard_map/ppermute | solution.py:307
  160.1 16.2 %copy-start.28 = (f32[8,7680]{1,0:T(8,128)S(1)}, f32[8,7680]{1,0:T(8,128)}, u32[]{:S(2)}) copy-start(f32[8,7680]{1,0:T(8,128)} %get-tuple-element.63) | copy-start | bytes 737284
  160.1 18.4 %copy-start.27 = (f32[8,7680]{1,0:T(8,128)S(1)}, f32[8,7680]{1,0:T(8,128)}, u32[]{:S(2)}) copy-start(f32[8,7680]{1,0:T(8,128)} %get-tuple-element.64) | copy-start | bytes 737284
  174.2 10.8 %copy-start.9 = (f32[8,7680]{1,0:T(8,128)}, f32[8,7680]{1,0:T(8,128)S(1)}, u32[]{:S(2)}) copy-start(f32[8,7680]{1,0:T(8,128)S(1)} %collective-permute-done.28.refs_2_) | copy-start | bytes 737284
  174.2 20.7 %collective-permute-start.15 = (f32[8,7680]{1,0:T(8,128)}, f32[8,7680]{1,0:T(8,128)S(1)}, u32[]{:S(2)}, u32[]{:S(2)}) collective-permute-start(f32[8,7680]{1,0:T(8,128)} %get-tuple-element.54), channel_id=1, source_target_pairs={{0,96},{32,0},{64,32},{96,64},{1,97},{33,1},{65,33},{97,65},{2,98}... | collective-permute-start | bytes 737288 | tf_op jit(solution)/shard_map/ppermute | solution.py:307
  176.2 8.8 %copy-start.10 = (f32[8,7680]{1,0:T(8,128)}, f32[8,7680]{1,0:T(8,128)S(1)}, u32[]{:S(2)}) copy-start(f32[8,7680]{1,0:T(8,128)S(1)} %collective-permute-done.29.refs_3_) | copy-start | bytes 737284
  176.2 11.2 %collective-permute-start.22 = (f32[8,7680]{1,0:T(8,128)S(1)}, f32[8,7680]{1,0:T(8,128)S(1)}, u32[]{:S(2)}, u32[]{:S(2)}) collective-permute-start(f32[8,7680]{1,0:T(8,128)S(1)} %copy-done.28), channel_id=1, source_target_pairs={{0,64},{32,96},{64,0},{96,32},{1,65},{33,97},{65,1},{97,33},{2,66}... | collective-permute-start | bytes 737288 | tf_op jit(solution)/shard_map/ppermute | solution.py:307
  178.5 13.4 %collective-permute-start.23 = (f32[8,7680]{1,0:T(8,128)S(1)}, f32[8,7680]{1,0:T(8,128)S(1)}, u32[]{:S(2)}, u32[]{:S(2)}) collective-permute-start(f32[8,7680]{1,0:T(8,128)S(1)} %copy-done.27), channel_id=1, source_target_pairs={{0,32},{32,64},{64,96},{96,0},{1,33},{33,65},{65,97},{97,1},{2,34}... | collective-permute-start | bytes 737288 | tf_op jit(solution)/shard_map/ppermute | solution.py:307
  178.6 16.4 %collective-permute-start.16 = (f32[8,7680]{1,0:T(8,128)}, f32[8,7680]{1,0:T(8,128)S(1)}, u32[]{:S(2)}, u32[]{:S(2)}) collective-permute-start(f32[8,7680]{1,0:T(8,128)} %get-tuple-element.55), channel_id=1, source_target_pairs={{0,64},{32,96},{64,0},{96,32},{1,65},{33,97},{65,1},{97,33},{2,66}... | collective-permute-start | bytes 737288 | tf_op jit(solution)/shard_map/ppermute | solution.py:307
  180.7 16.5 %collective-permute-start.17 = (f32[8,7680]{1,0:T(8,128)}, f32[8,7680]{1,0:T(8,128)S(1)}, u32[]{:S(2)}, u32[]{:S(2)}) collective-permute-start(f32[8,7680]{1,0:T(8,128)} %get-tuple-element.56), channel_id=1, source_target_pairs={{0,32},{32,64},{64,96},{96,0},{1,33},{33,65},{65,97},{97,1},{2,34}... | collective-permute-start | bytes 737288 | tf_op jit(solution)/shard_map/ppermute | solution.py:307
  (21 other events, 60.2 us)

commit v2 on v0

v2 whole, which is shorter than its diff:
```python
import functools

import jax
import jax.numpy as jnp
from jax import lax
from jax.experimental import pallas as pl
from jax.experimental.pallas import tpu as pltpu
from jax.sharding import PartitionSpec as P

MEMBERS = 80
BLOCKS = 4
POINTS = 4
OBS = 256
GROUPS = 4
ROWS = MEMBERS // GROUPS
PADDED = 24
CELLS = 12288
CHUNKS = 4
EARLY = (0, 1, 2)
LATE = (3,)
PERMUTED = (1, 3)
CHUNK = CELLS // CHUNKS
HALF = CHUNK // 2
PACKED = 5 * HALF
COLS = OBS + (BLOCKS - 1) * POINTS * OBS
PART = COLS // 2
FAR = 128 + POINTS * 128
WIDE = 1024
UNROLL = 4
VMEM = 60 * 1024 * 1024

f32 = jnp.float32
bf16 = jnp.bfloat16


def split(x):
    hi = x.astype(bf16)
    lo = (x - hi.astype(f32)).astype(bf16)
    return hi, lo


def whole(n):
    return [pl.BlockSpec(memory_space=pltpu.VMEM)] * n


def smem(n):
    return [pl.BlockSpec(memory_space=pltpu.SMEM)] * n


def params():
    return pltpu.CompilerParams(vmem_limit_bytes=VMEM)


def cost(micros):
    return pl.CostEstimate(flops=0, bytes_accessed=int(micros * 1024), transcendentals=0)


def pack_kernel(ens_ref, *outs):
    for out_ref, chunks in zip(outs, (EARLY, LATE)):
        for q in range(GROUPS):
            for i, c in enumerate(chunks):
                o = i * PACKED
                at = q * CELLS + c * CHUNK
                mid = at + HALF
                out_ref[q, :, o : o + CHUNK] = ens_ref[0:8, at : at + CHUNK]
                out_ref[q, :, o + CHUNK : o + 2 * CHUNK] = ens_ref[8:16, at : at + CHUNK]
                out_ref[q, 0:4, o + 2 * CHUNK : o + PACKED] = ens_ref[16:20, at : at + HALF]
                out_ref[q, 4:8, o + 2 * CHUNK : o + PACKED] = ens_ref[16:20, mid : mid + HALF]


def pack(ensemble):
    return pl.pallas_call(
        pack_kernel,
        out_shape=[jax.ShapeDtypeStruct((GROUPS, 8, PACKED * len(c)), f32) for c in (EARLY, LATE)],
        in_specs=whole(1),
        out_specs=whole(2),
        compiler_params=params(),
        cost_estimate=cost(3),
        name="pack",
    )(ensemble)


def after_kernel(x_ref, first_ref, out_ref):
    pass


def after(x, first):
    anywhere = pl.BlockSpec(memory_space=pl.ANY)
    return pl.pallas_call(
        after_kernel,
        out_shape=jax.ShapeDtypeStruct(x.shape, x.dtype),
        in_specs=[anywhere, anywhere],
        out_specs=anywhere,
        input_output_aliases={0: 0},
        compiler_params=params(),
        cost_estimate=cost(1),
        name="after",
    )(x, first)


def pick_kernel(slab_ref, order_ref, owner_ref, cells_ref, weight_ref, ens_ref, after_ref, keep_ref, send_ref, held, *bufs):
    del after_ref
    slab = slab_ref[0]
    buf = bufs[POINTS]
    for point in bufs[:POINTS]:
        point[...] = jnp.zeros_like(point)

    blocks = [order_ref[t] for t in range(BLOCKS)]

    def scan(s, counts):
        counts = list(counts)
        for u in range(4):
            j = s * 4 + u
            for t in range(BLOCKS):
                held[t, counts[t]] = j
                counts[t] = counts[t] + jnp.where((owner_ref[blocks[t], j] >> 2) == slab, 1, 0)
        return tuple(counts)

    counts = lax.fori_loop(0, OBS // 4, scan, (jnp.int32(0),) * BLOCKS)
    lanes = lax.broadcasted_iota(jnp.int32, (8, 128), 1)
    lanes4 = lax.broadcasted_iota(jnp.int32, (4, 128), 1)
    for t in range(BLOCKS):
        count = counts[t]
        b = blocks[t]

        def some(s, carry):
            for u in range(UNROLL):
                i = s * UNROLL + u
                valid = i < count
                j = jnp.where(valid, held[t, i], 0)
                base = (owner_ref[b, j] & 3) * CELLS
                n = j & 127
                lane = jnp.where(valid, n, -1)
                hit = lanes == lane
                hit4 = lanes4 == lane
                dst = pl.ds(pl.multiple_of(t * OBS + (j - n), 128), 128)
                for k in range(POINTS):
                    point = bufs[k].at[u]
                    place = jnp.where(valid, base + cells_ref[b, k, j], 0)
                    src = pl.ds(pl.multiple_of((place >> 7) * 128, 128), 128)
                    shift = (n - place) & 127
                    point[0:8, dst] = jnp.where(hit, pltpu.roll(ens_ref[0:8, src], shift, 1), point[0:8, dst])
                    point[8:16, dst] = jnp.where(hit, pltpu.roll(ens_ref[8:16, src], shift, 1), point[8:16, dst])
                    point[16:20, dst] = jnp.where(hit4, pltpu.roll(ens_ref[16:20, src], shift, 1), point[16:20, dst])
            return carry

        lax.fori_loop(0, (count + UNROLL - 1) // UNROLL, some, 0)
    points = [sum(point[u] for u in range(1, UNROLL)) + point[0] for point in bufs[:POINTS]]
    weight = weight_ref[blocks[0]]
    total = points[0][:, 0:OBS] * weight[0:1, :]
    for k in range(1, POINTS):
        total = total + points[k][:, 0:OBS] * weight[k : k + 1, :]
    for h in range(2):
        half = slice(h * 128, h * 128 + 128)
        buf[h, :, 0:128] = total[:, half]
        for t in range(1, BLOCKS):
            for k in range(POINTS):
                o = 128 + ((t - 1) * POINTS + k) * 128
                at = t * OBS + h * 128
                buf[h, :, o : o + 128] = points[k][:, at : at + 128]
    part = lax.rem(slab, 2)
    keep_ref[...] = buf[part]
    send_ref[...] = buf[1 - part]


def pick(slab, order, owner, cells, weight, ensemble, after):
    return pl.pallas_call(
        pick_kernel,
        out_shape=[jax.ShapeDtypeStruct((PADDED, PART), f32)] * 2,
        in_specs=smem(4) + whole(2) + [pl.BlockSpec(memory_space=pl.ANY)],
        out_specs=whole(2),
        scratch_shapes=[pltpu.SMEM((BLOCKS, OBS + UNROLL), jnp.int32)]
        + [pltpu.VMEM((UNROLL, PADDED, BLOCKS * OBS), f32)] * POINTS
        + [pltpu.VMEM((2, PADDED, PART), f32)],
        compiler_params=params(),
        cost_estimate=cost(8),
        name="pick",
    )(slab, order, owner, cells, weight, ensemble, after)


def updated(x, place, lhs, driver, centre, inverse, slots):
    reps = x.shape[1] // 128
    mean = jnp.sum(x, axis=0, keepdims=True) * f32(1.0 / MEMBERS)
    hi, lo = split(x - mean)
    cov = jnp.dot(lhs, jnp.concatenate([hi, lo, hi], axis=0), preferred_element_type=f32)
    centre = jnp.concatenate([centre] * reps, axis=1)
    inverse = jnp.concatenate([inverse] * reps, axis=1)
    loc = jnp.maximum(f32(0.0), f32(1.0) - jnp.abs(place - centre) * inverse)
    hi, lo = split(loc * cov)
    if slots == 64:
        return x + jnp.dot(driver, jnp.concatenate([hi, lo, hi], axis=0), preferred_element_type=f32)
    if slots == 128:
        both = jnp.dot(driver, jnp.concatenate([hi, lo], axis=0), preferred_element_type=f32)
        return x + (both[:MEMBERS] + both[MEMBERS:])
    both = jnp.dot(driver, hi, preferred_element_type=f32)
    rest = jnp.dot(driver[:MEMBERS], lo, preferred_element_type=f32)
    return x + (both[:MEMBERS] + both[MEMBERS:] + rest)


def drivers_kernel(here_ref, order_ref, owner_ref, cells_ref, weight_ref, radius_ref, value_ref, variance_ref, *refs):
    mine_ref, other_ref = refs[:2]
    count_ref, lhs_ref, driver_ref, centre_ref, inverse_ref, z, place, full, whole_lhs, wide = refs[2:]
    here = here_ref[0]
    part = lax.rem(here // GROUPS, 2)
    for src, h in ((mine_ref, part), (other_ref, 1 - part)):
        for p in range(GROUPS):
            for i in range(PART // 128):
                cols = slice(i * 128, i * 128 + 128)
                at = pl.ds(pl.multiple_of(i * OBS + h * 128, 128), 128)
                z[16 * p : 16 * p + 16, at] = src[PADDED * p : PADDED * p + 16, cols]
                z[64 + 4 * p : 68 + 4 * p, at] = src[PADDED * p + 16 : PADDED * p + 20, cols]
    slot = lax.broadcasted_iota(jnp.int32, (OBS, OBS), 0)
    column = lax.broadcasted_iota(jnp.int32, (OBS, OBS), 1)
    before = jnp.where(slot < column, f32(1.0), f32(0.0)).astype(bf16)
    begin = (here * CELLS).astype(f32)
    end = begin + f32(CELLS - 1)

    for t in range(BLOCKS):
        b = order_ref[t]
        everywhere = (owner_ref[pl.ds(b, 1), :] * CELLS + cells_ref[b]).astype(f32)
        if t > 0:
            for k in range(POINTS):
                o = OBS + (t - 1) * POINTS * OBS + k * OBS
                place[:, o : o + OBS] = everywhere[k : k + 1, :]

    for t in range(BLOCKS):
        b = order_ref[t]
        start = OBS + (t - 1) * POINTS * OBS
        weight = weight_ref[b]
        if t == 0:
            prior = z[:, 0:OBS]
        else:
            prior = z[:, start : start + OBS] * weight[0:1, :]
            for k in range(1, POINTS):
                prior = prior + z[:, start + k * OBS : start + (k + 1) * OBS] * weight[k : k + 1, :]
        value = value_ref[pl.ds(b, 1), :]
        variance = variance_ref[pl.ds(b, 1), :]
        centre = (owner_ref[pl.ds(b, 1), :] * CELLS + cells_ref[b, 0:1, :]).astype(f32)
        radius = radius_ref[pl.ds(b, 1), :].astype(f32)
        inverse = f32(1.0) / radius
        ybar = jnp.sum(prior, axis=0, keepdims=True) * f32(1.0 / MEMBERS)
        anomaly = prior - ybar
        spread = jnp.sum(anomaly * anomaly, axis=0, keepdims=True) * f32(1.0 / (MEMBERS - 1))
        gain = f32(1.0) / (spread + variance)
        shrink = -gain / (f32(1.0) + jnp.sqrt(variance * gain))
        coeff = gain * (value - ybar)
        driver = coeff + shrink * anomaly
        hi, lo = split((anomaly * f32(1.0 / (MEMBERS - 1))).T)
        lhs = jnp.concatenate([hi, hi, lo], axis=1)
        dhi, dlo = split(driver)
        both = jnp.concatenate([dhi, dlo], axis=0)

        if t < BLOCKS - 1:
            terms = jnp.concatenate([centre, inverse, jnp.zeros((6, OBS), f32)], axis=0).T
            whole_lhs[...] = lhs
            full[...] = both
            wide[0] = jnp.broadcast_to(terms[:, 0:1], (OBS, 128))
            wide[1] = jnp.broadcast_to(terms[:, 1:2], (OBS, 128))

            def evolve(i, carry):
                cols = pl.ds(pl.multiple_of(OBS + i * WIDE, 128), WIDE)
                z[:, cols] = updated(z[:, cols], place[:, cols], whole_lhs[...], full[...], wide[0], wide[1], OBS)
                return carry

            lax.fori_loop(t * POINTS * OBS // WIDE, (BLOCKS - 1) * POINTS * OBS // WIDE, evolve, 0)

        away = jnp.maximum(jnp.maximum(begin - centre, centre - end), f32(0.0))
        active = jnp.where(away < radius, f32(1.0), f32(0.0))
        count = jnp.sum(active).astype(jnp.int32)
        count_ref[t] = count
        ahead = jnp.dot(jnp.broadcast_to(active, (8, OBS)).astype(bf16), before, preferred_element_type=f32)
        index = jnp.where(active > 0, ahead[0:1, :], f32(-1.0)).astype(jnp.int32)
        hit = index == slot
        chosen = jnp.where(hit, f32(1.0), f32(0.0)).astype(bf16)
        lhs_ref[t] = jnp.dot(chosen, lhs, preferred_element_type=f32).astype(bf16)
        centre_ref[t] = jnp.broadcast_to(jnp.sum(jnp.where(hit, centre, f32(0.0)), axis=1, keepdims=True), (OBS, 128))
        inverse_ref[t] = jnp.broadcast_to(jnp.sum(jnp.where(hit, inverse, f32(0.0)), axis=1, keepdims=True), (OBS, 128))
        nt = (((1,), (1,)), ((), ()))

        @pl.when(count <= 64)
        def _():
            again = jnp.where(index == (slot & 63), f32(1.0), f32(0.0)).astype(bf16)
            kept = lax.dot_general(both, again, nt, preferred_element_type=f32)
            lane = lax.broadcasted_iota(jnp.int32, (MEMBERS, OBS), 1)
            driver_ref[t, 0:MEMBERS] = jnp.where(lane < 128, kept[:MEMBERS], kept[MEMBERS:]).astype(bf16)

        @pl.when(count > 64)
        def _():
            kept = lax.dot_general(both, chosen, nt, preferred_element_type=f32).astype(bf16)
            driver_ref[t] = kept

            @pl.when(count <= 128)
            def _():
                driver_ref[t, 0:MEMBERS, 128:256] = kept[:MEMBERS, 0:128]
                driver_ref[t, MEMBERS : 2 * MEMBERS, 128:256] = jnp.zeros((MEMBERS, 128), bf16)


def drivers(here, order, owner, cells, weight, radius, value, variance, mine, other):
    return pl.pallas_call(
        drivers_kernel,
        out_shape=[
            jax.ShapeDtypeStruct((BLOCKS,), jnp.int32),
            jax.ShapeDtypeStruct((BLOCKS, OBS, 3 * MEMBERS), bf16),
            jax.ShapeDtypeStruct((BLOCKS, 2 * MEMBERS, OBS), bf16),
            jax.ShapeDtypeStruct((BLOCKS, OBS, 128), f32),
            jax.ShapeDtypeStruct((BLOCKS, OBS, 128), f32),
        ],
        in_specs=smem(2) + whole(8),
        out_specs=smem(1) + whole(4),
        scratch_shapes=[
            pltpu.VMEM((MEMBERS, COLS), f32),
            pltpu.VMEM((1, COLS), f32),
            pltpu.VMEM((2 * MEMBERS, OBS), bf16),
            pltpu.VMEM((OBS, 3 * MEMBERS), bf16),
            pltpu.VMEM((2, OBS, 128), f32),
        ],
        compiler_params=params(),
        cost_estimate=cost(8),
        name="drivers",
    )(here, order, owner, cells, weight, radius, value, variance, mine, other)


def update_kernel(chunk, apart, here_ref, count_ref, lhs_ref, driver_ref, centre_ref, inverse_ref, *refs):
    in_ref, x = refs[0], refs[-1]
    out_ref = refs[-2] if apart else refs[1]
    ins = [in_ref.at[q] for q in range(GROUPS)]
    outs = [out_ref.at[q] for q in range(GROUPS)]
    low = lax.broadcasted_iota(jnp.int32, (8, HALF), 0) < 4
    offsets = lax.broadcasted_iota(jnp.int32, (1, HALF), 1)
    first = here_ref[0] * CELLS + chunk * CHUNK

    def join(a, b):
        return jnp.where(low, a, pltpu.roll(b, 4, 0)), jnp.where(low, pltpu.roll(a, 4, 0), b)

    for p, ref in enumerate(ins):
        for h in range(2):
            x[h, 16 * p : 16 * p + 8] = ref[:, h * HALF : (h + 1) * HALF]
            x[h, 16 * p + 8 : 16 * p + 16] = ref[:, CHUNK + h * HALF : CHUNK + (h + 1) * HALF]
    for q in range(2):
        rest = join(ins[2 * q][:, 2 * CHUNK : PACKED], ins[2 * q + 1][:, 2 * CHUNK : PACKED])
        for h in range(2):
            x[h, 64 + 8 * q : 72 + 8 * q] = rest[h]

    def block(t, carry):
        count = count_ref[t]

        def apply(slots):
            width = 192 if slots == 64 else OBS
            height = MEMBERS if slots == 64 else 2 * MEMBERS
            lhs = lhs_ref[t, 0:slots]
            driver = driver_ref[t, 0:height, 0:width]
            for h in range(2):
                place = (first + h * HALF + offsets).astype(f32)
                x[h] = updated(x[h], place, lhs, driver, centre_ref[t, 0:slots], inverse_ref[t, 0:slots], slots)

        @pl.when((count > 0) & (count <= 64))
        def _():
            apply(64)

        @pl.when((count > 64) & (count <= 128))
        def _():
            apply(128)

        @pl.when(count > 128)
        def _():
            apply(OBS)

        return carry

    lax.fori_loop(0, BLOCKS, block, 0)
    for p, ref in enumerate(outs):
        for h in range(2):
            ref[:, h * HALF : (h + 1) * HALF] = x[h, 16 * p : 16 * p + 8]
            ref[:, CHUNK + h * HALF : CHUNK + (h + 1) * HALF] = x[h, 16 * p + 8 : 16 * p + 16]
    for q in range(2):
        a, b = join(x[0, 64 + 8 * q : 72 + 8 * q], x[1, 64 + 8 * q : 72 + 8 * q])
        outs[2 * q][:, 2 * CHUNK : PACKED] = a
        outs[2 * q + 1][:, 2 * CHUNK : PACKED] = b
    if apart:
        for d in range(GROUPS):
            refs[1 + d][...] = out_ref[lax.rem(here_ref[0] + d, GROUPS)]


def fixed(shape, index):
    return pl.BlockSpec(shape, lambda i: index, pipeline_mode=pl.Buffered(1))


def update(chunk, apart, index, here, terms, arrived):
    gathered = (GROUPS, 8, PACKED)
    shapes = [gathered[1:]] * GROUPS if apart else [gathered]
    return pl.pallas_call(
        functools.partial(update_kernel, chunk, apart),
        grid=(1,),
        out_shape=[jax.ShapeDtypeStruct(shape, f32) for shape in shapes],
        in_specs=smem(2)
        + [fixed(a.shape, (0, 0, 0)) for a in terms[1:]]
        + [fixed((GROUPS, 8, PACKED), (0, 0, index))],
        out_specs=[fixed(shape, (0,) * len(shape)) for shape in shapes],
        scratch_shapes=[pltpu.VMEM(gathered, f32)] * apart
        + [pltpu.VMEM((2, MEMBERS, HALF), f32)],
        compiler_params=params(),
        cost_estimate=cost(8),
        name="update",
    )(here, *terms, arrived)


def unpack_kernel(chunk, apart, rank_ref, *refs):
    out_ref, rows, sems = refs[-3:]
    copies = []
    for i in range(GROUPS):
        src = refs[i] if apart else refs[0].at[i]
        quarter = lax.rem(rank_ref[0] + GROUPS - i, GROUPS) if apart else i
        rows[i, 0:8, :] = src[:, 0:CHUNK]
        rows[i, 8:16, :] = src[:, CHUNK : 2 * CHUNK]
        rows[i, 16:20, 0:HALF] = src[0:4, 2 * CHUNK : PACKED]
        rows[i, 16:20, HALF:CHUNK] = src[4:8, 2 * CHUNK : PACKED]
        at = pl.multiple_of(quarter * CELLS + chunk * CHUNK, 128)
        copy = pltpu.make_async_copy(rows.at[i], out_ref.at[:, pl.ds(at, CHUNK)], sems.at[i])
        copy.start()
        copies.append(copy)
    for copy in copies:
        copy.wait()


def unpack(chunk, apart, rank, pieces, out):
    held = [] if out is None else [out]
    return pl.pallas_call(
        functools.partial(unpack_kernel, chunk, apart),
        out_shape=jax.ShapeDtypeStruct((ROWS, GROUPS * CELLS), f32),
        in_specs=smem(1) + whole(len(pieces)) + [pl.BlockSpec(memory_space=pl.ANY)] * len(held),
        out_specs=pl.BlockSpec(memory_space=pl.ANY),
        scratch_shapes=[pltpu.VMEM((GROUPS, ROWS, CHUNK), f32), pltpu.SemaphoreType.DMA((GROUPS,))],
        input_output_aliases={1 + len(pieces): 0} if held else {},
        compiler_params=params(),
        cost_estimate=cost(2),
        name="unpack",
    )(rank, *pieces, *held)


def shifted(x, axis, size, by):
    return lax.ppermute(x, axis, [(i, (i + by) % size) for i in range(size)])


def exchanged(x):
    return lax.all_to_all(x, "member", split_axis=0, concat_axis=0, tiled=True)


def per_device(
    ensemble,
    block_order,
    obs_owner,
    interp_cells,
    interp_weight,
    obs_radius,
    obs_value,
    obs_variance,
):
    slabs = lax.axis_size("slab")
    member_rank = lax.axis_index("member")
    slab_rank = lax.axis_index("slab")
    rank = member_rank.reshape(1)
    slab = slab_rank.reshape(1)
    here = slab * GROUPS + rank

    early, late = pack(ensemble)
    arrived = [exchanged(early)]

    cells = interp_cells.transpose(0, 2, 1)
    weight = interp_weight.transpose(0, 2, 1)
    keep, send = pick(slab, block_order, obs_owner, cells, weight, ensemble, early)
    chip = keep + lax.ppermute(send, "slab", [(i, i ^ 1) for i in range(slabs)])
    near = chip + shifted(chip, "slab", slabs, 2) + shifted(chip, "slab", slabs, -2)
    far = shifted(chip[:, :FAR], "slab", slabs, 4) + shifted(chip[:, :FAR], "slab", slabs, -4)
    window = jnp.concatenate([near[:, :FAR] + far, near[:, FAR:]], axis=1)
    mine = lax.all_gather(after(window, arrived[0]), "member", axis=0, tiled=True)
    other = lax.ppermute(mine, "slab", [(i, i ^ 1) for i in range(slabs)])
    arrived.append(exchanged(after(late, other)))
    terms = drivers(
        here, block_order, obs_owner, cells, weight, obs_radius, obs_value, obs_variance, mine, other
    )

    out = None
    for c in range(CHUNKS):
        group, index = (0, EARLY.index(c)) if c in EARLY else (1, LATE.index(c))
        apart = c in PERMUTED
        new = update(c, apart, index, here, terms, arrived[group])
        if c == 0:
            new = [after(new[0], arrived[1])]
        if apart:
            back = [new[0]] + [shifted(new[d], "member", GROUPS, d) for d in range(1, GROUPS)]
        else:
            back = [exchanged(new[0])]
        out = unpack(c, apart, rank, back, out)
    return out


def solution(mesh):
    in_specs = (P("member", "slab"), P(), P(), P(), P(), P(), P(), P())
    out_specs = P("member", "slab")
    return jax.shard_map(
        per_device, mesh=mesh, in_specs=in_specs, out_specs=out_specs, check_vma=False
    )
```

time: 916 us -> 145 us (0.16)
  waiting for transfers between devices: 591 us -> 28.4 us
  matrix products: 130 us -> 0 us
  local copies, waits for them, and re-layouts: 80.5 us -> 5.93 us
  Pallas kernels: 0 us -> 57.9 us
  blocking collectives: 58.5 us -> 13.8 us
  starting transfers between devices: 5.3 us -> 35.8 us
  between operations: 21.5 us -> 0.33 us
  other arithmetic: 22.8 us -> 1.65 us
    psum x4 -> x0, waiting for transfers between devices: 551 us -> none  [per_device(): lax.psum(local_priors(state, offsets, interp_weight[which], mine), ('memb...]
    dot_general x8 -> x0, matrix products: 130 us -> none  [the longest x4 70.3 us: apply_terms(): jnp.einsum('ec,be->cb', anomaly_x, anomaly_y, precision=lax.Precision.HIG...]
    all_to_all x1 -> x0, blocking collectives: 58.5 us -> none  [per_device(): lax.all_to_all(state, 'member', split_axis=0, concat_axis=1, tiled=True)]
    pallas_call x0 -> x14, Pallas kernels: none -> 57.9 us  [the longest x4 24.2 us: update(): pl.pallas_call(functools.partial(update_kernel, chunk, apart), grid=(1,),...]
    all_to_all x6 -> x0, local copies, waits for them, and re-layouts: 28.9 us -> none  [the longest x4 22.4 us: per_device(): lax.all_to_all(ensemble, 'member', split_axis=1, concat_axis=0, tiled=True)]
    all_to_all x1 -> x4, waiting for transfers between devices: 40.1 us -> 12.2 us  [exchanged(): return lax.all_to_all(x, 'member', split_axis=0, concat_axis=0, tiled=True)]
    gather x4 -> x0, local copies, waits for them, and re-layouts: 22.4 us -> none  [local_priors(): picked = jnp.take(state, cells, axis=1)]
    ppermute x0 -> x12, starting transfers between devices: none -> 19.6 us  [the longest x10 19.6 us: shifted(): return lax.ppermute(x, axis, [(i, (i + by) % size) for i in range(size)])]
  transfers between devices with their start and end apart: 5 -> 16, of which waited for: 5 -> 8; matrix products, arithmetic and copies ran while one was open for 1% -> 1% of each run, Pallas kernels for 0% -> 35%
where the time goes in v2:
time: 145 us; the launch traced here: 144 us
  Pallas kernels  57.9 us (40%)
  starting transfers between devices  35.8 us (25%)
  waiting for transfers between devices  28.4 us (20%)
  blocking collectives  13.8 us (10%)
  local copies, waits for them, and re-layouts  5.93 us (4%)
  other arithmetic  1.65 us (1%)
    pallas_call x4, Pallas kernels, update(): pl.pallas_call(functools.partial(update_kernel, chunk, apart), grid=(1,),...  24.2 us
    ppermute x10, starting transfers between devices, shifted(): return lax.ppermute(x, axis, [(i, (i + by) % size) for i in range(size)])  19.6 us
    all_to_all x4, starting transfers between devices, exchanged(): return lax.all_to_all(x, 'member', split_axis=0, concat_axis=0, tiled=True)  16.1 us
    all_gather x1, blocking collectives, per_device(): lax.all_gather(after(window, arrived[0]), 'member', axis=0, tiled=True)  13.8 us
    ppermute x10, waiting for transfers between devices, shifted(): return lax.ppermute(x, axis, [(i, (i + by) % size) for i in range(size)])  12.5 us
    all_to_all x4, waiting for transfers between devices, exchanged(): return lax.all_to_all(x, 'member', split_axis=0, concat_axis=0, tiled=True)  12.2 us
    pallas_call x1, Pallas kernels, drivers(): pl.pallas_call(drivers_kernel, out_shape=[jax.ShapeDtypeStruct((BLOCKS,),...  10 us
    pallas_call x1, Pallas kernels, pick(): pl.pallas_call(pick_kernel, out_shape=[jax.ShapeDtypeStruct((PADDED, PART...  9.86 us
  transfers between devices with their start and end apart: 16, of which 8 were waited for; matrix products, arithmetic and copies ran while one was open for 1% of the time, Pallas kernels for 35%

profile of v2, /device:TPU:0, one launch (start us, length us, event | category | flops | bytes accessed | tf_op | source)
XLA Modules:
  0.0 143.8 jit_solution(466854704857469073)
XLA Ops:
  0.0 4.5 %pack.1 = (f32[4,8,23040]{2,1,0:T(8,128)}, f32[4,8,7680]{2,1,0:T(8,128)}) custom-call(f32[20,49152]{1,0:T(8,128)} %ens_ref.3), custom_call_target="tpu_custom_call" | custom-call | bytes 3072 | tf_op jit(solution)/shard_map/pack/pallas_call | solution.py:72
  4.5 4.4 %all-to-all-start = ((f32[4,8,23040]{2,1,0:T(8,128)}), f32[4,8,23040]{2,1,0:T(8,128)S(1)}, u32[]{:S(2)}, u32[]{:S(2)}) async-start(f32[4,8,23040]{2,1,0:T(8,128)} %get-tuple-element.22.after_ref), calls=%async_computation | async-start | bytes 5898240 | tf_op jit(solution)/shard_map/all_to_all | solution.py:445
  8.9 9.9 %pick.1 = (f32[24,1664]{1,0:T(8,128)}, f32[24,1664]{1,0:T(8,128)}) custom-call(s32[1]{0:T(128)} %bitcast.1.slab_ref, s32[4]{0:T(128)} %order_ref.3, s32[4,256]{1,0:T(4,128)} %owner_ref.3, s32[4,4,256]{2,1,0:T(4,128)} %bitcast.4, f32[4,4,256]{2,1,0:T(4,128)} %bitcast.6, f32[20,49152]{1,0:T(8,128)} %ens_ref.3, f32[4,8,23040]{2,1,0:T(8,128)} %get-tuple-element.22.after_ref), custom_call_target="tpu_custom_call" | custom-call | bytes 8192 | tf_op jit(solution)/shard_map/pick/pallas_call | solution.py:167
  18.8 0.0 collective-permute-start
  18.8 1.6 %collective-permute-done = f32[24,1664]{1,0:T(8,128)S(1)} collective-permute-done((f32[24,1664]{1,0:T(8,128)}, f32[24,1664]{1,0:T(8,128)S(1)}, u32[]{:S(2)}, u32[]{:S(2)}) %collective-permute-start) | collective-permute-done | bytes 159776 | tf_op jit(solution)/shard_map/ppermute | solution.py:471
  20.4 0.9 add.19
  21.3 6.7 %collective-permute-start.2 = (f32[24,1664]{1,0:T(8,128)S(1)}, f32[24,1664]{1,0:T(8,128)S(1)}, u32[]{:S(2)}, u32[]{:S(2)}) collective-permute-start(f32[24,1664]{1,0:T(8,128)S(1)} %add.19), channel_id=1, source_target_pairs={{0,30},{1,31},{2,0},{3,1},{4,2},{5,3},{6,4},{7,5},{8,6},{9,7},{10,... | collective-permute-start | bytes 479240 | tf_op jit(solution)/shard_map/ppermute | solution.py:441
  28.0 0.0 collective-permute-start.1
  28.0 2.9 %collective-permute-start.4 = (f32[24,640]{1,0:T(8,128)S(1)}, f32[24,640]{1,0:T(8,128)S(1)}, u32[]{:S(2)}, u32[]{:S(2)}) collective-permute-start(f32[24,640]{1,0:T(8,128)S(1)} %slice.14), channel_id=1, source_target_pairs={{0,28},{1,29},{2,30},{3,31},{4,0},{5,1},{6,2},{7,3},{8,4},{9,5},{1... | collective-permute-start | bytes 184328 | tf_op jit(solution)/shard_map/ppermute | solution.py:441
  30.9 1.9 %collective-permute-start.3 = (f32[24,640]{1,0:T(8,128)S(1)}, f32[24,640]{1,0:T(8,128)S(1)}, u32[]{:S(2)}, u32[]{:S(2)}) collective-permute-start(f32[24,640]{1,0:T(8,128)S(1)} %slice.14), channel_id=1, source_target_pairs={{0,4},{1,5},{2,6},{3,7},{4,8},{5,9},{6,10},{7,11},{8,12},{9,13},{1... | collective-permute-start | bytes 184328 | tf_op jit(solution)/shard_map/ppermute | solution.py:441
  32.8 0.0 collective-permute-done.2
  32.8 7.0 %collective-permute-done.1 = f32[24,1664]{1,0:T(8,128)S(1)} collective-permute-done((f32[24,1664]{1,0:T(8,128)S(1)}, f32[24,1664]{1,0:T(8,128)S(1)}, u32[]{:S(2)}, u32[]{:S(2)}) %collective-permute-start.1) | collective-permute-done | bytes 159776 | tf_op jit(solution)/shard_map/ppermute | solution.py:441
  39.8 0.0 collective-permute-done.4
  39.8 0.0 collective-permute-done.3
  39.9 0.7 pad_maximum_fusion.x_ref
  40.5 3.8 %all-to-all-done.first_ref.refs_0_ = f32[4,8,23040]{2,1,0:T(8,128)S(1)} async-done(((f32[4,8,23040]{2,1,0:T(8,128)}), f32[4,8,23040]{2,1,0:T(8,128)S(1)}, u32[]{:S(2)}, u32[]{:S(2)}) %all-to-all-start) | async-done | bytes 2949152 | tf_op jit(solution)/shard_map/all_to_all | solution.py:445
  44.4 0.0 copy-start
  44.4 1.6 %copy-done = f32[4,8,23040]{2,1,0:T(8,128)} copy-done((f32[4,8,23040]{2,1,0:T(8,128)}, f32[4,8,23040]{2,1,0:T(8,128)S(1)}, u32[]{:S(2)}) %copy-start) | copy-done | bytes 2949144
  46.0 13.8 %all_gather.3.refs_0_ = f32[96,1664]{1,0:T(8,128)S(1)} all-gather(f32[24,1664]{1,0:T(8,128)} %after.3), channel_id=1, replica_groups=mesh['member'=4,'slab'=32] {'member'}, dimensions={0}, use_global_device_ids=true | all-gather | bytes 798720 | tf_op jit(solution)/shard_map/all_gather | solution.py:475
  59.8 0.0 copy-start.5
  59.8 0.0 collective-permute-start.5
  59.8 2.1 %collective-permute-done.5.refs_1_.first_ref = f32[96,1664]{1,0:T(8,128)S(1)} collective-permute-done((f32[96,1664]{1,0:T(8,128)S(1)}, f32[96,1664]{1,0:T(8,128)S(1)}, u32[]{:S(2)}, u32[]{:S(2)}) %collective-permute-start.5) | collective-permute-done | bytes 639008 | tf_op jit(solution)/shard_map/ppermute | solution.py:476
  61.8 0.0 copy-start.4
  61.8 0.8 copy-done.4
  62.7 3.5 %all-to-all-start.1 = ((f32[4,8,7680]{2,1,0:T(8,128)}), f32[4,8,7680]{2,1,0:T(8,128)S(1)}, u32[]{:S(2)}, u32[]{:S(2)}) async-start(f32[4,8,7680]{2,1,0:T(8,128)} %after.4), calls=%async_computation.1 | async-start | bytes 1966080 | tf_op jit(solution)/shard_map/all_to_all | solution.py:445
  66.2 0.0 copy-done.5
  66.2 10.0 %drivers.1 = (s32[4]{0:T(128)}, bf16[4,256,240]{2,1,0:T(8,128)(2,1)}, bf16[4,160,256]{2,1,0:T(8,128)(2,1)}, f32[4,256,128]{2,1,0:T(8,128)}, f32[4,256,128]{2,1,0:T(8,128)}) custom-call(s32[1]{0:T(128)S(6)} %add.18.here_ref, s32[4]{0:T(128)} %order_ref.3, s32[4,256]{1,0:T(4,128)} %owner_ref.3, s32[4,4,256]{2,1,0:T(4,128)} %bitcast.5, f32[4,4,256]{2,1,0:T(4,128)} %bitcast.7, ...), custom_call_target="tpu_custom_call" | custom-call | bytes 8192 | tf_op jit(solution)/shard_map/drivers/pallas_call | solution.py:299
  76.2 6.0 %update.7.x_ref = f32[4,8,7680]{2,1,0:T(8,128)} custom-call(s32[1]{0:T(128)S(6)} %add.18.here_ref, s32[4]{0:T(128)} %get-tuple-element.25.count_ref, bf16[4,256,240]{2,1,0:T(8,128)(2,1)} %get-tuple-element.26.lhs_ref, bf16[4,160,256]{2,1,0:T(8,128)(2,1)} %get-tuple-element.27.driver_ref, f32[4,256,128]{2,1,0:T(8,128)} %get-tuple-element.28.centre_ref, ...), custom_call_target="tpu_custom_call" | custom-call | bytes 8192 | tf_op jit(solution)/shard_map/update/pallas_call | solution.py:391
  82.3 0.0 all-to-all-done.1.refs_0_.first_ref
  82.3 0.0 copy-start.1
  82.3 0.9 copy-done.1
  83.2 4.8 %all-to-all-start.3 = ((f32[4,8,7680]{2,1,0:T(8,128)}), f32[4,8,7680]{2,1,0:T(8,128)S(1)}, u32[]{:S(2)}, u32[]{:S(2)}) async-start(f32[4,8,7680]{2,1,0:T(8,128)} %after.5), calls=%async_computation.3 | async-start | bytes 1966080 | tf_op jit(solution)/shard_map/all_to_all | solution.py:445
  88.0 6.0 %update.5 = f32[4,8,7680]{2,1,0:T(8,128)} custom-call(s32[1]{0:T(128)S(6)} %add.18.here_ref, s32[4]{0:T(128)} %get-tuple-element.25.count_ref, bf16[4,256,240]{2,1,0:T(8,128)(2,1)} %get-tuple-element.26.lhs_ref, bf16[4,160,256]{2,1,0:T(8,128)(2,1)} %get-tuple-element.27.driver_ref, f32[4,256,128]{2,1,0:T(8,128)} %get-tuple-element.28.centre_ref, ...), custom_call_target="tpu_custom_call" | custom-call | bytes 8192 | tf_op jit(solution)/shard_map/update/pallas_call | solution.py:391
  94.0 8.4 %all-to-all-done.3.refs_0_ = f32[4,8,7680]{2,1,0:T(8,128)S(1)} async-done(((f32[4,8,7680]{2,1,0:T(8,128)}), f32[4,8,7680]{2,1,0:T(8,128)S(1)}, u32[]{:S(2)}, u32[]{:S(2)}) %all-to-all-start.3) | async-done | bytes 983072 | tf_op jit(solution)/shard_map/all_to_all | solution.py:445
  102.4 3.5 %all-to-all-start.2 = ((f32[4,8,7680]{2,1,0:T(8,128)}), f32[4,8,7680]{2,1,0:T(8,128)S(1)}, u32[]{:S(2)}, u32[]{:S(2)}) async-start(f32[4,8,7680]{2,1,0:T(8,128)} %update.5), calls=%async_computation.2 | async-start | bytes 1966080 | tf_op jit(solution)/shard_map/all_to_all | solution.py:445
  105.9 6.1 %update.6 = (f32[8,7680]{1,0:T(8,128)}, f32[8,7680]{1,0:T(8,128)}, f32[8,7680]{1,0:T(8,128)}, f32[8,7680]{1,0:T(8,128)}) custom-call(s32[1]{0:T(128)S(6)} %add.18.here_ref, s32[4]{0:T(128)} %get-tuple-element.25.count_ref, bf16[4,256,240]{2,1,0:T(8,128)(2,1)} %get-tuple-element.26.lhs_ref, bf16[4,160,256]{2,1,0:T(8,128)(2,1)} %get-tuple-element.27.driver_ref, ...), custom_call_target="tpu_custom_call" | custom-call | bytes 8192 | tf_op jit(solution)/shard_map/update/pallas_call | solution.py:391
  112.0 2.0 %collective-permute-start.9 = (f32[8,7680]{1,0:T(8,128)}, f32[8,7680]{1,0:T(8,128)S(1)}, u32[]{:S(2)}, u32[]{:S(2)}) collective-permute-start(f32[8,7680]{1,0:T(8,128)} %get-tuple-element.36), channel_id=1, source_target_pairs={{0,32},{32,64},{64,96},{96,0},{1,33},{33,65},{65,97},{97,1},{2,34}... | collective-permute-start | bytes 737288 | tf_op jit(solution)/shard_map/ppermute | solution.py:441
  114.0 2.7 %collective-permute-start.10 = (f32[8,7680]{1,0:T(8,128)}, f32[8,7680]{1,0:T(8,128)S(1)}, u32[]{:S(2)}, u32[]{:S(2)}) collective-permute-start(f32[8,7680]{1,0:T(8,128)} %get-tuple-element.37), channel_id=1, source_target_pairs={{0,64},{32,96},{64,0},{96,32},{1,65},{33,97},{65,1},{97,33},{2,66}... | collective-permute-start | bytes 737288 | tf_op jit(solution)/shard_map/ppermute | solution.py:441
  116.6 1.5 %collective-permute-start.11 = (f32[8,7680]{1,0:T(8,128)}, f32[8,7680]{1,0:T(8,128)S(1)}, u32[]{:S(2)}, u32[]{:S(2)}) collective-permute-start(f32[8,7680]{1,0:T(8,128)} %get-tuple-element.38), channel_id=1, source_target_pairs={{0,96},{32,0},{64,32},{96,64},{1,97},{33,1},{65,33},{97,65},{2,98}... | collective-permute-start | bytes 737288 | tf_op jit(solution)/shard_map/ppermute | solution.py:441
  118.1 6.1 %update.4 = (f32[8,7680]{1,0:T(8,128)}, f32[8,7680]{1,0:T(8,128)}, f32[8,7680]{1,0:T(8,128)}, f32[8,7680]{1,0:T(8,128)}) custom-call(s32[1]{0:T(128)S(6)} %add.18.here_ref, s32[4]{0:T(128)} %get-tuple-element.25.count_ref, bf16[4,256,240]{2,1,0:T(8,128)(2,1)} %get-tuple-element.26.lhs_ref, bf16[4,160,256]{2,1,0:T(8,128)(2,1)} %get-tuple-element.27.driver_ref, ...), custom_call_target="tpu_custom_call" | custom-call | bytes 8192 | tf_op jit(solution)/shard_map/update/pallas_call | solution.py:391
  124.1 0.0 copy-done.2
  124.1 0.6 collective-permute-start.6
  124.7 0.9 collective-permute-start.7
  125.6 1.4 collective-permute-done.9.refs_1_
  127.0 0.6 collective-permute-start.8
  127.6 2.3 %unpack.4.refs_4_ = f32[20,49152]{1,0:T(8,128)} custom-call(s32[1]{0:T(128)} %bitcast.rank_ref, f32[4,8,7680]{2,1,0:T(8,128)} %copy-done.2), custom_call_target="tpu_custom_call" | custom-call | bytes 2048 | tf_op jit(solution)/shard_map/unpack/pallas_call | solution.py:427
  129.8 2.4 %collective-permute-done.10.refs_2_ = f32[8,7680]{1,0:T(8,128)S(1)} collective-permute-done((f32[8,7680]{1,0:T(8,128)}, f32[8,7680]{1,0:T(8,128)S(1)}, u32[]{:S(2)}, u32[]{:S(2)}) %collective-permute-start.10) | collective-permute-done | bytes 245792 | tf_op jit(solution)/shard_map/ppermute | solution.py:441
  132.3 0.0 collective-permute-done.11.refs_3_
  132.3 0.0 copy-done.8
  132.3 0.7 copy-done.9
  133.0 0.1 copy-done.10
  133.1 2.4 %unpack.5.refs_1_ = f32[20,49152]{1,0:T(8,128)} custom-call(s32[1]{0:T(128)} %bitcast.rank_ref, f32[8,7680]{1,0:T(8,128)} %get-tuple-element.35.refs_0_, f32[8,7680]{1,0:T(8,128)} %copy-done.8, f32[8,7680]{1,0:T(8,128)} %copy-done.9, f32[8,7680]{1,0:T(8,128)} %copy-done.10, f32[20,49152]{1,0:T(8,128)} %unpack.4.refs_4_), custom_call_target="tpu_custom_call", output_to_operand_aliasing={{}: (5, {})} | custom-call | bytes 2048 | tf_op jit(solution)/shard_map/unpack/pallas_call | solution.py:427
  135.4 0.0 all-to-all-done.2.refs_0_
  135.5 0.0 copy-start.3
  135.5 0.9 copy-done.3
  136.4 2.3 %unpack.6.refs_4_ = f32[20,49152]{1,0:T(8,128)} custom-call(s32[1]{0:T(128)} %bitcast.rank_ref, f32[4,8,7680]{2,1,0:T(8,128)} %copy-done.3, f32[20,49152]{1,0:T(8,128)} %unpack.5.refs_1_), custom_call_target="tpu_custom_call", output_to_operand_aliasing={{}: (2, {})} | custom-call | bytes 2048 | tf_op jit(solution)/shard_map/unpack/pallas_call | solution.py:427
  138.7 0.0 collective-permute-done.6.refs_1_
  138.7 0.0 copy-start.6
  138.7 1.7 %collective-permute-done.7.refs_2_ = f32[8,7680]{1,0:T(8,128)S(1)} collective-permute-done((f32[8,7680]{1,0:T(8,128)}, f32[8,7680]{1,0:T(8,128)S(1)}, u32[]{:S(2)}, u32[]{:S(2)}) %collective-permute-start.7) | collective-permute-done | bytes 245792 | tf_op jit(solution)/shard_map/ppermute | solution.py:441
  140.4 0.0 collective-permute-done.8.refs_3_
  140.4 0.0 copy-done.6
  140.4 0.7 copy-done.7
  141.1 0.1 copy-done.11
  141.2 2.4 %unpack.7 = f32[20,49152]{1,0:T(8,128)} custom-call(s32[1]{0:T(128)} %bitcast.rank_ref, f32[8,7680]{1,0:T(8,128)} %get-tuple-element.31.refs_0_, f32[8,7680]{1,0:T(8,128)} %copy-done.6, f32[8,7680]{1,0:T(8,128)} %copy-done.7, f32[8,7680]{1,0:T(8,128)} %copy-done.11, f32[20,49152]{1,0:T(8,128)} %unpack.6.refs_4_), custom_call_target="tpu_custom_call", output_to_operand_aliasing={{}: (5, {})} | custom-call | bytes 2048 | tf_op jit(solution)/shard_map/unpack/pallas_call | solution.py:427
  (13 shorter events, 0.1 us)
Async XLA Ops:
  4.5 39.8 %all-to-all-start = ((f32[4,8,23040]{2,1,0:T(8,128)}), f32[4,8,23040]{2,1,0:T(8,128)S(1)}, u32[]{:S(2)}, u32[]{:S(2)}) async-start(f32[4,8,23040]{2,1,0:T(8,128)} %get-tuple-element.22.after_ref), calls=%async_computation | async-start | bytes 5898240 | tf_op jit(solution)/shard_map/all_to_all | solution.py:445
  18.8 1.6 %collective-permute-start = (f32[24,1664]{1,0:T(8,128)}, f32[24,1664]{1,0:T(8,128)S(1)}, u32[]{:S(2)}, u32[]{:S(2)}) collective-permute-start(f32[24,1664]{1,0:T(8,128)} %get-tuple-element.24), channel_id=1, source_target_pairs={{0,1},{1,0},{2,3},{3,2},{4,5},{5,4},{6,7},{7,6},{8,9},{9,8},{10,11... | collective-permute-start | bytes 479240 | tf_op jit(solution)/shard_map/ppermute | solution.py:471
  21.3 11.5 %collective-permute-start.2 = (f32[24,1664]{1,0:T(8,128)S(1)}, f32[24,1664]{1,0:T(8,128)S(1)}, u32[]{:S(2)}, u32[]{:S(2)}) collective-permute-start(f32[24,1664]{1,0:T(8,128)S(1)} %add.19), channel_id=1, source_target_pairs={{0,30},{1,31},{2,0},{3,1},{4,2},{5,3},{6,4},{7,5},{8,6},{9,7},{10,... | collective-permute-start | bytes 479240 | tf_op jit(solution)/shard_map/ppermute | solution.py:441
  28.0 11.8 %collective-permute-start.1 = (f32[24,1664]{1,0:T(8,128)S(1)}, f32[24,1664]{1,0:T(8,128)S(1)}, u32[]{:S(2)}, u32[]{:S(2)}) collective-permute-start(f32[24,1664]{1,0:T(8,128)S(1)} %add.19), channel_id=1, source_target_pairs={{0,2},{1,3},{2,4},{3,5},{4,6},{5,7},{6,8},{7,9},{8,10},{9,11},{10,... | collective-permute-start | bytes 479240 | tf_op jit(solution)/shard_map/ppermute | solution.py:441
  28.0 11.8 %collective-permute-start.4 = (f32[24,640]{1,0:T(8,128)S(1)}, f32[24,640]{1,0:T(8,128)S(1)}, u32[]{:S(2)}, u32[]{:S(2)}) collective-permute-start(f32[24,640]{1,0:T(8,128)S(1)} %slice.14), channel_id=1, source_target_pairs={{0,28},{1,29},{2,30},{3,31},{4,0},{5,1},{6,2},{7,3},{8,4},{9,5},{1... | collective-permute-start | bytes 184328 | tf_op jit(solution)/shard_map/ppermute | solution.py:441
  30.9 8.9 %collective-permute-start.3 = (f32[24,640]{1,0:T(8,128)S(1)}, f32[24,640]{1,0:T(8,128)S(1)}, u32[]{:S(2)}, u32[]{:S(2)}) collective-permute-start(f32[24,640]{1,0:T(8,128)S(1)} %slice.14), channel_id=1, source_target_pairs={{0,4},{1,5},{2,6},{3,7},{4,8},{5,9},{6,10},{7,11},{8,12},{9,13},{1... | collective-permute-start | bytes 184328 | tf_op jit(solution)/shard_map/ppermute | solution.py:441
  44.4 1.6 %copy-start = (f32[4,8,23040]{2,1,0:T(8,128)}, f32[4,8,23040]{2,1,0:T(8,128)S(1)}, u32[]{:S(2)}) copy-start(f32[4,8,23040]{2,1,0:T(8,128)S(1)} %all-to-all-done.first_ref.refs_0_) | copy-start | bytes 8847364
  59.8 6.4 %copy-start.5 = (f32[96,1664]{1,0:T(8,128)}, f32[96,1664]{1,0:T(8,128)S(1)}, u32[]{:S(2)}) copy-start(f32[96,1664]{1,0:T(8,128)S(1)} %all_gather.3.refs_0_) | copy-start | bytes 1916932
  59.8 2.1 %collective-permute-start.5 = (f32[96,1664]{1,0:T(8,128)S(1)}, f32[96,1664]{1,0:T(8,128)S(1)}, u32[]{:S(2)}, u32[]{:S(2)}) collective-permute-start(f32[96,1664]{1,0:T(8,128)S(1)} %all_gather.3.refs_0_), channel_id=1, source_target_pairs={{0,1},{1,0},{2,3},{3,2},{4,5},{5,4},{6,7},{7,6},{8,9},{9,8},{10,11... | collective-permute-start | bytes 1916936 | tf_op jit(solution)/shard_map/ppermute | solution.py:476
  61.8 0.8 copy-start.4
  62.7 19.6 %all-to-all-start.1 = ((f32[4,8,7680]{2,1,0:T(8,128)}), f32[4,8,7680]{2,1,0:T(8,128)S(1)}, u32[]{:S(2)}, u32[]{:S(2)}) async-start(f32[4,8,7680]{2,1,0:T(8,128)} %after.4), calls=%async_computation.1 | async-start | bytes 1966080 | tf_op jit(solution)/shard_map/all_to_all | solution.py:445
  82.3 0.9 copy-start.1
  83.2 19.2 %all-to-all-start.3 = ((f32[4,8,7680]{2,1,0:T(8,128)}), f32[4,8,7680]{2,1,0:T(8,128)S(1)}, u32[]{:S(2)}, u32[]{:S(2)}) async-start(f32[4,8,7680]{2,1,0:T(8,128)} %after.5), calls=%async_computation.3 | async-start | bytes 1966080 | tf_op jit(solution)/shard_map/all_to_all | solution.py:445
  102.4 21.8 %copy-start.2 = (f32[4,8,7680]{2,1,0:T(8,128)}, f32[4,8,7680]{2,1,0:T(8,128)S(1)}, u32[]{:S(2)}) copy-start(f32[4,8,7680]{2,1,0:T(8,128)S(1)} %all-to-all-done.3.refs_0_) | copy-start | bytes 2949124
  102.4 33.1 %all-to-all-start.2 = ((f32[4,8,7680]{2,1,0:T(8,128)}), f32[4,8,7680]{2,1,0:T(8,128)S(1)}, u32[]{:S(2)}, u32[]{:S(2)}) async-start(f32[4,8,7680]{2,1,0:T(8,128)} %update.5), calls=%async_computation.2 | async-start | bytes 1966080 | tf_op jit(solution)/shard_map/all_to_all | solution.py:445
  112.0 15.0 %collective-permute-start.9 = (f32[8,7680]{1,0:T(8,128)}, f32[8,7680]{1,0:T(8,128)S(1)}, u32[]{:S(2)}, u32[]{:S(2)}) collective-permute-start(f32[8,7680]{1,0:T(8,128)} %get-tuple-element.36), channel_id=1, source_target_pairs={{0,32},{32,64},{64,96},{96,0},{1,33},{33,65},{65,97},{97,1},{2,34}... | collective-permute-start | bytes 737288 | tf_op jit(solution)/shard_map/ppermute | solution.py:441
  114.0 18.3 %collective-permute-start.10 = (f32[8,7680]{1,0:T(8,128)}, f32[8,7680]{1,0:T(8,128)S(1)}, u32[]{:S(2)}, u32[]{:S(2)}) collective-permute-start(f32[8,7680]{1,0:T(8,128)} %get-tuple-element.37), channel_id=1, source_target_pairs={{0,64},{32,96},{64,0},{96,32},{1,65},{33,97},{65,1},{97,33},{2,66}... | collective-permute-start | bytes 737288 | tf_op jit(solution)/shard_map/ppermute | solution.py:441
  116.6 15.7 %collective-permute-start.11 = (f32[8,7680]{1,0:T(8,128)}, f32[8,7680]{1,0:T(8,128)S(1)}, u32[]{:S(2)}, u32[]{:S(2)}) collective-permute-start(f32[8,7680]{1,0:T(8,128)} %get-tuple-element.38), channel_id=1, source_target_pairs={{0,96},{32,0},{64,32},{96,64},{1,97},{33,1},{65,33},{97,65},{2,98}... | collective-permute-start | bytes 737288 | tf_op jit(solution)/shard_map/ppermute | solution.py:441
  124.1 14.5 %collective-permute-start.6 = (f32[8,7680]{1,0:T(8,128)}, f32[8,7680]{1,0:T(8,128)S(1)}, u32[]{:S(2)}, u32[]{:S(2)}) collective-permute-start(f32[8,7680]{1,0:T(8,128)} %get-tuple-element.32), channel_id=1, source_target_pairs={{0,32},{32,64},{64,96},{96,0},{1,33},{33,65},{65,97},{97,1},{2,34}... | collective-permute-start | bytes 737288 | tf_op jit(solution)/shard_map/ppermute | solution.py:441
  124.7 15.7 %collective-permute-start.7 = (f32[8,7680]{1,0:T(8,128)}, f32[8,7680]{1,0:T(8,128)S(1)}, u32[]{:S(2)}, u32[]{:S(2)}) collective-permute-start(f32[8,7680]{1,0:T(8,128)} %get-tuple-element.33), channel_id=1, source_target_pairs={{0,64},{32,96},{64,0},{96,32},{1,65},{33,97},{65,1},{97,33},{2,66}... | collective-permute-start | bytes 737288 | tf_op jit(solution)/shard_map/ppermute | solution.py:441
  127.0 5.3 %copy-start.8 = (f32[8,7680]{1,0:T(8,128)}, f32[8,7680]{1,0:T(8,128)S(1)}, u32[]{:S(2)}) copy-start(f32[8,7680]{1,0:T(8,128)S(1)} %collective-permute-done.9.refs_1_) | copy-start | bytes 737284
  127.0 13.4 %collective-permute-start.8 = (f32[8,7680]{1,0:T(8,128)}, f32[8,7680]{1,0:T(8,128)S(1)}, u32[]{:S(2)}, u32[]{:S(2)}) collective-permute-start(f32[8,7680]{1,0:T(8,128)} %get-tuple-element.34), channel_id=1, source_target_pairs={{0,96},{32,0},{64,32},{96,64},{1,97},{33,1},{65,33},{97,65},{2,98}... | collective-permute-start | bytes 737288 | tf_op jit(solution)/shard_map/ppermute | solution.py:441
  132.3 0.7 copy-start.9
  132.3 0.8 copy-start.10
  135.5 1.0 copy-start.3
  138.7 1.7 %copy-start.6 = (f32[8,7680]{1,0:T(8,128)}, f32[8,7680]{1,0:T(8,128)S(1)}, u32[]{:S(2)}) copy-start(f32[8,7680]{1,0:T(8,128)S(1)} %collective-permute-done.6.refs_1_) | copy-start | bytes 737284
  140.4 0.7 copy-start.7
  140.4 0.8 copy-start.11

commit v3 on v2

--- a/solution.py
+++ b/solution.py
@@ -16,8 +16,8 @@
 PADDED = 24
 CELLS = 12288
 CHUNKS = 4
-EARLY = (0, 1, 2)
-LATE = (3,)
+EARLY = (0, 1)
+LATE = (2, 3)
 PERMUTED = (1, 3)
 CHUNK = CELLS // CHUNKS
 HALF = CHUNK // 2
@@ -27,7 +27,7 @@
 FAR = 128 + POINTS * 128
 WIDE = 1024
 UNROLL = 4
-VMEM = 60 * 1024 * 1024
+MIB = 1024 * 1024
 
 f32 = jnp.float32
 bf16 = jnp.bfloat16
@@ -47,58 +47,103 @@
     return [pl.BlockSpec(memory_space=pltpu.SMEM)] * n
 
 
-def params():
-    return pltpu.CompilerParams(vmem_limit_bytes=VMEM)
+def params(mib):
+    return pltpu.CompilerParams(vmem_limit_bytes=mib * MIB)
 
 
 def cost(micros):
     return pl.CostEstimate(flops=0, bytes_accessed=int(micros * 1024), transcendentals=0)
 
 
-def pack_kernel(ens_ref, *outs):
-    for out_ref, chunks in zip(outs, (EARLY, LATE)):
-        for q in range(GROUPS):
-            for i, c in enumerate(chunks):
-                o = i * PACKED
-                at = q * CELLS + c * CHUNK
-                mid = at + HALF
-                out_ref[q, :, o : o + CHUNK] = ens_ref[0:8, at : at + CHUNK]
-                out_ref[q, :, o + CHUNK : o + 2 * CHUNK] = ens_ref[8:16, at : at + CHUNK]
-                out_ref[q, 0:4, o + 2 * CHUNK : o + PACKED] = ens_ref[16:20, at : at + HALF]
-                out_ref[q, 4:8, o + 2 * CHUNK : o + PACKED] = ens_ref[16:20, mid : mid + HALF]
-
-
-def pack(ensemble):
+def place_piece(out, o, ens_ref, c):
+    at, mid = c * CHUNK, c * CHUNK + HALF
+    out[:, o : o + CHUNK] = ens_ref[0:8, at : at + CHUNK]
+    out[:, o + CHUNK : o + 2 * CHUNK] = ens_ref[8:16, at : at + CHUNK]
+    out[0:4, o + 2 * CHUNK : o + PACKED] = ens_ref[16:20, at : at + HALF]
+    out[4:8, o + 2 * CHUNK : o + PACKED] = ens_ref[16:20, mid : mid + HALF]
+
+
+def pack_kernel(rank_ref, slab_ref, order_ref, owner_ref, ens_ref, early_ref, *refs):
+    late_refs, lists_ref, owners = refs[:GROUPS], refs[GROUPS], refs[GROUPS + 1]
+    step = pl.program_id(0)
+
+    @pl.when(step == 1)
+    def _():
+        owners[...] = jnp.full_like(owners, -1)
+        for t in range(BLOCKS):
+            owners[t : t + 1, :] = owner_ref[pl.ds(order_ref[t], 1), :]
+        row = lax.broadcasted_iota(jnp.int32, (OBS, OBS), 0)
+        column = lax.broadcasted_iota(jnp.int32, (OBS, OBS), 1)
+        before = jnp.where(row < column, f32(1.0), f32(0.0)).astype(bf16)
+        inside = (owners[...] >> 2) == slab_ref[0]
+        ahead = jnp.dot(jnp.where(inside, f32(1.0), f32(0.0)).astype(bf16), before, preferred_element_type=f32)
+        index = jnp.where(inside, ahead, f32(-1.0)).T
+        for t in range(BLOCKS):
+            hit = index[:, t : t + 1] == column.astype(f32)
+            held = jnp.sum(jnp.where(hit, row.astype(f32), f32(0.0)), axis=0, keepdims=True)
+            lists_ref[t : t + 1, :] = held.astype(jnp.int32)
+        total = jnp.sum(jnp.where(inside, f32(1.0), f32(0.0)), axis=1, keepdims=True)
+        lists_ref[BLOCKS : 2 * BLOCKS, :] = jnp.broadcast_to(total[0:BLOCKS], (BLOCKS, OBS)).astype(jnp.int32)
+
+    for i, c in enumerate(EARLY):
+        place_piece(early_ref.at[0], i * PACKED, ens_ref, c)
+    for d in range(GROUPS):
+
+        @pl.when(step == d)
+        def _():
+            for i, c in enumerate(LATE):
+                place_piece(late_refs[d], i * PACKED, ens_ref, c)
+
+
+def pack(rank, slab, order, owner, ensemble):
+    late = jax.ShapeDtypeStruct((8, PACKED * len(LATE)), f32)
+
+    def quarter(i, rank_ref):
+        return lax.rem(rank_ref[0] + i, GROUPS)
+
     return pl.pallas_call(
         pack_kernel,
-        out_shape=[jax.ShapeDtypeStruct((GROUPS, 8, PACKED * len(c)), f32) for c in (EARLY, LATE)],
-        in_specs=whole(1),
-        out_specs=whole(2),
-        compiler_params=params(),
+        grid_spec=pltpu.PrefetchScalarGridSpec(
+            num_scalar_prefetch=3,
+            grid=(GROUPS,),
+            in_specs=[
+                pl.BlockSpec((BLOCKS, OBS), lambda i, *_: (0, 0)),
+                pl.BlockSpec((ROWS, CELLS), lambda i, r, *_: (0, quarter(i, r))),
+            ],
+            out_specs=[pl.BlockSpec((1, 8, PACKED * len(EARLY)), lambda i, r, *_: (quarter(i, r), 0, 0))]
+            + [pl.BlockSpec(late.shape, lambda i, *_: (0, 0))] * GROUPS
+            + [pl.BlockSpec((2 * BLOCKS, OBS), lambda i, *_: (0, 0))],
+            scratch_shapes=[pltpu.VMEM((2 * BLOCKS, OBS), jnp.int32)],
+        ),
+        out_shape=[jax.ShapeDtypeStruct((GROUPS, 8, PACKED * len(EARLY)), f32)]
+        + [late] * GROUPS
+        + [jax.ShapeDtypeStruct((2 * BLOCKS, OBS), jnp.int32)],
+        compiler_params=params(60),
         cost_estimate=cost(3),
         name="pack",
-    )(ensemble)
-
-
-def after_kernel(x_ref, first_ref, out_ref):
+    )(rank, slab, order, owner, ensemble)
+
+
+def after_kernel(*refs):
     pass
 
 
-def after(x, first):
+def after(xs, *firsts):
     anywhere = pl.BlockSpec(memory_space=pl.ANY)
+    n = len(xs)
     return pl.pallas_call(
         after_kernel,
-        out_shape=jax.ShapeDtypeStruct(x.shape, x.dtype),
-        in_specs=[anywhere, anywhere],
-        out_specs=anywhere,
-        input_output_aliases={0: 0},
-        compiler_params=params(),
+        out_shape=[jax.ShapeDtypeStruct(x.shape, x.dtype) for x in xs],
+        in_specs=[anywhere] * (n + len(firsts)),
+        out_specs=[anywhere] * n,
+        input_output_aliases={i: i for i in range(n)},
+        compiler_params=params(60),
         cost_estimate=cost(1),
         name="after",
-    )(x, first)
-
-
-def pick_kernel(slab_ref, order_ref, owner_ref, cells_ref, weight_ref, ens_ref, after_ref, keep_ref, send_ref, held, *bufs):
+    )(*xs, *firsts)
+
+
+def pick_kernel(slab_ref, order_ref, owner_ref, cells_ref, held, weight_ref, ens_ref, after_ref, keep_ref, send_ref, *bufs):
     del after_ref
     slab = slab_ref[0]
     buf = bufs[POINTS]
@@ -106,21 +151,10 @@
         point[...] = jnp.zeros_like(point)
 
     blocks = [order_ref[t] for t in range(BLOCKS)]
-
-    def scan(s, counts):
-        counts = list(counts)
-        for u in range(4):
-            j = s * 4 + u
-            for t in range(BLOCKS):
-                held[t, counts[t]] = j
-                counts[t] = counts[t] + jnp.where((owner_ref[blocks[t], j] >> 2) == slab, 1, 0)
-        return tuple(counts)
-
-    counts = lax.fori_loop(0, OBS // 4, scan, (jnp.int32(0),) * BLOCKS)
     lanes = lax.broadcasted_iota(jnp.int32, (8, 128), 1)
     lanes4 = lax.broadcasted_iota(jnp.int32, (4, 128), 1)
     for t in range(BLOCKS):
-        count = counts[t]
+        count = held[BLOCKS + t, 0]
         b = blocks[t]
 
         def some(s, carry):
@@ -163,19 +197,92 @@
     send_ref[...] = buf[1 - part]
 
 
-def pick(slab, order, owner, cells, weight, ensemble, after):
+def pick(slab, order, owner, cells, lists, weight, ensemble, after):
     return pl.pallas_call(
         pick_kernel,
         out_shape=[jax.ShapeDtypeStruct((PADDED, PART), f32)] * 2,
-        in_specs=smem(4) + whole(2) + [pl.BlockSpec(memory_space=pl.ANY)],
+        in_specs=smem(5) + whole(2) + [pl.BlockSpec(memory_space=pl.ANY)],
         out_specs=whole(2),
-        scratch_shapes=[pltpu.SMEM((BLOCKS, OBS + UNROLL), jnp.int32)]
-        + [pltpu.VMEM((UNROLL, PADDED, BLOCKS * OBS), f32)] * POINTS
+        scratch_shapes=[pltpu.VMEM((UNROLL, PADDED, BLOCKS * OBS), f32)] * POINTS
         + [pltpu.VMEM((2, PADDED, PART), f32)],
-        compiler_params=params(),
+        compiler_params=params(60),
         cost_estimate=cost(8),
         name="pick",
-    )(slab, order, owner, cells, weight, ensemble, after)
+    )(slab, order, owner, cells, lists, weight, ensemble, after)
+
+
+def window_kernel(chip_ref, *refs):
+    near, far, out_ref = refs[0:2], refs[2:4], refs[-1]
+    total = chip_ref[...] + near[0][...] + near[1][...]
+    out_ref[:, 0:FAR] = total[:, 0:FAR] + far[0][...] + far[1][...]
+    out_ref[:, FAR:PART] = total[:, FAR:PART]
+
+
+def window(chip, near, far, firsts):
+    return pl.pallas_call(
+        window_kernel,
+        out_shape=jax.ShapeDtypeStruct((PADDED, PART), f32),
+        in_specs=whole(5) + [pl.BlockSpec(memory_space=pl.ANY)] * len(firsts),
+        out_specs=pl.BlockSpec(memory_space=pltpu.VMEM),
+        compiler_params=params(4),
+        cost_estimate=cost(1),
+        name="window",
+    )(chip, *near, *far, *firsts)
+
+
+def reach_kernel(here_ref, order_ref, owner_ref, cells_ref, radius_ref, after_ref, *refs):
+    del after_ref
+    count_ref, index_ref, chosen_ref, centre_ref, inverse_ref, wide_ref, place = refs
+    slot = lax.broadcasted_iota(jnp.int32, (OBS, OBS), 0)
+    column = lax.broadcasted_iota(jnp.int32, (OBS, OBS), 1)
+    before = jnp.where(slot < column, f32(1.0), f32(0.0)).astype(bf16)
+    begin = (here_ref[0] * CELLS).astype(f32)
+    end = begin + f32(CELLS - 1)
+    place[:, 0:OBS] = jnp.zeros((1, OBS), f32)
+    for t in range(BLOCKS):
+        b = order_ref[t]
+        everywhere = (owner_ref[pl.ds(b, 1), :] * CELLS + cells_ref[b]).astype(f32)
+        if t > 0:
+            for k in range(POINTS):
+                o = OBS + (t - 1) * POINTS * OBS + k * OBS
+                place[:, o : o + OBS] = everywhere[k : k + 1, :]
+        centre = everywhere[0:1, :]
+        radius = radius_ref[pl.ds(b, 1), :].astype(f32)
+        inverse = f32(1.0) / radius
+        terms = jnp.concatenate([centre, inverse, jnp.zeros((6, OBS), f32)], axis=0).T
+        wide_ref[t, 0] = jnp.broadcast_to(terms[:, 0:1], (OBS, 128))
+        wide_ref[t, 1] = jnp.broadcast_to(terms[:, 1:2], (OBS, 128))
+        away = jnp.maximum(jnp.maximum(begin - centre, centre - end), f32(0.0))
+        active = jnp.where(away < radius, f32(1.0), f32(0.0))
+        count_ref[t] = jnp.sum(active).astype(jnp.int32)
+        ahead = jnp.dot(jnp.broadcast_to(active, (8, OBS)).astype(bf16), before, preferred_element_type=f32)
+        index = jnp.where(active > 0, ahead[0:1, :], f32(-1.0)).astype(jnp.int32)
+        index_ref[t] = index
+        hit = index == slot
+        chosen_ref[t] = jnp.where(hit, f32(1.0), f32(0.0)).astype(bf16)
+        centre_ref[t] = jnp.broadcast_to(jnp.sum(jnp.where(hit, centre, f32(0.0)), axis=1, keepdims=True), (OBS, 128))
+        inverse_ref[t] = jnp.broadcast_to(jnp.sum(jnp.where(hit, inverse, f32(0.0)), axis=1, keepdims=True), (OBS, 128))
+
+
+def reach(here, order, owner, cells, radius, first):
+    shape = jax.ShapeDtypeStruct
+    return pl.pallas_call(
+        reach_kernel,
+        out_shape=[
+            shape((BLOCKS,), jnp.int32),
+            shape((BLOCKS, 1, OBS), jnp.int32),
+            shape((BLOCKS, OBS, OBS), bf16),
+            shape((BLOCKS, OBS, 128), f32),
+            shape((BLOCKS, OBS, 128), f32),
+            shape((BLOCKS, 2, OBS, 128), f32),
+            shape((1, COLS), f32),
+        ],
+        in_specs=smem(2) + whole(3) + [pl.BlockSpec(memory_space=pl.ANY)],
+        out_specs=smem(1) + whole(6),
+        compiler_params=params(60),
+        cost_estimate=cost(2),
+        name="reach",
+    )(here, order, owner, cells, radius, first)
 
 
 def updated(x, place, lhs, driver, centre, inverse, slots):
@@ -197,11 +304,10 @@
     return x + (both[:MEMBERS] + both[MEMBERS:] + rest)
 
 
-def drivers_kernel(here_ref, order_ref, owner_ref, cells_ref, weight_ref, radius_ref, value_ref, variance_ref, *refs):
-    mine_ref, other_ref = refs[:2]
-    count_ref, lhs_ref, driver_ref, centre_ref, inverse_ref, z, place, full, whole_lhs, wide = refs[2:]
-    here = here_ref[0]
-    part = lax.rem(here // GROUPS, 2)
+def drivers_kernel(here_ref, order_ref, count_ref, *refs):
+    weight_ref, value_ref, variance_ref, index_ref, chosen_ref, wide, place, mine_ref, other_ref = refs[:9]
+    lhs_ref, driver_ref, z, full, whole_lhs = refs[9:]
+    part = lax.rem(here_ref[0] // GROUPS, 2)
     for src, h in ((mine_ref, part), (other_ref, 1 - part)):
         for p in range(GROUPS):
             for i in range(PART // 128):
@@ -209,19 +315,6 @@
                 at = pl.ds(pl.multiple_of(i * OBS + h * 128, 128), 128)
                 z[16 * p : 16 * p + 16, at] = src[PADDED * p : PADDED * p + 16, cols]
                 z[64 + 4 * p : 68 + 4 * p, at] = src[PADDED * p + 16 : PADDED * p + 20, cols]
-    slot = lax.broadcasted_iota(jnp.int32, (OBS, OBS), 0)
-    column = lax.broadcasted_iota(jnp.int32, (OBS, OBS), 1)
-    before = jnp.where(slot < column, f32(1.0), f32(0.0)).astype(bf16)
-    begin = (here * CELLS).astype(f32)
-    end = begin + f32(CELLS - 1)
-
-    for t in range(BLOCKS):
-        b = order_ref[t]
-        everywhere = (owner_ref[pl.ds(b, 1), :] * CELLS + cells_ref[b]).astype(f32)
-        if t > 0:
-            for k in range(POINTS):
-                o = OBS + (t - 1) * POINTS * OBS + k * OBS
-                place[:, o : o + OBS] = everywhere[k : k + 1, :]
 
     for t in range(BLOCKS):
         b = order_ref[t]
@@ -235,9 +328,6 @@
                 prior = prior + z[:, start + k * OBS : start + (k + 1) * OBS] * weight[k : k + 1, :]
         value = value_ref[pl.ds(b, 1), :]
         variance = variance_ref[pl.ds(b, 1), :]
-        centre = (owner_ref[pl.ds(b, 1), :] * CELLS + cells_ref[b, 0:1, :]).astype(f32)
-        radius = radius_ref[pl.ds(b, 1), :].astype(f32)
-        inverse = f32(1.0) / radius
         ybar = jnp.sum(prior, axis=0, keepdims=True) * f32(1.0 / MEMBERS)
         anomaly = prior - ybar
         spread = jnp.sum(anomaly * anomaly, axis=0, keepdims=True) * f32(1.0 / (MEMBERS - 1))
@@ -251,42 +341,31 @@
         both = jnp.concatenate([dhi, dlo], axis=0)
 
         if t < BLOCKS - 1:
-            terms = jnp.concatenate([centre, inverse, jnp.zeros((6, OBS), f32)], axis=0).T
             whole_lhs[...] = lhs
             full[...] = both
-            wide[0] = jnp.broadcast_to(terms[:, 0:1], (OBS, 128))
-            wide[1] = jnp.broadcast_to(terms[:, 1:2], (OBS, 128))
 
             def evolve(i, carry):
                 cols = pl.ds(pl.multiple_of(OBS + i * WIDE, 128), WIDE)
-                z[:, cols] = updated(z[:, cols], place[:, cols], whole_lhs[...], full[...], wide[0], wide[1], OBS)
+                z[:, cols] = updated(z[:, cols], place[:, cols], whole_lhs[...], full[...], wide[t, 0], wide[t, 1], OBS)
                 return carry
 
             lax.fori_loop(t * POINTS * OBS // WIDE, (BLOCKS - 1) * POINTS * OBS // WIDE, evolve, 0)
 
-        away = jnp.maximum(jnp.maximum(begin - centre, centre - end), f32(0.0))
-        active = jnp.where(away < radius, f32(1.0), f32(0.0))
-        count = jnp.sum(active).astype(jnp.int32)
-        count_ref[t] = count
-        ahead = jnp.dot(jnp.broadcast_to(active, (8, OBS)).astype(bf16), before, preferred_element_type=f32)
-        index = jnp.where(active > 0, ahead[0:1, :], f32(-1.0)).astype(jnp.int32)
-        hit = index == slot
-        chosen = jnp.where(hit, f32(1.0), f32(0.0)).astype(bf16)
-        lhs_ref[t] = jnp.dot(chosen, lhs, preferred_element_type=f32).astype(bf16)
-        centre_ref[t] = jnp.broadcast_to(jnp.sum(jnp.where(hit, centre, f32(0.0)), axis=1, keepdims=True), (OBS, 128))
-        inverse_ref[t] = jnp.broadcast_to(jnp.sum(jnp.where(hit, inverse, f32(0.0)), axis=1, keepdims=True), (OBS, 128))
+        count = count_ref[t]
+        lhs_ref[t] = jnp.dot(chosen_ref[t], lhs, preferred_element_type=f32).astype(bf16)
         nt = (((1,), (1,)), ((), ()))
 
         @pl.when(count <= 64)
         def _():
-            again = jnp.where(index == (slot & 63), f32(1.0), f32(0.0)).astype(bf16)
+            slot = lax.broadcasted_iota(jnp.int32, (OBS, OBS), 0)
+            again = jnp.where(index_ref[t] == (slot & 63), f32(1.0), f32(0.0)).astype(bf16)
             kept = lax.dot_general(both, again, nt, preferred_element_type=f32)
             lane = lax.broadcasted_iota(jnp.int32, (MEMBERS, OBS), 1)
             driver_ref[t, 0:MEMBERS] = jnp.where(lane < 128, kept[:MEMBERS], kept[MEMBERS:]).astype(bf16)
 
         @pl.when(count > 64)
         def _():
-            kept = lax.dot_general(both, chosen, nt, preferred_element_type=f32).astype(bf16)
+            kept = lax.dot_general(both, chosen_ref[t], nt, preferred_element_type=f32).astype(bf16)
             driver_ref[t] = kept
 
             @pl.when(count <= 128)
@@ -295,34 +374,37 @@
                 driver_ref[t, MEMBERS : 2 * MEMBERS, 128:256] = jnp.zeros((MEMBERS, 128), bf16)
 
 
-def drivers(here, order, owner, cells, weight, radius, value, variance, mine, other):
+def drivers(here, order, count, weight, value, variance, index, chosen, wide, place, mine, other):
     return pl.pallas_call(
         drivers_kernel,
         out_shape=[
-            jax.ShapeDtypeStruct((BLOCKS,), jnp.int32),
             jax.ShapeDtypeStruct((BLOCKS, OBS, 3 * MEMBERS), bf16),
             jax.ShapeDtypeStruct((BLOCKS, 2 * MEMBERS, OBS), bf16),
-            jax.ShapeDtypeStruct((BLOCKS, OBS, 128), f32),
-            jax.ShapeDtypeStruct((BLOCKS, OBS, 128), f32),
         ],
-        in_specs=smem(2) + whole(8),
-        out_specs=smem(1) + whole(4),
+        in_specs=smem(3) + whole(9),
+        out_specs=whole(2),
         scratch_shapes=[
             pltpu.VMEM((MEMBERS, COLS), f32),
-            pltpu.VMEM((1, COLS), f32),
             pltpu.VMEM((2 * MEMBERS, OBS), bf16),
             pltpu.VMEM((OBS, 3 * MEMBERS), bf16),
-            pltpu.VMEM((2, OBS, 128), f32),
         ],
-        compiler_params=params(),
+        compiler_params=params(60),
         cost_estimate=cost(8),
         name="drivers",
-    )(here, order, owner, cells, weight, radius, value, variance, mine, other)
-
-
-def update_kernel(chunk, apart, here_ref, count_ref, lhs_ref, driver_ref, centre_ref, inverse_ref, *refs):
-    in_ref, x = refs[0], refs[-1]
-    out_ref = refs[-2] if apart else refs[1]
+    )(here, order, count, weight, value, variance, index, chosen, wide, place, mine, other)
+
+
+def update_kernel(chunk, late, apart, here_ref, count_ref, lhs_ref, driver_ref, centre_ref, inverse_ref, *refs):
+    n_in = GROUPS if late else 1
+    given, made = refs[:n_in], refs[-3 - (GROUPS if apart else 1) :]
+    x, in_ref, out_ref = made[-3:]
+    if late:
+        for d in range(GROUPS):
+            in_ref[lax.rem(here_ref[0] + GROUPS - d, GROUPS)] = given[d][...]
+    else:
+        in_ref = given[0]
+    if not apart:
+        out_ref = made[0]
     ins = [in_ref.at[q] for q in range(GROUPS)]
     outs = [out_ref.at[q] for q in range(GROUPS)]
     low = lax.broadcasted_iota(jnp.int32, (8, HALF), 0) < 4
@@ -378,30 +460,30 @@
         outs[2 * q + 1][:, 2 * CHUNK : PACKED] = b
     if apart:
         for d in range(GROUPS):
-            refs[1 + d][...] = out_ref[lax.rem(here_ref[0] + d, GROUPS)]
+            made[d][...] = out_ref[lax.rem(here_ref[0] + d, GROUPS)]
 
 
 def fixed(shape, index):
     return pl.BlockSpec(shape, lambda i: index, pipeline_mode=pl.Buffered(1))
 
 
-def update(chunk, apart, index, here, terms, arrived):
+def update(chunk, late, apart, index, here, terms, arrived, firsts):
     gathered = (GROUPS, 8, PACKED)
     shapes = [gathered[1:]] * GROUPS if apart else [gathered]
     return pl.pallas_call(
-        functools.partial(update_kernel, chunk, apart),
+        functools.partial(update_kernel, chunk, late, apart),
         grid=(1,),
         out_shape=[jax.ShapeDtypeStruct(shape, f32) for shape in shapes],
         in_specs=smem(2)
         + [fixed(a.shape, (0, 0, 0)) for a in terms[1:]]
-        + [fixed((GROUPS, 8, PACKED), (0, 0, index))],
+        + ([fixed((8, PACKED), (0, index))] * GROUPS if late else [fixed(gathered, (0, 0, index))])
+        + [pl.BlockSpec(memory_space=pl.ANY)] * len(firsts),
         out_specs=[fixed(shape, (0,) * len(shape)) for shape in shapes],
-        scratch_shapes=[pltpu.VMEM(gathered, f32)] * apart
-        + [pltpu.VMEM((2, MEMBERS, HALF), f32)],
-        compiler_params=params(),
+        scratch_shapes=[pltpu.VMEM((2, MEMBERS, HALF), f32)] + [pltpu.VMEM(gathered, f32)] * 2,
+        compiler_params=params(60),
         cost_estimate=cost(8),
         name="update",
-    )(here, *terms, arrived)
+    )(here, *terms, *arrived, *firsts)
 
 
 def unpack_kernel(chunk, apart, rank_ref, *refs):
@@ -431,7 +513,7 @@
         out_specs=pl.BlockSpec(memory_space=pl.ANY),
         scratch_shapes=[pltpu.VMEM((GROUPS, ROWS, CHUNK), f32), pltpu.SemaphoreType.DMA((GROUPS,))],
         input_output_aliases={1 + len(pieces): 0} if held else {},
-        compiler_params=params(),
+        compiler_params=params(60),
         cost_estimate=cost(2),
         name="unpack",
     )(rank, *pieces, *held)
@@ -462,35 +544,42 @@
     slab = slab_rank.reshape(1)
     here = slab * GROUPS + rank
 
-    early, late = pack(ensemble)
-    arrived = [exchanged(early)]
-
     cells = interp_cells.transpose(0, 2, 1)
     weight = interp_weight.transpose(0, 2, 1)
-    keep, send = pick(slab, block_order, obs_owner, cells, weight, ensemble, early)
+    early, *late, lists = pack(rank, slab, block_order, obs_owner, ensemble)
+    entered = [exchanged(early)]
+    keep, send = pick(slab, block_order, obs_owner, cells, lists, weight, ensemble, early)
     chip = keep + lax.ppermute(send, "slab", [(i, i ^ 1) for i in range(slabs)])
-    near = chip + shifted(chip, "slab", slabs, 2) + shifted(chip, "slab", slabs, -2)
-    far = shifted(chip[:, :FAR], "slab", slabs, 4) + shifted(chip[:, :FAR], "slab", slabs, -4)
-    window = jnp.concatenate([near[:, :FAR] + far, near[:, FAR:]], axis=1)
-    mine = lax.all_gather(after(window, arrived[0]), "member", axis=0, tiled=True)
+    near = [shifted(chip, "slab", slabs, by) for by in (2, -2)]
+    far = [shifted(chip[:, :FAR], "slab", slabs, by) for by in (4, -4)]
+    count, index, chosen, centre, inverse, wide, place = reach(
+        here, block_order, obs_owner, cells, obs_radius, chip
+    )
+    summed = window(chip, near, far, [count])
+    mine = lax.all_gather(summed, "member", axis=0, tiled=True)
     other = lax.ppermute(mine, "slab", [(i, i ^ 1) for i in range(slabs)])
-    arrived.append(exchanged(after(late, other)))
-    terms = drivers(
-        here, block_order, obs_owner, cells, weight, obs_radius, obs_value, obs_variance, mine, other
+    late = after(late, mine, entered[0][0, :, 0:128])
+    late = [late[0]] + [shifted(late[d], "member", GROUPS, d) for d in range(1, GROUPS)]
+    lhs, driver = drivers(
+        here, block_order, count, weight, obs_value, obs_variance, index, chosen, wide, place, mine, other
     )
-
+    terms = (count, lhs, driver, centre, inverse)
+
+    made, firsts = [], []
+    for c in range(CHUNKS):
+        held = c in LATE
+        at = LATE.index(c) if held else EARLY.index(c)
+        made.append(update(c, held, c in PERMUTED, at, here, terms, late if held else entered, firsts))
+        firsts = [made[c][0]]
+    made[0] = after(made[0], *late[1:], made[1][0])
+    made[2] = after(made[2], made[3][0])
     out = None
-    for c in range(CHUNKS):
-        group, index = (0, EARLY.index(c)) if c in EARLY else (1, LATE.index(c))
-        apart = c in PERMUTED
-        new = update(c, apart, index, here, terms, arrived[group])
-        if c == 0:
-            new = [after(new[0], arrived[1])]
-        if apart:
+    for c, new in enumerate(made):
+        if c in PERMUTED:
             back = [new[0]] + [shifted(new[d], "member", GROUPS, d) for d in range(1, GROUPS)]
         else:
             back = [exchanged(new[0])]
-        out = unpack(c, apart, rank, back, out)
+        out = unpack(c, c in PERMUTED, rank, back, out)
     return out
 
 

time: 145 us -> 144 us (level)
  starting transfers between devices: 35.8 us -> 33.5 us
  Pallas kernels: 57.9 us -> 59.8 us
    ppermute x10 -> x13, waiting for transfers between devices: 12.5 us -> 23.4 us  [shifted(): return lax.ppermute(x, axis, [(i, (i + by) % size) for i in range(size)])]
    all_to_all x4 -> x3, waiting for transfers between devices: 12.2 us -> 2.13 us  [exchanged(): return lax.all_to_all(x, 'member', split_axis=0, concat_axis=0, tiled=True)]
    all_to_all x4 -> x3, starting transfers between devices: 16.1 us -> 11.6 us  [exchanged(): return lax.all_to_all(x, 'member', split_axis=0, concat_axis=0, tiled=True)]
    pallas_call x9 -> x11, Pallas kernels: 38.7 us -> 43 us  [the longest x4 24.3 us: update(): pl.pallas_call(functools.partial(update_kernel, chunk, late, apart), grid...]
    pallas_call x1, Pallas kernels: 9.86 us -> 7.39 us  [pick(): pl.pallas_call(pick_kernel, out_shape=[jax.ShapeDtypeStruct((PADDED, PART...]
    ppermute x10 -> x13, starting transfers between devices: 19.6 us -> 21.9 us  [shifted(): return lax.ppermute(x, axis, [(i, (i + by) % size) for i in range(size)])]
    ppermute x1, waiting for transfers between devices: 2.07 us -> 0.01 us  [per_device(): other = lax.ppermute(mine, 'slab', [(i, i ^ 1) for i in range(slabs)])]
    unnamed x24 -> x36, local copies, waits for them, and re-layouts: 5.91 us -> 5.84 us
  transfers between devices with their start and end apart: 16 -> 18, of which waited for: 8 -> 5; matrix products, arithmetic and copies ran while one was open for 1% -> 1% of each run, Pallas kernels for 35% -> 36%
where the time goes in v3:
time: 144 us; the launch traced here: 143 us
  Pallas kernels  59.8 us (42%)
  starting transfers between devices  33.5 us (23%)
  waiting for transfers between devices  27.1 us (19%)
  blocking collectives  14.4 us (10%)
  local copies, waits for them, and re-layouts  6.48 us (4%)
    pallas_call x4, Pallas kernels, update(): pl.pallas_call(functools.partial(update_kernel, chunk, late, apart), grid...  24.3 us
    ppermute x13, waiting for transfers between devices, shifted(): return lax.ppermute(x, axis, [(i, (i + by) % size) for i in range(size)])  23.4 us
    ppermute x13, starting transfers between devices, shifted(): return lax.ppermute(x, axis, [(i, (i + by) % size) for i in range(size)])  21.9 us
    all_gather x1, blocking collectives, per_device(): mine = lax.all_gather(summed, 'member', axis=0, tiled=True)  14.4 us
    all_to_all x3, starting transfers between devices, exchanged(): return lax.all_to_all(x, 'member', split_axis=0, concat_axis=0, tiled=True)  11.6 us
    pallas_call x4, Pallas kernels, unpack(): pl.pallas_call(functools.partial(unpack_kernel, chunk, apart), out_shape=...  9.35 us
    pallas_call x1, Pallas kernels, drivers(): pl.pallas_call(drivers_kernel, out_shape=[jax.ShapeDtypeStruct((BLOCKS, O...  9.33 us
    pallas_call x1, Pallas kernels, pick(): pl.pallas_call(pick_kernel, out_shape=[jax.ShapeDtypeStruct((PADDED, PART...  7.39 us
  transfers between devices with their start and end apart: 18, of which 5 were waited for; matrix products, arithmetic and copies ran while one was open for 1% of the time, Pallas kernels for 36%

profile of v3, /device:TPU:0, one launch (start us, length us, event | category | flops | bytes accessed | tf_op | source)
XLA Modules:
  0.0 142.6 jit_solution(7253960452648073145)
XLA Ops:
  0.0 6.1 %pack.1 = (f32[4,8,15360]{2,1,0:T(8,128)}, f32[8,15360]{1,0:T(8,128)}, f32[8,15360]{1,0:T(8,128)}, f32[8,15360]{1,0:T(8,128)}, f32[8,15360]{1,0:T(8,128)}, /*index=5*/s32[8,256]{1,0:T(8,128)}) custom-call(s32[1]{0:T(128)} %bitcast.rank_ref, s32[1]{0:T(128)} %bitcast.1.slab_ref, s32[4]{0:T(128)} %order_ref.7, s32[4,256]{1,0:T(4,128)} %owner_ref.5, ...), custom_call_target="tpu_custom_call" | custom-call | bytes 3072 | tf_op jit(solution)/shard_map/pack/pallas_call | solution.py:104
  6.1 4.4 %all-to-all-start = ((f32[4,8,15360]{2,1,0:T(8,128)}), f32[4,8,15360]{2,1,0:T(8,128)S(1)}, u32[]{:S(2)}, u32[]{:S(2)}) async-start(f32[4,8,15360]{2,1,0:T(8,128)} %get-tuple-element.35.after_ref), calls=%async_computation | async-start | bytes 3932160 | tf_op jit(solution)/shard_map/all_to_all | solution.py:527
  10.5 7.4 %pick.1 = (f32[24,1664]{1,0:T(8,128)}, f32[24,1664]{1,0:T(8,128)}) custom-call(s32[1]{0:T(128)} %bitcast.1.slab_ref, s32[4]{0:T(128)} %order_ref.7, s32[4,256]{1,0:T(4,128)} %owner_ref.5, s32[4,4,256]{2,1,0:T(4,128)} %bitcast.8, s32[8,256]{1,0:T(8,128)} %get-tuple-element.34.held, f32[4,4,256]{2,1,0:T(4,128)} %bitcast.6, f32[20,49152]{1,0:T(8,128)} %ens_ref.3, ...), custom_call_target="tpu_custom_call" | custom-call | bytes 8192 | tf_op jit(solution)/shard_map/pick/pallas_call | solution.py:201
  17.9 0.0 collective-permute-start
  17.9 1.6 %collective-permute-done = f32[24,1664]{1,0:T(8,128)S(1)} collective-permute-done((f32[24,1664]{1,0:T(8,128)}, f32[24,1664]{1,0:T(8,128)S(1)}, u32[]{:S(2)}, u32[]{:S(2)}) %collective-permute-start) | collective-permute-done | bytes 159776 | tf_op jit(solution)/shard_map/ppermute | solution.py:552
  19.5 0.9 add.7.after_ref.chip_ref
  20.4 0.0 copy-start
  20.4 3.9 %collective-permute-start.2 = (f32[24,1664]{1,0:T(8,128)S(1)}, f32[24,1664]{1,0:T(8,128)S(1)}, u32[]{:S(2)}, u32[]{:S(2)}) collective-permute-start(f32[24,1664]{1,0:T(8,128)S(1)} %add.7.after_ref.chip_ref), channel_id=1, source_target_pairs={{0,30},{1,31},{2,0},{3,1},{4,2},{5,3},{6,4},{7,5},{8,6},{9,7},{10,... | collective-permute-start | bytes 479240 | tf_op jit(solution)/shard_map/ppermute | solution.py:523
  24.3 0.0 collective-permute-start.1
  24.3 6.3 %collective-permute-start.4 = (f32[24,640]{1,0:T(8,128)S(1)}, f32[24,640]{1,0:T(8,128)S(1)}, u32[]{:S(2)}, u32[]{:S(2)}) collective-permute-start(f32[24,640]{1,0:T(8,128)S(1)} %slice.9), channel_id=1, source_target_pairs={{0,28},{1,29},{2,30},{3,31},{4,0},{5,1},{6,2},{7,3},{8,4},{9,5},{1... | collective-permute-start | bytes 184328 | tf_op jit(solution)/shard_map/ppermute | solution.py:523
  30.6 0.0 collective-permute-start.3
  30.6 3.2 %reach.1 = (s32[4]{0:T(128)}, s32[4,1,256]{2,1,0:T(1,128)}, bf16[4,256,256]{2,1,0:T(8,128)(2,1)}, f32[4,256,128]{2,1,0:T(8,128)}, f32[4,256,128]{2,1,0:T(8,128)}...) custom-call(s32[1]{0:T(128)S(6)} %add.6.here_ref, s32[4]{0:T(128)} %order_ref.7, s32[4,256]{1,0:T(4,128)} %owner_ref.5, ...), custom_call_target="tpu_custom_call" | custom-call | bytes 2048 | tf_op jit(solution)/shard_map/reach/pallas_call | solution.py:269
  33.9 0.0 collective-permute-done.4.refs_3_
  33.9 4.6 %collective-permute-done.3.refs_2_ = f32[24,640]{1,0:T(8,128)S(1)} collective-permute-done((f32[24,640]{1,0:T(8,128)S(1)}, f32[24,640]{1,0:T(8,128)S(1)}, u32[]{:S(2)}, u32[]{:S(2)}) %collective-permute-start.3) | collective-permute-done | bytes 61472 | tf_op jit(solution)/shard_map/ppermute | solution.py:523
  38.5 0.0 collective-permute-done.2.refs_1_
  38.5 0.0 collective-permute-done.1.refs_0_
  38.5 0.9 copy-done.1
  39.4 0.6 copy-done.2
  40.1 14.4 %all_gather.3.refs_7_.refs_4_ = f32[96,1664]{1,0:T(8,128)S(1)} all-gather(f32[24,1664]{1,0:T(8,128)S(1)} %window.1), channel_id=1, replica_groups=mesh['member'=4,'slab'=32] {'member'}, dimensions={0}, use_global_device_ids=true | all-gather | bytes 798720 | tf_op jit(solution)/shard_map/all_gather | solution.py:559
  54.4 0.0 collective-permute-start.5
  54.4 0.0 all-to-all-done.refs_0_
  54.4 0.0 copy-start.3
  54.4 0.6 slice_bitcast_fusion.refs_5_
  55.1 0.2 copy-done.4
  55.3 0.7 collective-permute-start.6
  55.9 2.7 %collective-permute-start.7 = (f32[8,15360]{1,0:T(8,128)}, f32[8,15360]{1,0:T(8,128)S(1)}, u32[]{:S(2)}, u32[]{:S(2)}) collective-permute-start(f32[8,15360]{1,0:T(8,128)} %get-tuple-element.53), channel_id=1, source_target_pairs={{0,64},{32,96},{64,0},{96,32},{1,65},{33,97},{65,1},{97,33},{2,66}... | collective-permute-start | bytes 1474568 | tf_op jit(solution)/shard_map/ppermute | solution.py:523
  58.6 0.8 collective-permute-start.8
  59.4 0.0 collective-permute-done.5.refs_8_
  59.4 9.3 %drivers.1 = (bf16[4,256,240]{2,1,0:T(8,128)(2,1)}, bf16[4,160,256]{2,1,0:T(8,128)(2,1)}) custom-call(s32[1]{0:T(128)S(6)} %add.6.here_ref, s32[4]{0:T(128)} %order_ref.7, s32[4]{0:T(128)} %get-tuple-element.38.refs_4_.count_ref, f32[4,4,256]{2,1,0:T(4,128)} %bitcast.7, f32[4,256]{1,0:T(4,128)} %refs_1_.1, f32[4,256]{1,0:T(4,128)} %refs_2_.1, ...), custom_call_target="tpu_custom_call" | custom-call | bytes 8192 | tf_op jit(solution)/shard_map/drivers/pallas_call | solution.py:378
  68.7 6.0 %update.4.refs_1_.refs_0_ = f32[4,8,7680]{2,1,0:T(8,128)} custom-call(s32[1]{0:T(128)S(6)} %add.6.here_ref, s32[4]{0:T(128)} %get-tuple-element.38.refs_4_.count_ref, bf16[4,256,240]{2,1,0:T(8,128)(2,1)} %get-tuple-element.43.lhs_ref, bf16[4,160,256]{2,1,0:T(8,128)(2,1)} %get-tuple-element.44.driver_ref, f32[4,256,128]{2,1,0:T(8,128)} %get-tuple-element.45.centre_ref, ...), custom_call_target="tpu_custom_call" | custom-call | bytes 8192 | tf_op jit(solution)/shard_map/update/pallas_call | solution.py:473
  74.7 6.0 %update.5 = (f32[8,7680]{1,0:T(8,128)}, f32[8,7680]{1,0:T(8,128)}, f32[8,7680]{1,0:T(8,128)}, f32[8,7680]{1,0:T(8,128)}) custom-call(s32[1]{0:T(128)S(6)} %add.6.here_ref, s32[4]{0:T(128)} %get-tuple-element.38.refs_4_.count_ref, bf16[4,256,240]{2,1,0:T(8,128)(2,1)} %get-tuple-element.43.lhs_ref, bf16[4,160,256]{2,1,0:T(8,128)(2,1)} %get-tuple-element.44.driver_ref, ...), custom_call_target="tpu_custom_call" | custom-call | bytes 8192 | tf_op jit(solution)/shard_map/update/pallas_call | solution.py:473
  80.7 0.0 collective-permute-done.6.refs_1_
  80.8 0.0 collective-permute-done.7.refs_2_
  80.8 0.6 collective-permute-done.8.refs_3_
  81.4 0.2 copy-done.5
  81.5 0.2 copy-done.6
  81.7 3.7 %all-to-all-start.2 = ((f32[4,8,7680]{2,1,0:T(8,128)}), f32[4,8,7680]{2,1,0:T(8,128)S(1)}, u32[]{:S(2)}, u32[]{:S(2)}) async-start(f32[4,8,7680]{2,1,0:T(8,128)} %after.5), calls=%async_computation.2 | async-start | bytes 1966080 | tf_op jit(solution)/shard_map/all_to_all | solution.py:527
  85.4 6.1 %update.6.refs_4_.refs_0_ = f32[4,8,7680]{2,1,0:T(8,128)} custom-call(s32[1]{0:T(128)S(6)} %add.6.here_ref, s32[4]{0:T(128)} %get-tuple-element.38.refs_4_.count_ref, bf16[4,256,240]{2,1,0:T(8,128)(2,1)} %get-tuple-element.43.lhs_ref, bf16[4,160,256]{2,1,0:T(8,128)(2,1)} %get-tuple-element.44.driver_ref, f32[4,256,128]{2,1,0:T(8,128)} %get-tuple-element.45.centre_ref, ...), custom_call_target="tpu_custom_call" | custom-call | bytes 8192 | tf_op jit(solution)/shard_map/update/pallas_call | solution.py:473
  91.6 6.2 %update.7 = (f32[8,7680]{1,0:T(8,128)}, f32[8,7680]{1,0:T(8,128)}, f32[8,7680]{1,0:T(8,128)}, f32[8,7680]{1,0:T(8,128)}) custom-call(s32[1]{0:T(128)S(6)} %add.6.here_ref, s32[4]{0:T(128)} %get-tuple-element.38.refs_4_.count_ref, bf16[4,256,240]{2,1,0:T(8,128)(2,1)} %get-tuple-element.43.lhs_ref, bf16[4,160,256]{2,1,0:T(8,128)(2,1)} %get-tuple-element.44.driver_ref, ...), custom_call_target="tpu_custom_call" | custom-call | bytes 8192 | tf_op jit(solution)/shard_map/update/pallas_call | solution.py:473
  97.7 2.1 %all-to-all-done.2.refs_0_ = f32[4,8,7680]{2,1,0:T(8,128)S(1)} async-done(((f32[4,8,7680]{2,1,0:T(8,128)}), f32[4,8,7680]{2,1,0:T(8,128)S(1)}, u32[]{:S(2)}, u32[]{:S(2)}) %all-to-all-start.2) | async-done | bytes 983072 | tf_op jit(solution)/shard_map/all_to_all | solution.py:527
  99.9 3.5 %all-to-all-start.1 = ((f32[4,8,7680]{2,1,0:T(8,128)}), f32[4,8,7680]{2,1,0:T(8,128)S(1)}, u32[]{:S(2)}, u32[]{:S(2)}) async-start(f32[4,8,7680]{2,1,0:T(8,128)} %after.4), calls=%async_computation.1 | async-start | bytes 1966080 | tf_op jit(solution)/shard_map/all_to_all | solution.py:527
  103.4 2.0 %collective-permute-start.12 = (f32[8,7680]{1,0:T(8,128)S(1)}, f32[8,7680]{1,0:T(8,128)S(1)}, u32[]{:S(2)}, u32[]{:S(2)}) collective-permute-start(f32[8,7680]{1,0:T(8,128)S(1)} %copy-done.17), channel_id=1, source_target_pairs={{0,32},{32,64},{64,96},{96,0},{1,33},{33,65},{65,97},{97,1},{2,34}... | collective-permute-start | bytes 737288 | tf_op jit(solution)/shard_map/ppermute | solution.py:523
  105.4 2.7 %collective-permute-start.13 = (f32[8,7680]{1,0:T(8,128)S(1)}, f32[8,7680]{1,0:T(8,128)S(1)}, u32[]{:S(2)}, u32[]{:S(2)}) collective-permute-start(f32[8,7680]{1,0:T(8,128)S(1)} %copy-done.16), channel_id=1, source_target_pairs={{0,64},{32,96},{64,0},{96,32},{1,65},{33,97},{65,1},{97,33},{2,66}... | collective-permute-start | bytes 737288 | tf_op jit(solution)/shard_map/ppermute | solution.py:523
  108.1 1.5 %collective-permute-start.14 = (f32[8,7680]{1,0:T(8,128)S(1)}, f32[8,7680]{1,0:T(8,128)S(1)}, u32[]{:S(2)}, u32[]{:S(2)}) collective-permute-start(f32[8,7680]{1,0:T(8,128)S(1)} %copy-done.15), channel_id=1, source_target_pairs={{0,96},{32,0},{64,32},{96,64},{1,97},{33,1},{65,33},{97,65},{2,98}... | collective-permute-start | bytes 737288 | tf_op jit(solution)/shard_map/ppermute | solution.py:523
  109.5 0.6 collective-permute-start.9
  110.1 0.9 collective-permute-start.10
  111.0 18.2 %collective-permute-done.12.refs_1_ = f32[8,7680]{1,0:T(8,128)S(1)} collective-permute-done((f32[8,7680]{1,0:T(8,128)S(1)}, f32[8,7680]{1,0:T(8,128)S(1)}, u32[]{:S(2)}, u32[]{:S(2)}) %collective-permute-start.12) | collective-permute-done | bytes 245792 | tf_op jit(solution)/shard_map/ppermute | solution.py:523
  129.2 0.0 collective-permute-start.11
  129.2 2.4 %unpack.4.refs_4_ = f32[20,49152]{1,0:T(8,128)} custom-call(s32[1]{0:T(128)} %bitcast.rank_ref, f32[4,8,7680]{2,1,0:T(8,128)} %copy-done.7), custom_call_target="tpu_custom_call" | custom-call | bytes 2048 | tf_op jit(solution)/shard_map/unpack/pallas_call | solution.py:509
  131.5 0.0 collective-permute-done.13.refs_2_
  131.5 0.0 collective-permute-done.14.refs_3_
  131.6 0.7 copy-done.13
  132.2 0.7 copy-done.14
  132.9 2.4 %unpack.5.refs_1_ = f32[20,49152]{1,0:T(8,128)} custom-call(s32[1]{0:T(128)} %bitcast.rank_ref, f32[8,7680]{1,0:T(8,128)} %get-tuple-element.55.refs_4_.refs_0_, f32[8,7680]{1,0:T(8,128)} %copy-done.12, f32[8,7680]{1,0:T(8,128)} %copy-done.13, f32[8,7680]{1,0:T(8,128)} %copy-done.14, f32[20,49152]{1,0:T(8,128)} %unpack.4.refs_4_), custom_call_target="tpu_custom_call", output_to_operand_aliasing={{}: (5, {})} | custom-call | bytes 2048 | tf_op jit(solution)/shard_map/unpack/pallas_call | solution.py:509
  135.3 0.0 all-to-all-done.1.refs_0_
  135.3 1.0 copy-done.8
  136.3 2.3 %unpack.6.refs_4_ = f32[20,49152]{1,0:T(8,128)} custom-call(s32[1]{0:T(128)} %bitcast.rank_ref, f32[4,8,7680]{2,1,0:T(8,128)} %copy-done.8, f32[20,49152]{1,0:T(8,128)} %unpack.5.refs_1_), custom_call_target="tpu_custom_call", output_to_operand_aliasing={{}: (2, {})} | custom-call | bytes 2048 | tf_op jit(solution)/shard_map/unpack/pallas_call | solution.py:509
  138.6 0.0 collective-permute-done.9.refs_1_
  138.6 0.0 collective-permute-done.10.refs_2_
  138.6 0.0 collective-permute-done.11.refs_3_
  138.6 0.7 copy-done.9
  139.3 0.1 copy-done.10
  139.4 0.7 copy-done.11
  140.1 2.4 %unpack.7 = f32[20,49152]{1,0:T(8,128)} custom-call(s32[1]{0:T(128)} %bitcast.rank_ref, f32[8,7680]{1,0:T(8,128)} %get-tuple-element.56.refs_1_.refs_0_, f32[8,7680]{1,0:T(8,128)} %copy-done.9, f32[8,7680]{1,0:T(8,128)} %copy-done.10, f32[8,7680]{1,0:T(8,128)} %copy-done.11, f32[20,49152]{1,0:T(8,128)} %unpack.6.refs_4_), custom_call_target="tpu_custom_call", output_to_operand_aliasing={{}: (5, {})} | custom-call | bytes 2048 | tf_op jit(solution)/shard_map/unpack/pallas_call | solution.py:509
  (28 shorter events, 0.1 us)
Async XLA Ops:
  6.1 48.3 %all-to-all-start = ((f32[4,8,15360]{2,1,0:T(8,128)}), f32[4,8,15360]{2,1,0:T(8,128)S(1)}, u32[]{:S(2)}, u32[]{:S(2)}) async-start(f32[4,8,15360]{2,1,0:T(8,128)} %get-tuple-element.35.after_ref), calls=%async_computation | async-start | bytes 3932160 | tf_op jit(solution)/shard_map/all_to_all | solution.py:527
  17.9 1.6 %collective-permute-start = (f32[24,1664]{1,0:T(8,128)}, f32[24,1664]{1,0:T(8,128)S(1)}, u32[]{:S(2)}, u32[]{:S(2)}) collective-permute-start(f32[24,1664]{1,0:T(8,128)} %get-tuple-element.37), channel_id=1, source_target_pairs={{0,1},{1,0},{2,3},{3,2},{4,5},{5,4},{6,7},{7,6},{8,9},{9,8},{10,11... | collective-permute-start | bytes 479240 | tf_op jit(solution)/shard_map/ppermute | solution.py:552
  20.4 10.2 %copy-start = (f32[24,1664]{1,0:T(8,128)}, f32[24,1664]{1,0:T(8,128)S(1)}, u32[]{:S(2)}) copy-start(f32[24,1664]{1,0:T(8,128)S(1)} %add.7.after_ref.chip_ref) | copy-start | bytes 479236
  20.4 18.1 %collective-permute-start.2 = (f32[24,1664]{1,0:T(8,128)S(1)}, f32[24,1664]{1,0:T(8,128)S(1)}, u32[]{:S(2)}, u32[]{:S(2)}) collective-permute-start(f32[24,1664]{1,0:T(8,128)S(1)} %add.7.after_ref.chip_ref), channel_id=1, source_target_pairs={{0,30},{1,31},{2,0},{3,1},{4,2},{5,3},{6,4},{7,5},{8,6},{9,7},{10,... | collective-permute-start | bytes 479240 | tf_op jit(solution)/shard_map/ppermute | solution.py:523
  24.3 14.2 %collective-permute-start.1 = (f32[24,1664]{1,0:T(8,128)S(1)}, f32[24,1664]{1,0:T(8,128)S(1)}, u32[]{:S(2)}, u32[]{:S(2)}) collective-permute-start(f32[24,1664]{1,0:T(8,128)S(1)} %add.7.after_ref.chip_ref), channel_id=1, source_target_pairs={{0,2},{1,3},{2,4},{3,5},{4,6},{5,7},{6,8},{7,9},{8,10},{9,11},{10,... | collective-permute-start | bytes 479240 | tf_op jit(solution)/shard_map/ppermute | solution.py:523
  24.3 9.5 %collective-permute-start.4 = (f32[24,640]{1,0:T(8,128)S(1)}, f32[24,640]{1,0:T(8,128)S(1)}, u32[]{:S(2)}, u32[]{:S(2)}) collective-permute-start(f32[24,640]{1,0:T(8,128)S(1)} %slice.9), channel_id=1, source_target_pairs={{0,28},{1,29},{2,30},{3,31},{4,0},{5,1},{6,2},{7,3},{8,4},{9,5},{1... | collective-permute-start | bytes 184328 | tf_op jit(solution)/shard_map/ppermute | solution.py:523
  30.6 7.8 %collective-permute-start.3 = (f32[24,640]{1,0:T(8,128)S(1)}, f32[24,640]{1,0:T(8,128)S(1)}, u32[]{:S(2)}, u32[]{:S(2)}) collective-permute-start(f32[24,640]{1,0:T(8,128)S(1)} %slice.9), channel_id=1, source_target_pairs={{0,4},{1,5},{2,6},{3,7},{4,8},{5,9},{6,10},{7,11},{8,12},{9,13},{1... | collective-permute-start | bytes 184328 | tf_op jit(solution)/shard_map/ppermute | solution.py:523
  38.5 0.9 copy-start.1
  39.4 0.6 copy-start.2
  54.4 0.8 copy-start.4
  54.4 4.9 %collective-permute-start.5 = (f32[96,1664]{1,0:T(8,128)S(1)}, f32[96,1664]{1,0:T(8,128)}, u32[]{:S(2)}, u32[]{:S(2)}) collective-permute-start(f32[96,1664]{1,0:T(8,128)S(1)} %all_gather.3.refs_7_.refs_4_), channel_id=1, source_target_pairs={{0,1},{1,0},{2,3},{3,2},{4,5},{5,4},{6,7},{7,6},{8,9},{9,8},{10,11... | collective-permute-start | bytes 1916936 | tf_op jit(solution)/shard_map/ppermute | solution.py:560
  54.4 14.3 %copy-start.3 = (f32[4,8,15360]{2,1,0:T(8,128)}, f32[4,8,15360]{2,1,0:T(8,128)S(1)}, u32[]{:S(2)}) copy-start(f32[4,8,15360]{2,1,0:T(8,128)S(1)} %all-to-all-done.refs_0_) | copy-start | bytes 5898244
  55.3 25.5 %collective-permute-start.6 = (f32[8,15360]{1,0:T(8,128)}, f32[8,15360]{1,0:T(8,128)S(1)}, u32[]{:S(2)}, u32[]{:S(2)}) collective-permute-start(f32[8,15360]{1,0:T(8,128)} %get-tuple-element.52), channel_id=1, source_target_pairs={{0,32},{32,64},{64,96},{96,0},{1,33},{33,65},{65,97},{97,1},{2,34}... | collective-permute-start | bytes 1474568 | tf_op jit(solution)/shard_map/ppermute | solution.py:523
  55.9 24.8 %collective-permute-start.7 = (f32[8,15360]{1,0:T(8,128)}, f32[8,15360]{1,0:T(8,128)S(1)}, u32[]{:S(2)}, u32[]{:S(2)}) collective-permute-start(f32[8,15360]{1,0:T(8,128)} %get-tuple-element.53), channel_id=1, source_target_pairs={{0,64},{32,96},{64,0},{96,32},{1,65},{33,97},{65,1},{97,33},{2,66}... | collective-permute-start | bytes 1474568 | tf_op jit(solution)/shard_map/ppermute | solution.py:523
  58.6 22.8 %collective-permute-start.8 = (f32[8,15360]{1,0:T(8,128)}, f32[8,15360]{1,0:T(8,128)}, u32[]{:S(2)}, u32[]{:S(2)}) collective-permute-start(f32[8,15360]{1,0:T(8,128)} %get-tuple-element.54), channel_id=1, source_target_pairs={{0,96},{32,0},{64,32},{96,64},{1,97},{33,1},{65,33},{97,65},{2,98}... | collective-permute-start | bytes 1474568 | tf_op jit(solution)/shard_map/ppermute | solution.py:523
  80.8 0.8 copy-start.5
  80.8 0.9 copy-start.6
  81.7 18.2 %all-to-all-start.2 = ((f32[4,8,7680]{2,1,0:T(8,128)}), f32[4,8,7680]{2,1,0:T(8,128)S(1)}, u32[]{:S(2)}, u32[]{:S(2)}) async-start(f32[4,8,7680]{2,1,0:T(8,128)} %after.5), calls=%async_computation.2 | async-start | bytes 1966080 | tf_op jit(solution)/shard_map/all_to_all | solution.py:527
  91.5 11.8 %copy-start.17 = (f32[8,7680]{1,0:T(8,128)S(1)}, f32[8,7680]{1,0:T(8,128)}, u32[]{:S(2)}) copy-start(f32[8,7680]{1,0:T(8,128)} %get-tuple-element.60) | copy-start | bytes 737284
  91.5 13.8 %copy-start.16 = (f32[8,7680]{1,0:T(8,128)S(1)}, f32[8,7680]{1,0:T(8,128)}, u32[]{:S(2)}) copy-start(f32[8,7680]{1,0:T(8,128)} %get-tuple-element.61) | copy-start | bytes 737284
  91.5 16.5 %copy-start.15 = (f32[8,7680]{1,0:T(8,128)S(1)}, f32[8,7680]{1,0:T(8,128)}, u32[]{:S(2)}) copy-start(f32[8,7680]{1,0:T(8,128)} %get-tuple-element.62) | copy-start | bytes 737284
  99.9 29.3 %copy-start.7 = (f32[4,8,7680]{2,1,0:T(8,128)}, f32[4,8,7680]{2,1,0:T(8,128)S(1)}, u32[]{:S(2)}) copy-start(f32[4,8,7680]{2,1,0:T(8,128)S(1)} %all-to-all-done.2.refs_0_) | copy-start | bytes 2949124
  99.9 35.5 %all-to-all-start.1 = ((f32[4,8,7680]{2,1,0:T(8,128)}), f32[4,8,7680]{2,1,0:T(8,128)S(1)}, u32[]{:S(2)}, u32[]{:S(2)}) async-start(f32[4,8,7680]{2,1,0:T(8,128)} %after.4), calls=%async_computation.1 | async-start | bytes 1966080 | tf_op jit(solution)/shard_map/all_to_all | solution.py:527
  103.4 25.8 %collective-permute-start.12 = (f32[8,7680]{1,0:T(8,128)S(1)}, f32[8,7680]{1,0:T(8,128)S(1)}, u32[]{:S(2)}, u32[]{:S(2)}) collective-permute-start(f32[8,7680]{1,0:T(8,128)S(1)} %copy-done.17), channel_id=1, source_target_pairs={{0,32},{32,64},{64,96},{96,0},{1,33},{33,65},{65,97},{97,1},{2,34}... | collective-permute-start | bytes 737288 | tf_op jit(solution)/shard_map/ppermute | solution.py:523
  105.4 26.2 %collective-permute-start.13 = (f32[8,7680]{1,0:T(8,128)S(1)}, f32[8,7680]{1,0:T(8,128)S(1)}, u32[]{:S(2)}, u32[]{:S(2)}) collective-permute-start(f32[8,7680]{1,0:T(8,128)S(1)} %copy-done.16), channel_id=1, source_target_pairs={{0,64},{32,96},{64,0},{96,32},{1,65},{33,97},{65,1},{97,33},{2,66}... | collective-permute-start | bytes 737288 | tf_op jit(solution)/shard_map/ppermute | solution.py:523
  108.1 23.5 %collective-permute-start.14 = (f32[8,7680]{1,0:T(8,128)S(1)}, f32[8,7680]{1,0:T(8,128)S(1)}, u32[]{:S(2)}, u32[]{:S(2)}) collective-permute-start(f32[8,7680]{1,0:T(8,128)S(1)} %copy-done.15), channel_id=1, source_target_pairs={{0,96},{32,0},{64,32},{96,64},{1,97},{33,1},{65,33},{97,65},{2,98}... | collective-permute-start | bytes 737288 | tf_op jit(solution)/shard_map/ppermute | solution.py:523
  109.5 29.1 %collective-permute-start.9 = (f32[8,7680]{1,0:T(8,128)}, f32[8,7680]{1,0:T(8,128)S(1)}, u32[]{:S(2)}, u32[]{:S(2)}) collective-permute-start(f32[8,7680]{1,0:T(8,128)} %get-tuple-element.57), channel_id=1, source_target_pairs={{0,32},{32,64},{64,96},{96,0},{1,33},{33,65},{65,97},{97,1},{2,34}... | collective-permute-start | bytes 737288 | tf_op jit(solution)/shard_map/ppermute | solution.py:523
  110.1 28.5 %collective-permute-start.10 = (f32[8,7680]{1,0:T(8,128)}, f32[8,7680]{1,0:T(8,128)S(1)}, u32[]{:S(2)}, u32[]{:S(2)}) collective-permute-start(f32[8,7680]{1,0:T(8,128)} %get-tuple-element.58), channel_id=1, source_target_pairs={{0,64},{32,96},{64,0},{96,32},{1,65},{33,97},{65,1},{97,33},{2,66}... | collective-permute-start | bytes 737288 | tf_op jit(solution)/shard_map/ppermute | solution.py:523
  129.2 2.4 %copy-start.12 = (f32[8,7680]{1,0:T(8,128)}, f32[8,7680]{1,0:T(8,128)S(1)}, u32[]{:S(2)}) copy-start(f32[8,7680]{1,0:T(8,128)S(1)} %collective-permute-done.12.refs_1_) | copy-start | bytes 737284
  129.2 9.5 %collective-permute-start.11 = (f32[8,7680]{1,0:T(8,128)}, f32[8,7680]{1,0:T(8,128)S(1)}, u32[]{:S(2)}, u32[]{:S(2)}) collective-permute-start(f32[8,7680]{1,0:T(8,128)} %get-tuple-element.59), channel_id=1, source_target_pairs={{0,96},{32,0},{64,32},{96,64},{1,97},{33,1},{65,33},{97,65},{2,98}... | collective-permute-start | bytes 737288 | tf_op jit(solution)/shard_map/ppermute | solution.py:523
  131.5 0.7 copy-start.13
  132.2 0.7 copy-start.14
  135.3 1.0 copy-start.8
  138.6 0.7 copy-start.9
  138.6 0.8 copy-start.10
  139.4 0.7 copy-start.11

commit v4 on v3

--- a/solution.py
+++ b/solution.py
@@ -15,10 +15,10 @@
 ROWS = MEMBERS // GROUPS
 PADDED = 24
 CELLS = 12288
-CHUNKS = 4
-EARLY = (0, 1)
-LATE = (2, 3)
-PERMUTED = (1, 3)
+CHUNKS = 6
+EARLY = (0, 1, 2, 3)
+LATE = (4, 5)
+EXITS = ((0, 1), (2, 3), (4, 5))
 CHUNK = CELLS // CHUNKS
 HALF = CHUNK // 2
 PACKED = 5 * HALF
@@ -409,7 +409,7 @@
     outs = [out_ref.at[q] for q in range(GROUPS)]
     low = lax.broadcasted_iota(jnp.int32, (8, HALF), 0) < 4
     offsets = lax.broadcasted_iota(jnp.int32, (1, HALF), 1)
-    first = here_ref[0] * CELLS + chunk * CHUNK
+    first = here_ref[0] * CELLS + (chunk + pl.program_id(0)) * CHUNK
 
     def join(a, b):
         return jnp.where(low, a, pltpu.roll(b, 4, 0)), jnp.where(low, pltpu.roll(a, 4, 0), b)
@@ -467,18 +467,26 @@
     return pl.BlockSpec(shape, lambda i: index, pipeline_mode=pl.Buffered(1))
 
 
-def update(chunk, late, apart, index, here, terms, arrived, firsts):
+def update(chunks, late, apart, index, here, terms, arrived, firsts):
     gathered = (GROUPS, 8, PACKED)
     shapes = [gathered[1:]] * GROUPS if apart else [gathered]
-    return pl.pallas_call(
-        functools.partial(update_kernel, chunk, late, apart),
-        grid=(1,),
-        out_shape=[jax.ShapeDtypeStruct(shape, f32) for shape in shapes],
+    n = len(chunks)
+
+    def wide(shape):
+        return jax.ShapeDtypeStruct(shape[:-1] + (PACKED * n,), f32)
+
+    def blocks(shape, at):
+        return pl.BlockSpec(shape, lambda i: (0,) * (len(shape) - 1) + (at + i,))
+
+    return pl.pallas_call(
+        functools.partial(update_kernel, chunks[0], late, apart),
+        grid=(n,),
+        out_shape=[wide(shape) for shape in shapes],
         in_specs=smem(2)
         + [fixed(a.shape, (0, 0, 0)) for a in terms[1:]]
-        + ([fixed((8, PACKED), (0, index))] * GROUPS if late else [fixed(gathered, (0, 0, index))])
+        + ([blocks(gathered[1:], index)] * GROUPS if late else [blocks(gathered, index)])
         + [pl.BlockSpec(memory_space=pl.ANY)] * len(firsts),
-        out_specs=[fixed(shape, (0,) * len(shape)) for shape in shapes],
+        out_specs=[blocks(shape, 0) for shape in shapes],
         scratch_shapes=[pltpu.VMEM((2, MEMBERS, HALF), f32)] + [pltpu.VMEM(gathered, f32)] * 2,
         compiler_params=params(60),
         cost_estimate=cost(8),
@@ -496,7 +504,7 @@
         rows[i, 8:16, :] = src[:, CHUNK : 2 * CHUNK]
         rows[i, 16:20, 0:HALF] = src[0:4, 2 * CHUNK : PACKED]
         rows[i, 16:20, HALF:CHUNK] = src[4:8, 2 * CHUNK : PACKED]
-        at = pl.multiple_of(quarter * CELLS + chunk * CHUNK, 128)
+        at = pl.multiple_of(quarter * CELLS + (chunk + pl.program_id(0)) * CHUNK, 128)
         copy = pltpu.make_async_copy(rows.at[i], out_ref.at[:, pl.ds(at, CHUNK)], sems.at[i])
         copy.start()
         copies.append(copy)
@@ -504,12 +512,15 @@
         copy.wait()
 
 
-def unpack(chunk, apart, rank, pieces, out):
+def unpack(chunks, apart, rank, pieces, out):
     held = [] if out is None else [out]
-    return pl.pallas_call(
-        functools.partial(unpack_kernel, chunk, apart),
+    shape = (8, PACKED) if apart else (GROUPS, 8, PACKED)
+    block = pl.BlockSpec(shape, lambda i: (0,) * (len(shape) - 1) + (i,))
+    return pl.pallas_call(
+        functools.partial(unpack_kernel, chunks[0], apart),
+        grid=(len(chunks),),
         out_shape=jax.ShapeDtypeStruct((ROWS, GROUPS * CELLS), f32),
-        in_specs=smem(1) + whole(len(pieces)) + [pl.BlockSpec(memory_space=pl.ANY)] * len(held),
+        in_specs=smem(1) + [block] * len(pieces) + [pl.BlockSpec(memory_space=pl.ANY)] * len(held),
         out_specs=pl.BlockSpec(memory_space=pl.ANY),
         scratch_shapes=[pltpu.VMEM((GROUPS, ROWS, CHUNK), f32), pltpu.SemaphoreType.DMA((GROUPS,))],
         input_output_aliases={1 + len(pieces): 0} if held else {},
@@ -566,20 +577,22 @@
     terms = (count, lhs, driver, centre, inverse)
 
     made, firsts = [], []
-    for c in range(CHUNKS):
-        held = c in LATE
-        at = LATE.index(c) if held else EARLY.index(c)
-        made.append(update(c, held, c in PERMUTED, at, here, terms, late if held else entered, firsts))
-        firsts = [made[c][0]]
-    made[0] = after(made[0], *late[1:], made[1][0])
-    made[2] = after(made[2], made[3][0])
+    for e, chunks in enumerate(EXITS):
+        held = chunks[0] in LATE
+        group = LATE if held else EARLY
+        at = group.index(chunks[0])
+        new = update(chunks, held, e > 0, at, here, terms, late if held else entered, firsts)
+        if e == 0:
+            new = after(new, *late[1:])
+        made.append(new)
+        firsts = [new[0]]
     out = None
-    for c, new in enumerate(made):
-        if c in PERMUTED:
+    for e, (chunks, new) in enumerate(zip(EXITS, made)):
+        if e == 0:
+            back = [exchanged(new[0])]
+        else:
             back = [new[0]] + [shifted(new[d], "member", GROUPS, d) for d in range(1, GROUPS)]
-        else:
-            back = [exchanged(new[0])]
-        out = unpack(c, c in PERMUTED, rank, back, out)
+        out = unpack(chunks, e > 0, rank, back, out)
     return out
 
 

time: 144 us -> 132 us (0.917); the launches traced: 143 us -> 133 us
  waiting for transfers between devices: 27.1 us -> 18.8 us
  Pallas kernels: 59.8 us -> 51.9 us
  starting transfers between devices: 33.5 us -> 40 us
    ppermute x13, starting transfers between devices: 21.9 us -> 30.3 us  [shifted(): return lax.ppermute(x, axis, [(i, (i + by) % size) for i in range(size)])]
    ppermute x13, waiting for transfers between devices: 23.4 us -> 17.6 us  [shifted(): return lax.ppermute(x, axis, [(i, (i + by) % size) for i in range(size)])]
    pallas_call x8 -> x6, Pallas kernels: 33.7 us -> 29.7 us  [the longest x3 20.9 us: update(): pl.pallas_call(functools.partial(update_kernel, chunks[0], late, apart),...]
    pallas_call x1, Pallas kernels: 7.39 us -> 3.9 us  [pick(): pl.pallas_call(pick_kernel, out_shape=[jax.ShapeDtypeStruct((PADDED, PART...]
    all_to_all x3 -> x2, starting transfers between devices: 11.6 us -> 9 us  [exchanged(): return lax.all_to_all(x, 'member', split_axis=0, concat_axis=0, tiled=True)]
    all_to_all x3 -> x2, waiting for transfers between devices: 2.13 us -> 0.01 us  [exchanged(): return lax.all_to_all(x, 'member', split_axis=0, concat_axis=0, tiled=True)]
    unnamed x36 -> x26, local copies, waits for them, and re-layouts: 5.84 us -> 5.79 us
  transfers between devices with their start and end apart: 18 -> 17, of which waited for: 5 -> 6; matrix products, arithmetic and copies ran while one was open for 1% -> 1% of each run, Pallas kernels for 36% -> 32%
where the time goes in v4:
time: 132 us; the launch traced here: 133 us
  Pallas kernels  51.9 us (39%)
  starting transfers between devices  40 us (30%)
  waiting for transfers between devices  18.8 us (14%)
  blocking collectives  14.2 us (11%)
  local copies, waits for them, and re-layouts  6.45 us (5%)
    ppermute x13, starting transfers between devices, shifted(): return lax.ppermute(x, axis, [(i, (i + by) % size) for i in range(size)])  30.3 us
    pallas_call x3, Pallas kernels, update(): pl.pallas_call(functools.partial(update_kernel, chunks[0], late, apart),...  20.9 us
    ppermute x13, waiting for transfers between devices, shifted(): return lax.ppermute(x, axis, [(i, (i + by) % size) for i in range(size)])  17.6 us
    all_gather x1, blocking collectives, per_device(): mine = lax.all_gather(summed, 'member', axis=0, tiled=True)  14.2 us
    pallas_call x1, Pallas kernels, drivers(): pl.pallas_call(drivers_kernel, out_shape=[jax.ShapeDtypeStruct((BLOCKS, O...  9.17 us
    all_to_all x2, starting transfers between devices, exchanged(): return lax.all_to_all(x, 'member', split_axis=0, concat_axis=0, tiled=True)  9 us
    pallas_call x3, Pallas kernels, unpack(): pl.pallas_call(functools.partial(unpack_kernel, chunks[0], apart), grid=(...  8.81 us
    pallas_call x1, Pallas kernels, pack(): pl.pallas_call(pack_kernel, grid_spec=pltpu.PrefetchScalarGridSpec(num_sc...  6.01 us
  transfers between devices with their start and end apart: 17, of which 6 were waited for; matrix products, arithmetic and copies ran while one was open for 1% of the time, Pallas kernels for 32%

profile of v4, /device:TPU:0, one launch (start us, length us, event | category | flops | bytes accessed | tf_op | source)
XLA Modules:
  0.0 132.7 jit_solution(12230986010983144094)
XLA Ops:
  0.0 6.0 %pack.1 = (f32[4,8,20480]{2,1,0:T(8,128)}, f32[8,10240]{1,0:T(8,128)}, f32[8,10240]{1,0:T(8,128)}, f32[8,10240]{1,0:T(8,128)}, f32[8,10240]{1,0:T(8,128)}, /*index=5*/s32[8,256]{1,0:T(8,128)}) custom-call(s32[1]{0:T(128)} %bitcast.rank_ref, s32[1]{0:T(128)} %bitcast.1.slab_ref, s32[4]{0:T(128)} %order_ref.7, s32[4,256]{1,0:T(4,128)} %owner_ref.5, ...), custom_call_target="tpu_custom_call" | custom-call | bytes 3072 | tf_op jit(solution)/shard_map/pack/pallas_call | solution.py:104
  6.0 4.4 %all-to-all-start = ((f32[4,8,20480]{2,1,0:T(8,128)}), f32[4,8,20480]{2,1,0:T(8,128)S(1)}, u32[]{:S(2)}, u32[]{:S(2)}) async-start(f32[4,8,20480]{2,1,0:T(8,128)} %get-tuple-element.35.after_ref), calls=%async_computation | async-start | bytes 5242880 | tf_op jit(solution)/shard_map/all_to_all | solution.py:538
  10.4 3.9 %pick.1 = (f32[24,1664]{1,0:T(8,128)}, f32[24,1664]{1,0:T(8,128)}) custom-call(s32[1]{0:T(128)} %bitcast.1.slab_ref, s32[4]{0:T(128)} %order_ref.7, s32[4,256]{1,0:T(4,128)} %owner_ref.5, s32[4,4,256]{2,1,0:T(4,128)} %bitcast.8, s32[8,256]{1,0:T(8,128)} %get-tuple-element.34.held, f32[4,4,256]{2,1,0:T(4,128)} %bitcast.6, f32[20,49152]{1,0:T(8,128)} %ens_ref.3, ...), custom_call_target="tpu_custom_call" | custom-call | bytes 8192 | tf_op jit(solution)/shard_map/pick/pallas_call | solution.py:201
  14.3 0.7 collective-permute-start
  15.0 1.2 collective-permute-done
  16.2 0.9 add.7.after_ref.chip_ref
  17.2 0.0 copy-start
  17.2 6.7 %collective-permute-start.2 = (f32[24,1664]{1,0:T(8,128)S(1)}, f32[24,1664]{1,0:T(8,128)S(1)}, u32[]{:S(2)}, u32[]{:S(2)}) collective-permute-start(f32[24,1664]{1,0:T(8,128)S(1)} %add.7.after_ref.chip_ref), channel_id=1, source_target_pairs={{0,30},{1,31},{2,0},{3,1},{4,2},{5,3},{6,4},{7,5},{8,6},{9,7},{10,... | collective-permute-start | bytes 479240 | tf_op jit(solution)/shard_map/ppermute | solution.py:534
  23.8 0.0 collective-permute-start.1
  23.8 8.8 %collective-permute-start.4 = (f32[24,640]{1,0:T(8,128)S(1)}, f32[24,640]{1,0:T(8,128)S(1)}, u32[]{:S(2)}, u32[]{:S(2)}) collective-permute-start(f32[24,640]{1,0:T(8,128)S(1)} %slice.9), channel_id=1, source_target_pairs={{0,28},{1,29},{2,30},{3,31},{4,0},{5,1},{6,2},{7,3},{8,4},{9,5},{1... | collective-permute-start | bytes 184328 | tf_op jit(solution)/shard_map/ppermute | solution.py:534
  32.6 0.0 collective-permute-start.3
  32.6 0.0 copy-done
  32.6 3.1 %reach.1 = (s32[4]{0:T(128)}, s32[4,1,256]{2,1,0:T(1,128)}, bf16[4,256,256]{2,1,0:T(8,128)(2,1)}, f32[4,256,128]{2,1,0:T(8,128)}, f32[4,256,128]{2,1,0:T(8,128)}...) custom-call(s32[1]{0:T(128)S(6)} %add.6.here_ref, s32[4]{0:T(128)} %order_ref.7, s32[4,256]{1,0:T(4,128)} %owner_ref.5, ...), custom_call_target="tpu_custom_call" | custom-call | bytes 2048 | tf_op jit(solution)/shard_map/reach/pallas_call | solution.py:269
  35.7 0.0 collective-permute-done.4.refs_3_
  35.7 4.7 %collective-permute-done.3.refs_2_ = f32[24,640]{1,0:T(8,128)S(1)} collective-permute-done((f32[24,640]{1,0:T(8,128)S(1)}, f32[24,640]{1,0:T(8,128)S(1)}, u32[]{:S(2)}, u32[]{:S(2)}) %collective-permute-start.3) | collective-permute-done | bytes 61472 | tf_op jit(solution)/shard_map/ppermute | solution.py:534
  40.4 0.0 collective-permute-done.2.refs_1_
  40.4 0.0 collective-permute-done.1.refs_0_
  40.4 0.9 copy-done.1
  41.4 0.0 copy-start.2
  41.4 0.7 copy-done.2
  42.1 14.2 %all_gather.3.refs_7_.refs_4_ = f32[96,1664]{1,0:T(8,128)S(1)} all-gather(f32[24,1664]{1,0:T(8,128)S(1)} %window.1), channel_id=1, replica_groups=mesh['member'=4,'slab'=32] {'member'}, dimensions={0}, use_global_device_ids=true | all-gather | bytes 798720 | tf_op jit(solution)/shard_map/all_gather | solution.py:570
  56.3 0.0 copy-start.4
  56.3 0.0 collective-permute-start.5
  56.3 0.0 all-to-all-done.refs_0_
  56.3 0.0 copy-start.3
  56.3 0.7 slice_bitcast_fusion.refs_5_
  56.9 0.2 copy-done.4
  57.1 0.6 collective-permute-start.6
  57.7 2.7 %collective-permute-start.7 = (f32[8,10240]{1,0:T(8,128)}, f32[8,10240]{1,0:T(8,128)}, u32[]{:S(2)}, u32[]{:S(2)}) collective-permute-start(f32[8,10240]{1,0:T(8,128)} %get-tuple-element.53), channel_id=1, source_target_pairs={{0,64},{32,96},{64,0},{96,32},{1,65},{33,97},{65,1},{97,33},{2,66}... | collective-permute-start | bytes 983048 | tf_op jit(solution)/shard_map/ppermute | solution.py:534
  60.3 0.9 collective-permute-start.8
  61.2 0.0 collective-permute-done.5.refs_8_
  61.2 9.2 %drivers.1 = (bf16[4,256,240]{2,1,0:T(8,128)(2,1)}, bf16[4,160,256]{2,1,0:T(8,128)(2,1)}) custom-call(s32[1]{0:T(128)S(6)} %add.6.here_ref, s32[4]{0:T(128)} %order_ref.7, s32[4]{0:T(128)} %get-tuple-element.38.refs_4_.count_ref, f32[4,4,256]{2,1,0:T(4,128)} %bitcast.7, f32[4,256]{1,0:T(4,128)} %refs_1_.1, f32[4,256]{1,0:T(4,128)} %refs_2_.1, ...), custom_call_target="tpu_custom_call" | custom-call | bytes 8192 | tf_op jit(solution)/shard_map/drivers/pallas_call | solution.py:378
  70.4 0.0 copy-done.3
  70.4 6.8 %update.3.refs_0_ = f32[4,8,10240]{2,1,0:T(8,128)} custom-call(s32[1]{0:T(128)S(6)} %add.6.here_ref, s32[4]{0:T(128)} %get-tuple-element.38.refs_4_.count_ref, bf16[4,256,240]{2,1,0:T(8,128)(2,1)} %get-tuple-element.43.lhs_ref, bf16[4,160,256]{2,1,0:T(8,128)(2,1)} %get-tuple-element.44.driver_ref, f32[4,256,128]{2,1,0:T(8,128)} %get-tuple-element.45.centre_ref, ...), custom_call_target="tpu_custom_call" | custom-call | bytes 8192 | tf_op jit(solution)/shard_map/update/pallas_call | solution.py:481
  77.2 0.0 collective-permute-done.6.refs_1_
  77.2 0.0 collective-permute-done.7.refs_2_
  77.2 0.0 collective-permute-done.8.refs_3_
  77.2 0.7 copy-done.6
  77.9 4.6 %all-to-all-start.1 = ((f32[4,8,10240]{2,1,0:T(8,128)}), f32[4,8,10240]{2,1,0:T(8,128)S(1)}, u32[]{:S(2)}, u32[]{:S(2)}) async-start(f32[4,8,10240]{2,1,0:T(8,128)} %after.3.refs_1_), calls=%async_computation.1 | async-start | bytes 2621440 | tf_op jit(solution)/shard_map/all_to_all | solution.py:538
  82.6 6.9 %update.4 = (f32[8,10240]{1,0:T(8,128)}, f32[8,10240]{1,0:T(8,128)}, f32[8,10240]{1,0:T(8,128)}, f32[8,10240]{1,0:T(8,128)}) custom-call(s32[1]{0:T(128)S(6)} %add.6.here_ref, s32[4]{0:T(128)} %get-tuple-element.38.refs_4_.count_ref, bf16[4,256,240]{2,1,0:T(8,128)(2,1)} %get-tuple-element.43.lhs_ref, bf16[4,160,256]{2,1,0:T(8,128)(2,1)} %get-tuple-element.44.driver_ref, ...), custom_call_target="tpu_custom_call" | custom-call | bytes 8192 | tf_op jit(solution)/shard_map/update/pallas_call | solution.py:481
  89.4 3.3 %collective-permute-start.12 = (f32[8,10240]{1,0:T(8,128)}, f32[8,10240]{1,0:T(8,128)S(1)}, u32[]{:S(2)}, u32[]{:S(2)}) collective-permute-start(f32[8,10240]{1,0:T(8,128)} %get-tuple-element.60), channel_id=1, source_target_pairs={{0,32},{32,64},{64,96},{96,0},{1,33},{33,65},{65,97},{97,1},{2,34}... | collective-permute-start | bytes 983048 | tf_op jit(solution)/shard_map/ppermute | solution.py:534
  92.8 2.7 %collective-permute-start.13 = (f32[8,10240]{1,0:T(8,128)}, f32[8,10240]{1,0:T(8,128)S(1)}, u32[]{:S(2)}, u32[]{:S(2)}) collective-permute-start(f32[8,10240]{1,0:T(8,128)} %get-tuple-element.61), channel_id=1, source_target_pairs={{0,64},{32,96},{64,0},{96,32},{1,65},{33,97},{65,1},{97,33},{2,66}... | collective-permute-start | bytes 983048 | tf_op jit(solution)/shard_map/ppermute | solution.py:534
  95.4 1.5 %collective-permute-start.14 = (f32[8,10240]{1,0:T(8,128)}, f32[8,10240]{1,0:T(8,128)S(1)}, u32[]{:S(2)}, u32[]{:S(2)}) collective-permute-start(f32[8,10240]{1,0:T(8,128)} %get-tuple-element.62), channel_id=1, source_target_pairs={{0,96},{32,0},{64,32},{96,64},{1,97},{33,1},{65,33},{97,65},{2,98}... | collective-permute-start | bytes 983048 | tf_op jit(solution)/shard_map/ppermute | solution.py:534
  96.9 7.2 %update.5 = (f32[8,10240]{1,0:T(8,128)}, f32[8,10240]{1,0:T(8,128)}, f32[8,10240]{1,0:T(8,128)}, f32[8,10240]{1,0:T(8,128)}) custom-call(s32[1]{0:T(128)S(6)} %add.6.here_ref, s32[4]{0:T(128)} %get-tuple-element.38.refs_4_.count_ref, bf16[4,256,240]{2,1,0:T(8,128)(2,1)} %get-tuple-element.43.lhs_ref, bf16[4,160,256]{2,1,0:T(8,128)(2,1)} %get-tuple-element.44.driver_ref, ...), custom_call_target="tpu_custom_call" | custom-call | bytes 8192 | tf_op jit(solution)/shard_map/update/pallas_call | solution.py:481
  104.1 1.9 %collective-permute-start.9 = (f32[8,10240]{1,0:T(8,128)}, f32[8,10240]{1,0:T(8,128)S(1)}, u32[]{:S(2)}, u32[]{:S(2)}) collective-permute-start(f32[8,10240]{1,0:T(8,128)} %get-tuple-element.57), channel_id=1, source_target_pairs={{0,32},{32,64},{64,96},{96,0},{1,33},{33,65},{65,97},{97,1},{2,34}... | collective-permute-start | bytes 983048 | tf_op jit(solution)/shard_map/ppermute | solution.py:534
  106.0 0.9 collective-permute-start.10
  106.9 2.1 %collective-permute-done.12.refs_1_ = f32[8,10240]{1,0:T(8,128)S(1)} collective-permute-done((f32[8,10240]{1,0:T(8,128)}, f32[8,10240]{1,0:T(8,128)S(1)}, u32[]{:S(2)}, u32[]{:S(2)}) %collective-permute-start.12) | collective-permute-done | bytes 327712 | tf_op jit(solution)/shard_map/ppermute | solution.py:534
  109.1 0.5 collective-permute-start.11
  109.6 0.0 all-to-all-done.1.refs_0_
  109.6 1.1 copy-done.5
  110.6 2.9 %unpack.3.refs_4_ = f32[20,49152]{1,0:T(8,128)} custom-call(s32[1]{0:T(128)} %bitcast.rank_ref, f32[4,8,10240]{2,1,0:T(8,128)} %copy-done.5), custom_call_target="tpu_custom_call" | custom-call | bytes 2048 | tf_op jit(solution)/shard_map/unpack/pallas_call | solution.py:519
  113.5 2.5 %collective-permute-done.13.refs_2_ = f32[8,10240]{1,0:T(8,128)S(1)} collective-permute-done((f32[8,10240]{1,0:T(8,128)}, f32[8,10240]{1,0:T(8,128)S(1)}, u32[]{:S(2)}, u32[]{:S(2)}) %collective-permute-start.13) | collective-permute-done | bytes 327712 | tf_op jit(solution)/shard_map/ppermute | solution.py:534
  116.1 0.0 collective-permute-done.14.refs_3_
  116.1 0.0 copy-done.7
  116.1 0.7 copy-done.8
  116.8 0.7 copy-done.9
  117.5 3.0 %unpack.4.refs_4_ = f32[20,49152]{1,0:T(8,128)} custom-call(s32[1]{0:T(128)} %bitcast.rank_ref, f32[8,10240]{1,0:T(8,128)} %get-tuple-element.55.refs_4_.refs_0_, f32[8,10240]{1,0:T(8,128)} %copy-done.7, f32[8,10240]{1,0:T(8,128)} %copy-done.8, f32[8,10240]{1,0:T(8,128)} %copy-done.9, f32[20,49152]{1,0:T(8,128)} %unpack.3.refs_4_), custom_call_target="tpu_custom_call", output_to_operand_aliasing={{}: (5, {})} | custom-call | bytes 2048 | tf_op jit(solution)/shard_map/unpack/pallas_call | solution.py:519
  120.5 2.1 %collective-permute-done.9.refs_1_ = f32[8,10240]{1,0:T(8,128)S(1)} collective-permute-done((f32[8,10240]{1,0:T(8,128)}, f32[8,10240]{1,0:T(8,128)S(1)}, u32[]{:S(2)}, u32[]{:S(2)}) %collective-permute-start.9) | collective-permute-done | bytes 327712 | tf_op jit(solution)/shard_map/ppermute | solution.py:534
  122.6 6.1 %collective-permute-done.10.refs_2_ = f32[8,10240]{1,0:T(8,128)S(1)} collective-permute-done((f32[8,10240]{1,0:T(8,128)}, f32[8,10240]{1,0:T(8,128)S(1)}, u32[]{:S(2)}, u32[]{:S(2)}) %collective-permute-start.10) | collective-permute-done | bytes 327712 | tf_op jit(solution)/shard_map/ppermute | solution.py:534
  128.7 0.0 collective-permute-done.11.refs_3_
  128.7 0.0 copy-done.10
  128.7 0.7 copy-done.11
  129.4 0.1 copy-done.12
  129.5 3.0 %unpack.5 = f32[20,49152]{1,0:T(8,128)} custom-call(s32[1]{0:T(128)} %bitcast.rank_ref, f32[8,10240]{1,0:T(8,128)} %get-tuple-element.56.refs_0_, f32[8,10240]{1,0:T(8,128)} %copy-done.10, f32[8,10240]{1,0:T(8,128)} %copy-done.11, f32[8,10240]{1,0:T(8,128)} %copy-done.12, f32[20,49152]{1,0:T(8,128)} %unpack.4.refs_4_), custom_call_target="tpu_custom_call", output_to_operand_aliasing={{}: (5, {})} | custom-call | bytes 2048 | tf_op jit(solution)/shard_map/unpack/pallas_call | solution.py:519
  (13 shorter events, 0.1 us)
Async XLA Ops:
  6.0 50.3 %all-to-all-start = ((f32[4,8,20480]{2,1,0:T(8,128)}), f32[4,8,20480]{2,1,0:T(8,128)S(1)}, u32[]{:S(2)}, u32[]{:S(2)}) async-start(f32[4,8,20480]{2,1,0:T(8,128)} %get-tuple-element.35.after_ref), calls=%async_computation | async-start | bytes 5242880 | tf_op jit(solution)/shard_map/all_to_all | solution.py:538
  14.3 1.9 %collective-permute-start = (f32[24,1664]{1,0:T(8,128)}, f32[24,1664]{1,0:T(8,128)S(1)}, u32[]{:S(2)}, u32[]{:S(2)}) collective-permute-start(f32[24,1664]{1,0:T(8,128)} %get-tuple-element.37), channel_id=1, source_target_pairs={{0,1},{1,0},{2,3},{3,2},{4,5},{5,4},{6,7},{7,6},{8,9},{9,8},{10,11... | collective-permute-start | bytes 479240 | tf_op jit(solution)/shard_map/ppermute | solution.py:563
  17.2 15.5 %copy-start = (f32[24,1664]{1,0:T(8,128)}, f32[24,1664]{1,0:T(8,128)S(1)}, u32[]{:S(2)}) copy-start(f32[24,1664]{1,0:T(8,128)S(1)} %add.7.after_ref.chip_ref) | copy-start | bytes 479236
  17.2 23.3 %collective-permute-start.2 = (f32[24,1664]{1,0:T(8,128)S(1)}, f32[24,1664]{1,0:T(8,128)S(1)}, u32[]{:S(2)}, u32[]{:S(2)}) collective-permute-start(f32[24,1664]{1,0:T(8,128)S(1)} %add.7.after_ref.chip_ref), channel_id=1, source_target_pairs={{0,30},{1,31},{2,0},{3,1},{4,2},{5,3},{6,4},{7,5},{8,6},{9,7},{10,... | collective-permute-start | bytes 479240 | tf_op jit(solution)/shard_map/ppermute | solution.py:534
  23.8 16.6 %collective-permute-start.1 = (f32[24,1664]{1,0:T(8,128)S(1)}, f32[24,1664]{1,0:T(8,128)S(1)}, u32[]{:S(2)}, u32[]{:S(2)}) collective-permute-start(f32[24,1664]{1,0:T(8,128)S(1)} %add.7.after_ref.chip_ref), channel_id=1, source_target_pairs={{0,2},{1,3},{2,4},{3,5},{4,6},{5,7},{6,8},{7,9},{8,10},{9,11},{10,... | collective-permute-start | bytes 479240 | tf_op jit(solution)/shard_map/ppermute | solution.py:534
  23.8 11.9 %collective-permute-start.4 = (f32[24,640]{1,0:T(8,128)S(1)}, f32[24,640]{1,0:T(8,128)S(1)}, u32[]{:S(2)}, u32[]{:S(2)}) collective-permute-start(f32[24,640]{1,0:T(8,128)S(1)} %slice.9), channel_id=1, source_target_pairs={{0,28},{1,29},{2,30},{3,31},{4,0},{5,1},{6,2},{7,3},{8,4},{9,5},{1... | collective-permute-start | bytes 184328 | tf_op jit(solution)/shard_map/ppermute | solution.py:534
  32.6 7.8 %collective-permute-start.3 = (f32[24,640]{1,0:T(8,128)S(1)}, f32[24,640]{1,0:T(8,128)S(1)}, u32[]{:S(2)}, u32[]{:S(2)}) collective-permute-start(f32[24,640]{1,0:T(8,128)S(1)} %slice.9), channel_id=1, source_target_pairs={{0,4},{1,5},{2,6},{3,7},{4,8},{5,9},{6,10},{7,11},{8,12},{9,13},{1... | collective-permute-start | bytes 184328 | tf_op jit(solution)/shard_map/ppermute | solution.py:534
  40.4 0.9 copy-start.1
  41.4 0.7 copy-start.2
  56.3 0.8 copy-start.4
  56.3 4.9 %collective-permute-start.5 = (f32[96,1664]{1,0:T(8,128)S(1)}, f32[96,1664]{1,0:T(8,128)}, u32[]{:S(2)}, u32[]{:S(2)}) collective-permute-start(f32[96,1664]{1,0:T(8,128)S(1)} %all_gather.3.refs_7_.refs_4_), channel_id=1, source_target_pairs={{0,1},{1,0},{2,3},{3,2},{4,5},{5,4},{6,7},{7,6},{8,9},{9,8},{10,11... | collective-permute-start | bytes 1916936 | tf_op jit(solution)/shard_map/ppermute | solution.py:571
  56.3 14.1 %copy-start.3 = (f32[4,8,20480]{2,1,0:T(8,128)}, f32[4,8,20480]{2,1,0:T(8,128)S(1)}, u32[]{:S(2)}) copy-start(f32[4,8,20480]{2,1,0:T(8,128)S(1)} %all-to-all-done.refs_0_) | copy-start | bytes 7864324
  57.1 20.1 %collective-permute-start.6 = (f32[8,10240]{1,0:T(8,128)}, f32[8,10240]{1,0:T(8,128)S(1)}, u32[]{:S(2)}, u32[]{:S(2)}) collective-permute-start(f32[8,10240]{1,0:T(8,128)} %get-tuple-element.52), channel_id=1, source_target_pairs={{0,32},{32,64},{64,96},{96,0},{1,33},{33,65},{65,97},{97,1},{2,34}... | collective-permute-start | bytes 983048 | tf_op jit(solution)/shard_map/ppermute | solution.py:534
  57.7 19.5 %collective-permute-start.7 = (f32[8,10240]{1,0:T(8,128)}, f32[8,10240]{1,0:T(8,128)}, u32[]{:S(2)}, u32[]{:S(2)}) collective-permute-start(f32[8,10240]{1,0:T(8,128)} %get-tuple-element.53), channel_id=1, source_target_pairs={{0,64},{32,96},{64,0},{96,32},{1,65},{33,97},{65,1},{97,33},{2,66}... | collective-permute-start | bytes 983048 | tf_op jit(solution)/shard_map/ppermute | solution.py:534
  60.3 16.9 %collective-permute-start.8 = (f32[8,10240]{1,0:T(8,128)}, f32[8,10240]{1,0:T(8,128)}, u32[]{:S(2)}, u32[]{:S(2)}) collective-permute-start(f32[8,10240]{1,0:T(8,128)} %get-tuple-element.54), channel_id=1, source_target_pairs={{0,96},{32,0},{64,32},{96,64},{1,97},{33,1},{65,33},{97,65},{2,98}... | collective-permute-start | bytes 983048 | tf_op jit(solution)/shard_map/ppermute | solution.py:534
  77.2 0.7 copy-start.6
  77.9 31.6 %all-to-all-start.1 = ((f32[4,8,10240]{2,1,0:T(8,128)}), f32[4,8,10240]{2,1,0:T(8,128)S(1)}, u32[]{:S(2)}, u32[]{:S(2)}) async-start(f32[4,8,10240]{2,1,0:T(8,128)} %after.3.refs_1_), calls=%async_computation.1 | async-start | bytes 2621440 | tf_op jit(solution)/shard_map/all_to_all | solution.py:538
  89.4 19.6 %collective-permute-start.12 = (f32[8,10240]{1,0:T(8,128)}, f32[8,10240]{1,0:T(8,128)S(1)}, u32[]{:S(2)}, u32[]{:S(2)}) collective-permute-start(f32[8,10240]{1,0:T(8,128)} %get-tuple-element.60), channel_id=1, source_target_pairs={{0,32},{32,64},{64,96},{96,0},{1,33},{33,65},{65,97},{97,1},{2,34}... | collective-permute-start | bytes 983048 | tf_op jit(solution)/shard_map/ppermute | solution.py:534
  92.8 23.3 %collective-permute-start.13 = (f32[8,10240]{1,0:T(8,128)}, f32[8,10240]{1,0:T(8,128)S(1)}, u32[]{:S(2)}, u32[]{:S(2)}) collective-permute-start(f32[8,10240]{1,0:T(8,128)} %get-tuple-element.61), channel_id=1, source_target_pairs={{0,64},{32,96},{64,0},{96,32},{1,65},{33,97},{65,1},{97,33},{2,66}... | collective-permute-start | bytes 983048 | tf_op jit(solution)/shard_map/ppermute | solution.py:534
  95.4 20.6 %collective-permute-start.14 = (f32[8,10240]{1,0:T(8,128)}, f32[8,10240]{1,0:T(8,128)S(1)}, u32[]{:S(2)}, u32[]{:S(2)}) collective-permute-start(f32[8,10240]{1,0:T(8,128)} %get-tuple-element.62), channel_id=1, source_target_pairs={{0,96},{32,0},{64,32},{96,64},{1,97},{33,1},{65,33},{97,65},{2,98}... | collective-permute-start | bytes 983048 | tf_op jit(solution)/shard_map/ppermute | solution.py:534
  104.1 18.5 %collective-permute-start.9 = (f32[8,10240]{1,0:T(8,128)}, f32[8,10240]{1,0:T(8,128)S(1)}, u32[]{:S(2)}, u32[]{:S(2)}) collective-permute-start(f32[8,10240]{1,0:T(8,128)} %get-tuple-element.57), channel_id=1, source_target_pairs={{0,32},{32,64},{64,96},{96,0},{1,33},{33,65},{65,97},{97,1},{2,34}... | collective-permute-start | bytes 983048 | tf_op jit(solution)/shard_map/ppermute | solution.py:534
  106.0 22.7 %collective-permute-start.10 = (f32[8,10240]{1,0:T(8,128)}, f32[8,10240]{1,0:T(8,128)S(1)}, u32[]{:S(2)}, u32[]{:S(2)}) collective-permute-start(f32[8,10240]{1,0:T(8,128)} %get-tuple-element.58), channel_id=1, source_target_pairs={{0,64},{32,96},{64,0},{96,32},{1,65},{33,97},{65,1},{97,33},{2,66}... | collective-permute-start | bytes 983048 | tf_op jit(solution)/shard_map/ppermute | solution.py:534
  109.1 7.0 %copy-start.7 = (f32[8,10240]{1,0:T(8,128)}, f32[8,10240]{1,0:T(8,128)S(1)}, u32[]{:S(2)}) copy-start(f32[8,10240]{1,0:T(8,128)S(1)} %collective-permute-done.12.refs_1_) | copy-start | bytes 983044
  109.1 19.6 %collective-permute-start.11 = (f32[8,10240]{1,0:T(8,128)}, f32[8,10240]{1,0:T(8,128)S(1)}, u32[]{:S(2)}, u32[]{:S(2)}) collective-permute-start(f32[8,10240]{1,0:T(8,128)} %get-tuple-element.59), channel_id=1, source_target_pairs={{0,96},{32,0},{64,32},{96,64},{1,97},{33,1},{65,33},{97,65},{2,98}... | collective-permute-start | bytes 983048 | tf_op jit(solution)/shard_map/ppermute | solution.py:534
  109.6 1.1 copy-start.5
  116.1 0.7 copy-start.8
  116.8 0.7 copy-start.9
  122.6 6.1 %copy-start.10 = (f32[8,10240]{1,0:T(8,128)}, f32[8,10240]{1,0:T(8,128)S(1)}, u32[]{:S(2)}) copy-start(f32[8,10240]{1,0:T(8,128)S(1)} %collective-permute-done.9.refs_1_) | copy-start | bytes 983044
  128.7 0.7 copy-start.11
  128.7 0.8 copy-start.12

commit v5 on v4

--- a/solution.py
+++ b/solution.py
@@ -524,7 +524,7 @@
         out_specs=pl.BlockSpec(memory_space=pl.ANY),
         scratch_shapes=[pltpu.VMEM((GROUPS, ROWS, CHUNK), f32), pltpu.SemaphoreType.DMA((GROUPS,))],
         input_output_aliases={1 + len(pieces): 0} if held else {},
-        compiler_params=params(60),
+        compiler_params=params(8),
         cost_estimate=cost(2),
         name="unpack",
     )(rank, *pieces, *held)

time: 132 us -> 130 us (0.985); the launches traced: 133 us -> 129 us
  starting transfers between devices: 40 us -> 27.6 us
  Pallas kernels: 51.9 us -> 59.8 us
  waiting for transfers between devices: 18.8 us -> 23.7 us
  local copies, waits for them, and re-layouts: 6.45 us -> 3.08 us
    ppermute x13, starting transfers between devices: 30.3 us -> 19.5 us  [shifted(): return lax.ppermute(x, axis, [(i, (i + by) % size) for i in range(size)])]
    pallas_call x1, Pallas kernels: 3.9 us -> 10.2 us  [pick(): pl.pallas_call(pick_kernel, out_shape=[jax.ShapeDtypeStruct((PADDED, PART...]
    ppermute x13, waiting for transfers between devices: 17.6 us -> 22.1 us  [shifted(): return lax.ppermute(x, axis, [(i, (i + by) % size) for i in range(size)])]
    pallas_call x3, Pallas kernels: 20.9 us -> 24.8 us  [update(): pl.pallas_call(functools.partial(update_kernel, chunks[0], late, apart),...]
    unnamed x26 -> x16, local copies, waits for them, and re-layouts: 5.79 us -> 2.43 us
    pallas_call x3, Pallas kernels: 8.81 us -> 6.43 us  [unpack(): pl.pallas_call(functools.partial(unpack_kernel, chunks[0], apart), grid=(...]
  transfers between devices with their start and end apart: 17 -> 17, of which waited for: 6 -> 7; matrix products, arithmetic and copies ran while one was open for 1% -> 1% of each run, Pallas kernels for 32% -> 40%
where the time goes in v5:
time: 130 us; the launch traced here: 129 us
  Pallas kernels  59.8 us (46%)
  starting transfers between devices  27.6 us (21%)
  waiting for transfers between devices  23.7 us (18%)
  blocking collectives  13.9 us (11%)
  local copies, waits for them, and re-layouts  3.08 us (2%)
    pallas_call x3, Pallas kernels, update(): pl.pallas_call(functools.partial(update_kernel, chunks[0], late, apart),...  24.8 us
    ppermute x13, waiting for transfers between devices, shifted(): return lax.ppermute(x, axis, [(i, (i + by) % size) for i in range(size)])  22.1 us
    ppermute x13, starting transfers between devices, shifted(): return lax.ppermute(x, axis, [(i, (i + by) % size) for i in range(size)])  19.5 us
    all_gather x1, blocking collectives, per_device(): mine = lax.all_gather(summed, 'member', axis=0, tiled=True)  13.9 us
    pallas_call x1, Pallas kernels, pick(): pl.pallas_call(pick_kernel, out_shape=[jax.ShapeDtypeStruct((PADDED, PART...  10.2 us
    pallas_call x1, Pallas kernels, drivers(): pl.pallas_call(drivers_kernel, out_shape=[jax.ShapeDtypeStruct((BLOCKS, O...  9.14 us
    all_to_all x2, starting transfers between devices, exchanged(): return lax.all_to_all(x, 'member', split_axis=0, concat_axis=0, tiled=True)  8.09 us
    pallas_call x3, Pallas kernels, unpack(): pl.pallas_call(functools.partial(unpack_kernel, chunks[0], apart), grid=(...  6.43 us
  transfers between devices with their start and end apart: 17, of which 7 were waited for; matrix products, arithmetic and copies ran while one was open for 1% of the time, Pallas kernels for 40%

profile of v5, /device:TPU:0, one launch (start us, length us, event | category | flops | bytes accessed | tf_op | source)
XLA Modules:
  0.0 129.3 jit_solution(11610839749561061338)
XLA Ops:
  0.0 6.0 %pack.1 = (f32[4,8,20480]{2,1,0:T(8,128)}, f32[8,10240]{1,0:T(8,128)}, f32[8,10240]{1,0:T(8,128)}, f32[8,10240]{1,0:T(8,128)}, f32[8,10240]{1,0:T(8,128)}, /*index=5*/s32[8,256]{1,0:T(8,128)}) custom-call(s32[1]{0:T(128)} %bitcast.rank_ref, s32[1]{0:T(128)} %bitcast.1.slab_ref, s32[4]{0:T(128)} %order_ref.7, s32[4,256]{1,0:T(4,128)} %owner_ref.5, ...), custom_call_target="tpu_custom_call" | custom-call | bytes 3072 | tf_op jit(solution)/shard_map/pack/pallas_call | solution.py:104
  6.0 4.4 %all-to-all-start = ((f32[4,8,20480]{2,1,0:T(8,128)}), f32[4,8,20480]{2,1,0:T(8,128)S(1)}, u32[]{:S(2)}, u32[]{:S(2)}) async-start(f32[4,8,20480]{2,1,0:T(8,128)} %get-tuple-element.35.after_ref), calls=%async_computation | async-start | bytes 5242880 | tf_op jit(solution)/shard_map/all_to_all | solution.py:538
  10.4 10.2 %pick.1 = (f32[24,1664]{1,0:T(8,128)}, f32[24,1664]{1,0:T(8,128)}) custom-call(s32[1]{0:T(128)} %bitcast.1.slab_ref, s32[4]{0:T(128)} %order_ref.7, s32[4,256]{1,0:T(4,128)} %owner_ref.5, s32[4,4,256]{2,1,0:T(4,128)} %bitcast.8, s32[8,256]{1,0:T(8,128)} %get-tuple-element.34.held, f32[4,4,256]{2,1,0:T(4,128)} %bitcast.6, f32[20,49152]{1,0:T(8,128)} %ens_ref.3, ...), custom_call_target="tpu_custom_call" | custom-call | bytes 8192 | tf_op jit(solution)/shard_map/pick/pallas_call | solution.py:201
  20.6 0.0 collective-permute-start
  20.6 1.6 %collective-permute-done = f32[24,1664]{1,0:T(8,128)S(1)} collective-permute-done((f32[24,1664]{1,0:T(8,128)}, f32[24,1664]{1,0:T(8,128)S(1)}, u32[]{:S(2)}, u32[]{:S(2)}) %collective-permute-start) | collective-permute-done | bytes 159776 | tf_op jit(solution)/shard_map/ppermute | solution.py:563
  22.2 0.9 add.7.after_ref.chip_ref
  23.2 0.0 copy-start
  23.2 3.1 %collective-permute-start.2 = (f32[24,1664]{1,0:T(8,128)S(1)}, f32[24,1664]{1,0:T(8,128)S(1)}, u32[]{:S(2)}, u32[]{:S(2)}) collective-permute-start(f32[24,1664]{1,0:T(8,128)S(1)} %add.7.after_ref.chip_ref), channel_id=1, source_target_pairs={{0,30},{1,31},{2,0},{3,1},{4,2},{5,3},{6,4},{7,5},{8,6},{9,7},{10,... | collective-permute-start | bytes 479240 | tf_op jit(solution)/shard_map/ppermute | solution.py:534
  26.3 0.0 collective-permute-start.1
  26.3 1.5 %collective-permute-start.4 = (f32[24,640]{1,0:T(8,128)S(1)}, f32[24,640]{1,0:T(8,128)S(1)}, u32[]{:S(2)}, u32[]{:S(2)}) collective-permute-start(f32[24,640]{1,0:T(8,128)S(1)} %slice.9), channel_id=1, source_target_pairs={{0,28},{1,29},{2,30},{3,31},{4,0},{5,1},{6,2},{7,3},{8,4},{9,5},{1... | collective-permute-start | bytes 184328 | tf_op jit(solution)/shard_map/ppermute | solution.py:534
  27.8 2.1 %collective-permute-start.3 = (f32[24,640]{1,0:T(8,128)S(1)}, f32[24,640]{1,0:T(8,128)S(1)}, u32[]{:S(2)}, u32[]{:S(2)}) collective-permute-start(f32[24,640]{1,0:T(8,128)S(1)} %slice.9), channel_id=1, source_target_pairs={{0,4},{1,5},{2,6},{3,7},{4,8},{5,9},{6,10},{7,11},{8,12},{9,13},{1... | collective-permute-start | bytes 184328 | tf_op jit(solution)/shard_map/ppermute | solution.py:534
  29.9 0.0 copy-done
  29.9 3.2 %reach.1 = (s32[4]{0:T(128)}, s32[4,1,256]{2,1,0:T(1,128)}, bf16[4,256,256]{2,1,0:T(8,128)(2,1)}, f32[4,256,128]{2,1,0:T(8,128)}, f32[4,256,128]{2,1,0:T(8,128)}...) custom-call(s32[1]{0:T(128)S(6)} %add.6.here_ref, s32[4]{0:T(128)} %order_ref.7, s32[4,256]{1,0:T(4,128)} %owner_ref.5, ...), custom_call_target="tpu_custom_call" | custom-call | bytes 2048 | tf_op jit(solution)/shard_map/reach/pallas_call | solution.py:269
  33.1 0.0 collective-permute-done.4.refs_3_
  33.1 2.6 %collective-permute-done.3.refs_2_ = f32[24,640]{1,0:T(8,128)S(1)} collective-permute-done((f32[24,640]{1,0:T(8,128)S(1)}, f32[24,640]{1,0:T(8,128)S(1)}, u32[]{:S(2)}, u32[]{:S(2)}) %collective-permute-start.3) | collective-permute-done | bytes 61472 | tf_op jit(solution)/shard_map/ppermute | solution.py:534
  35.7 0.0 collective-permute-done.2.refs_1_
  35.7 2.0 %collective-permute-done.1.refs_0_ = f32[24,1664]{1,0:T(8,128)S(1)} collective-permute-done((f32[24,1664]{1,0:T(8,128)S(1)}, f32[24,1664]{1,0:T(8,128)S(1)}, u32[]{:S(2)}, u32[]{:S(2)}) %collective-permute-start.1) | collective-permute-done | bytes 159776 | tf_op jit(solution)/shard_map/ppermute | solution.py:534
  37.7 0.0 copy-start.1
  37.7 0.9 copy-done.1
  38.6 0.0 copy-start.4
  38.6 0.6 copy-done.4
  39.2 13.9 %all_gather.3.refs_7_.refs_4_ = f32[96,1664]{1,0:T(8,128)S(1)} all-gather(f32[24,1664]{1,0:T(8,128)S(1)} %window.1), channel_id=1, replica_groups=mesh['member'=4,'slab'=32] {'member'}, dimensions={0}, use_global_device_ids=true | all-gather | bytes 798720 | tf_op jit(solution)/shard_map/all_gather | solution.py:570
  53.1 0.0 copy-start.6
  53.1 0.0 collective-permute-start.5
  53.1 0.0 all-to-all-done.refs_0_
  53.1 0.0 copy-start.5
  53.1 0.6 slice_bitcast_fusion.refs_5_
  53.8 0.2 copy-done.6
  54.0 2.0 %collective-permute-start.6 = (f32[8,10240]{1,0:T(8,128)}, f32[8,10240]{1,0:T(8,128)S(1)}, u32[]{:S(2)}, u32[]{:S(2)}) collective-permute-start(f32[8,10240]{1,0:T(8,128)} %get-tuple-element.52), channel_id=1, source_target_pairs={{0,32},{32,64},{64,96},{96,0},{1,33},{33,65},{65,97},{97,1},{2,34}... | collective-permute-start | bytes 983048 | tf_op jit(solution)/shard_map/ppermute | solution.py:534
  56.0 2.7 %collective-permute-start.7 = (f32[8,10240]{1,0:T(8,128)}, f32[8,10240]{1,0:T(8,128)}, u32[]{:S(2)}, u32[]{:S(2)}) collective-permute-start(f32[8,10240]{1,0:T(8,128)} %get-tuple-element.53), channel_id=1, source_target_pairs={{0,64},{32,96},{64,0},{96,32},{1,65},{33,97},{65,1},{97,33},{2,66}... | collective-permute-start | bytes 983048 | tf_op jit(solution)/shard_map/ppermute | solution.py:534
  58.6 0.0 collective-permute-start.8
  58.6 0.0 collective-permute-done.5.refs_8_
  58.6 9.1 %drivers.1 = (bf16[4,256,240]{2,1,0:T(8,128)(2,1)}, bf16[4,160,256]{2,1,0:T(8,128)(2,1)}) custom-call(s32[1]{0:T(128)S(6)} %add.6.here_ref, s32[4]{0:T(128)} %order_ref.7, s32[4]{0:T(128)} %get-tuple-element.38.refs_4_.count_ref, f32[4,4,256]{2,1,0:T(4,128)} %bitcast.7, f32[4,256]{1,0:T(4,128)} %refs_1_.1, f32[4,256]{1,0:T(4,128)} %refs_2_.1, ...), custom_call_target="tpu_custom_call" | custom-call | bytes 8192 | tf_op jit(solution)/shard_map/drivers/pallas_call | solution.py:378
  67.8 0.0 copy-done.5
  67.8 8.1 %update.3.refs_0_ = f32[4,8,10240]{2,1,0:T(8,128)} custom-call(s32[1]{0:T(128)S(6)} %add.6.here_ref, s32[4]{0:T(128)} %get-tuple-element.38.refs_4_.count_ref, bf16[4,256,240]{2,1,0:T(8,128)(2,1)} %get-tuple-element.43.lhs_ref, bf16[4,160,256]{2,1,0:T(8,128)(2,1)} %get-tuple-element.44.driver_ref, f32[4,256,128]{2,1,0:T(8,128)} %get-tuple-element.45.centre_ref, ...), custom_call_target="tpu_custom_call" | custom-call | bytes 8192 | tf_op jit(solution)/shard_map/update/pallas_call | solution.py:481
  75.9 0.0 collective-permute-done.6.refs_1_
  75.9 0.0 copy-start.7
  75.9 0.0 collective-permute-done.7.refs_2_
  75.9 0.0 collective-permute-done.8.refs_3_
  75.9 0.7 copy-done.7
  76.6 3.7 %all-to-all-start.1 = ((f32[4,8,10240]{2,1,0:T(8,128)}), f32[4,8,10240]{2,1,0:T(8,128)S(1)}, u32[]{:S(2)}, u32[]{:S(2)}) async-start(f32[4,8,10240]{2,1,0:T(8,128)} %after.3.refs_1_), calls=%async_computation.1 | async-start | bytes 2621440 | tf_op jit(solution)/shard_map/all_to_all | solution.py:538
  80.4 8.2 %update.4 = (f32[8,10240]{1,0:T(8,128)}, f32[8,10240]{1,0:T(8,128)}, f32[8,10240]{1,0:T(8,128)}, f32[8,10240]{1,0:T(8,128)}) custom-call(s32[1]{0:T(128)S(6)} %add.6.here_ref, s32[4]{0:T(128)} %get-tuple-element.38.refs_4_.count_ref, bf16[4,256,240]{2,1,0:T(8,128)(2,1)} %get-tuple-element.43.lhs_ref, bf16[4,160,256]{2,1,0:T(8,128)(2,1)} %get-tuple-element.44.driver_ref, ...), custom_call_target="tpu_custom_call" | custom-call | bytes 8192 | tf_op jit(solution)/shard_map/update/pallas_call | solution.py:481
  88.6 2.0 %collective-permute-start.12 = (f32[8,10240]{1,0:T(8,128)}, f32[8,10240]{1,0:T(8,128)S(1)}, u32[]{:S(2)}, u32[]{:S(2)}) collective-permute-start(f32[8,10240]{1,0:T(8,128)} %get-tuple-element.60), channel_id=1, source_target_pairs={{0,32},{32,64},{64,96},{96,0},{1,33},{33,65},{65,97},{97,1},{2,34}... | collective-permute-start | bytes 983048 | tf_op jit(solution)/shard_map/ppermute | solution.py:534
  90.6 2.5 %collective-permute-start.13 = (f32[8,10240]{1,0:T(8,128)}, f32[8,10240]{1,0:T(8,128)S(1)}, u32[]{:S(2)}, u32[]{:S(2)}) collective-permute-start(f32[8,10240]{1,0:T(8,128)} %get-tuple-element.61), channel_id=1, source_target_pairs={{0,64},{32,96},{64,0},{96,32},{1,65},{33,97},{65,1},{97,33},{2,66}... | collective-permute-start | bytes 983048 | tf_op jit(solution)/shard_map/ppermute | solution.py:534
  93.0 1.5 %collective-permute-start.14 = (f32[8,10240]{1,0:T(8,128)}, f32[8,10240]{1,0:T(8,128)S(1)}, u32[]{:S(2)}, u32[]{:S(2)}) collective-permute-start(f32[8,10240]{1,0:T(8,128)} %get-tuple-element.62), channel_id=1, source_target_pairs={{0,96},{32,0},{64,32},{96,64},{1,97},{33,1},{65,33},{97,65},{2,98}... | collective-permute-start | bytes 983048 | tf_op jit(solution)/shard_map/ppermute | solution.py:534
  94.5 8.5 %update.5 = (f32[8,10240]{1,0:T(8,128)}, f32[8,10240]{1,0:T(8,128)}, f32[8,10240]{1,0:T(8,128)}, f32[8,10240]{1,0:T(8,128)}) custom-call(s32[1]{0:T(128)S(6)} %add.6.here_ref, s32[4]{0:T(128)} %get-tuple-element.38.refs_4_.count_ref, bf16[4,256,240]{2,1,0:T(8,128)(2,1)} %get-tuple-element.43.lhs_ref, bf16[4,160,256]{2,1,0:T(8,128)(2,1)} %get-tuple-element.44.driver_ref, ...), custom_call_target="tpu_custom_call" | custom-call | bytes 8192 | tf_op jit(solution)/shard_map/update/pallas_call | solution.py:481
  103.0 0.6 collective-permute-start.9
  103.6 1.1 collective-permute-start.10
  104.7 1.9 %collective-permute-done.12.refs_1_ = f32[8,10240]{1,0:T(8,128)S(1)} collective-permute-done((f32[8,10240]{1,0:T(8,128)}, f32[8,10240]{1,0:T(8,128)S(1)}, u32[]{:S(2)}, u32[]{:S(2)}) %collective-permute-start.12) | collective-permute-done | bytes 327712 | tf_op jit(solution)/shard_map/ppermute | solution.py:534
  106.6 0.0 copy-start.2
  106.6 0.5 collective-permute-start.11
  107.1 0.0 all-to-all-done.1.refs_0_
  107.1 1.9 %unpack.3.refs_4_ = f32[20,49152]{1,0:T(8,128)} custom-call(s32[1]{0:T(128)} %bitcast.rank_ref, f32[4,8,10240]{2,1,0:T(8,128)S(1)} %all-to-all-done.1.refs_0_), custom_call_target="tpu_custom_call" | custom-call | bytes 2048 | tf_op jit(solution)/shard_map/unpack/pallas_call | solution.py:519
  109.0 0.0 copy-start.3
  109.0 4.6 %collective-permute-done.13.refs_2_ = f32[8,10240]{1,0:T(8,128)S(1)} collective-permute-done((f32[8,10240]{1,0:T(8,128)}, f32[8,10240]{1,0:T(8,128)S(1)}, u32[]{:S(2)}, u32[]{:S(2)}) %collective-permute-start.13) | collective-permute-done | bytes 327712 | tf_op jit(solution)/shard_map/ppermute | solution.py:534
  113.6 0.0 collective-permute-done.14.refs_3_
  113.6 0.0 copy-done.2
  113.6 1.8 %unpack.4.refs_4_ = f32[20,49152]{1,0:T(8,128)} custom-call(s32[1]{0:T(128)} %bitcast.rank_ref, f32[8,10240]{1,0:T(8,128)S(1)} %copy-done.2, f32[8,10240]{1,0:T(8,128)S(1)} %collective-permute-done.12.refs_1_, f32[8,10240]{1,0:T(8,128)S(1)} %collective-permute-done.13.refs_2_, ...), custom_call_target="tpu_custom_call", output_to_operand_aliasing={{}: (5, {})} | custom-call | bytes 2048 | tf_op jit(solution)/shard_map/unpack/pallas_call | solution.py:519
  115.4 4.9 %collective-permute-done.9.refs_1_ = f32[8,10240]{1,0:T(8,128)S(1)} collective-permute-done((f32[8,10240]{1,0:T(8,128)}, f32[8,10240]{1,0:T(8,128)S(1)}, u32[]{:S(2)}, u32[]{:S(2)}) %collective-permute-start.9) | collective-permute-done | bytes 327712 | tf_op jit(solution)/shard_map/ppermute | solution.py:534
  120.3 6.1 %collective-permute-done.10.refs_2_ = f32[8,10240]{1,0:T(8,128)S(1)} collective-permute-done((f32[8,10240]{1,0:T(8,128)}, f32[8,10240]{1,0:T(8,128)S(1)}, u32[]{:S(2)}, u32[]{:S(2)}) %collective-permute-start.10) | collective-permute-done | bytes 327712 | tf_op jit(solution)/shard_map/ppermute | solution.py:534
  126.4 0.0 collective-permute-done.11.refs_3_
  126.4 0.0 copy-done.3
  126.4 2.7 %unpack.5 = f32[20,49152]{1,0:T(8,128)} custom-call(s32[1]{0:T(128)} %bitcast.rank_ref, f32[8,10240]{1,0:T(8,128)S(1)} %copy-done.3, f32[8,10240]{1,0:T(8,128)S(1)} %collective-permute-done.9.refs_1_, f32[8,10240]{1,0:T(8,128)S(1)} %collective-permute-done.10.refs_2_, f32[8,10240]{1,0:T(8,128)} %collective-permute-done.11.refs_3_, ...), custom_call_target="tpu_custom_call", output_to_operand_aliasing={{}: (5, {})} | custom-call | bytes 2048 | tf_op jit(solution)/shard_map/unpack/pallas_call | solution.py:519
  (4 shorter events, 0.0 us)
Async XLA Ops:
  6.0 47.1 %all-to-all-start = ((f32[4,8,20480]{2,1,0:T(8,128)}), f32[4,8,20480]{2,1,0:T(8,128)S(1)}, u32[]{:S(2)}, u32[]{:S(2)}) async-start(f32[4,8,20480]{2,1,0:T(8,128)} %get-tuple-element.35.after_ref), calls=%async_computation | async-start | bytes 5242880 | tf_op jit(solution)/shard_map/all_to_all | solution.py:538
  20.6 1.6 %collective-permute-start = (f32[24,1664]{1,0:T(8,128)}, f32[24,1664]{1,0:T(8,128)S(1)}, u32[]{:S(2)}, u32[]{:S(2)}) collective-permute-start(f32[24,1664]{1,0:T(8,128)} %get-tuple-element.37), channel_id=1, source_target_pairs={{0,1},{1,0},{2,3},{3,2},{4,5},{5,4},{6,7},{7,6},{8,9},{9,8},{10,11... | collective-permute-start | bytes 479240 | tf_op jit(solution)/shard_map/ppermute | solution.py:563
  23.2 6.7 %copy-start = (f32[24,1664]{1,0:T(8,128)}, f32[24,1664]{1,0:T(8,128)S(1)}, u32[]{:S(2)}) copy-start(f32[24,1664]{1,0:T(8,128)S(1)} %add.7.after_ref.chip_ref) | copy-start | bytes 479236
  23.2 12.5 %collective-permute-start.2 = (f32[24,1664]{1,0:T(8,128)S(1)}, f32[24,1664]{1,0:T(8,128)S(1)}, u32[]{:S(2)}, u32[]{:S(2)}) collective-permute-start(f32[24,1664]{1,0:T(8,128)S(1)} %add.7.after_ref.chip_ref), channel_id=1, source_target_pairs={{0,30},{1,31},{2,0},{3,1},{4,2},{5,3},{6,4},{7,5},{8,6},{9,7},{10,... | collective-permute-start | bytes 479240 | tf_op jit(solution)/shard_map/ppermute | solution.py:534
  26.3 11.4 %collective-permute-start.1 = (f32[24,1664]{1,0:T(8,128)S(1)}, f32[24,1664]{1,0:T(8,128)S(1)}, u32[]{:S(2)}, u32[]{:S(2)}) collective-permute-start(f32[24,1664]{1,0:T(8,128)S(1)} %add.7.after_ref.chip_ref), channel_id=1, source_target_pairs={{0,2},{1,3},{2,4},{3,5},{4,6},{5,7},{6,8},{7,9},{8,10},{9,11},{10,... | collective-permute-start | bytes 479240 | tf_op jit(solution)/shard_map/ppermute | solution.py:534
  26.3 6.8 %collective-permute-start.4 = (f32[24,640]{1,0:T(8,128)S(1)}, f32[24,640]{1,0:T(8,128)S(1)}, u32[]{:S(2)}, u32[]{:S(2)}) collective-permute-start(f32[24,640]{1,0:T(8,128)S(1)} %slice.9), channel_id=1, source_target_pairs={{0,28},{1,29},{2,30},{3,31},{4,0},{5,1},{6,2},{7,3},{8,4},{9,5},{1... | collective-permute-start | bytes 184328 | tf_op jit(solution)/shard_map/ppermute | solution.py:534
  27.8 7.8 %collective-permute-start.3 = (f32[24,640]{1,0:T(8,128)S(1)}, f32[24,640]{1,0:T(8,128)S(1)}, u32[]{:S(2)}, u32[]{:S(2)}) collective-permute-start(f32[24,640]{1,0:T(8,128)S(1)} %slice.9), channel_id=1, source_target_pairs={{0,4},{1,5},{2,6},{3,7},{4,8},{5,9},{6,10},{7,11},{8,12},{9,13},{1... | collective-permute-start | bytes 184328 | tf_op jit(solution)/shard_map/ppermute | solution.py:534
  37.7 0.9 copy-start.1
  38.6 0.6 copy-start.4
  53.1 0.8 copy-start.6
  53.1 5.5 %collective-permute-start.5 = (f32[96,1664]{1,0:T(8,128)S(1)}, f32[96,1664]{1,0:T(8,128)}, u32[]{:S(2)}, u32[]{:S(2)}) collective-permute-start(f32[96,1664]{1,0:T(8,128)S(1)} %all_gather.3.refs_7_.refs_4_), channel_id=1, source_target_pairs={{0,1},{1,0},{2,3},{3,2},{4,5},{5,4},{6,7},{7,6},{8,9},{9,8},{10,11... | collective-permute-start | bytes 1916936 | tf_op jit(solution)/shard_map/ppermute | solution.py:571
  53.1 14.7 %copy-start.5 = (f32[4,8,20480]{2,1,0:T(8,128)}, f32[4,8,20480]{2,1,0:T(8,128)S(1)}, u32[]{:S(2)}) copy-start(f32[4,8,20480]{2,1,0:T(8,128)S(1)} %all-to-all-done.refs_0_) | copy-start | bytes 7864324
  54.0 21.9 %collective-permute-start.6 = (f32[8,10240]{1,0:T(8,128)}, f32[8,10240]{1,0:T(8,128)S(1)}, u32[]{:S(2)}, u32[]{:S(2)}) collective-permute-start(f32[8,10240]{1,0:T(8,128)} %get-tuple-element.52), channel_id=1, source_target_pairs={{0,32},{32,64},{64,96},{96,0},{1,33},{33,65},{65,97},{97,1},{2,34}... | collective-permute-start | bytes 983048 | tf_op jit(solution)/shard_map/ppermute | solution.py:534
  56.0 19.9 %collective-permute-start.7 = (f32[8,10240]{1,0:T(8,128)}, f32[8,10240]{1,0:T(8,128)}, u32[]{:S(2)}, u32[]{:S(2)}) collective-permute-start(f32[8,10240]{1,0:T(8,128)} %get-tuple-element.53), channel_id=1, source_target_pairs={{0,64},{32,96},{64,0},{96,32},{1,65},{33,97},{65,1},{97,33},{2,66}... | collective-permute-start | bytes 983048 | tf_op jit(solution)/shard_map/ppermute | solution.py:534
  58.6 17.3 %collective-permute-start.8 = (f32[8,10240]{1,0:T(8,128)}, f32[8,10240]{1,0:T(8,128)}, u32[]{:S(2)}, u32[]{:S(2)}) collective-permute-start(f32[8,10240]{1,0:T(8,128)} %get-tuple-element.54), channel_id=1, source_target_pairs={{0,96},{32,0},{64,32},{96,64},{1,97},{33,1},{65,33},{97,65},{2,98}... | collective-permute-start | bytes 983048 | tf_op jit(solution)/shard_map/ppermute | solution.py:534
  75.9 0.7 copy-start.7
  76.6 30.5 %all-to-all-start.1 = ((f32[4,8,10240]{2,1,0:T(8,128)}), f32[4,8,10240]{2,1,0:T(8,128)S(1)}, u32[]{:S(2)}, u32[]{:S(2)}) async-start(f32[4,8,10240]{2,1,0:T(8,128)} %after.3.refs_1_), calls=%async_computation.1 | async-start | bytes 2621440 | tf_op jit(solution)/shard_map/all_to_all | solution.py:538
  88.6 18.0 %collective-permute-start.12 = (f32[8,10240]{1,0:T(8,128)}, f32[8,10240]{1,0:T(8,128)S(1)}, u32[]{:S(2)}, u32[]{:S(2)}) collective-permute-start(f32[8,10240]{1,0:T(8,128)} %get-tuple-element.60), channel_id=1, source_target_pairs={{0,32},{32,64},{64,96},{96,0},{1,33},{33,65},{65,97},{97,1},{2,34}... | collective-permute-start | bytes 983048 | tf_op jit(solution)/shard_map/ppermute | solution.py:534
  90.6 23.0 %collective-permute-start.13 = (f32[8,10240]{1,0:T(8,128)}, f32[8,10240]{1,0:T(8,128)S(1)}, u32[]{:S(2)}, u32[]{:S(2)}) collective-permute-start(f32[8,10240]{1,0:T(8,128)} %get-tuple-element.61), channel_id=1, source_target_pairs={{0,64},{32,96},{64,0},{96,32},{1,65},{33,97},{65,1},{97,33},{2,66}... | collective-permute-start | bytes 983048 | tf_op jit(solution)/shard_map/ppermute | solution.py:534
  93.0 20.6 %collective-permute-start.14 = (f32[8,10240]{1,0:T(8,128)}, f32[8,10240]{1,0:T(8,128)S(1)}, u32[]{:S(2)}, u32[]{:S(2)}) collective-permute-start(f32[8,10240]{1,0:T(8,128)} %get-tuple-element.62), channel_id=1, source_target_pairs={{0,96},{32,0},{64,32},{96,64},{1,97},{33,1},{65,33},{97,65},{2,98}... | collective-permute-start | bytes 983048 | tf_op jit(solution)/shard_map/ppermute | solution.py:534
  103.0 17.4 %collective-permute-start.9 = (f32[8,10240]{1,0:T(8,128)}, f32[8,10240]{1,0:T(8,128)S(1)}, u32[]{:S(2)}, u32[]{:S(2)}) collective-permute-start(f32[8,10240]{1,0:T(8,128)} %get-tuple-element.57), channel_id=1, source_target_pairs={{0,32},{32,64},{64,96},{96,0},{1,33},{33,65},{65,97},{97,1},{2,34}... | collective-permute-start | bytes 983048 | tf_op jit(solution)/shard_map/ppermute | solution.py:534
  103.6 22.8 %collective-permute-start.10 = (f32[8,10240]{1,0:T(8,128)}, f32[8,10240]{1,0:T(8,128)S(1)}, u32[]{:S(2)}, u32[]{:S(2)}) collective-permute-start(f32[8,10240]{1,0:T(8,128)} %get-tuple-element.58), channel_id=1, source_target_pairs={{0,64},{32,96},{64,0},{96,32},{1,65},{33,97},{65,1},{97,33},{2,66}... | collective-permute-start | bytes 983048 | tf_op jit(solution)/shard_map/ppermute | solution.py:534
  106.6 7.0 %copy-start.2 = (f32[8,10240]{1,0:T(8,128)S(1)}, f32[8,10240]{1,0:T(8,128)}, u32[]{:S(2)}) copy-start(f32[8,10240]{1,0:T(8,128)} %get-tuple-element.55.refs_4_.refs_0_) | copy-start | bytes 983044
  106.6 19.8 %collective-permute-start.11 = (f32[8,10240]{1,0:T(8,128)}, f32[8,10240]{1,0:T(8,128)}, u32[]{:S(2)}, u32[]{:S(2)}) collective-permute-start(f32[8,10240]{1,0:T(8,128)} %get-tuple-element.59), channel_id=1, source_target_pairs={{0,96},{32,0},{64,32},{96,64},{1,97},{33,1},{65,33},{97,65},{2,98}... | collective-permute-start | bytes 983048 | tf_op jit(solution)/shard_map/ppermute | solution.py:534
  109.0 17.4 %copy-start.3 = (f32[8,10240]{1,0:T(8,128)S(1)}, f32[8,10240]{1,0:T(8,128)}, u32[]{:S(2)}) copy-start(f32[8,10240]{1,0:T(8,128)} %get-tuple-element.56.refs_0_) | copy-start | bytes 983044
